TPU v7x, 32 devices: a whole 2x2x4 slice. The times are simulated.
32 devices in a mesh: groups: 2 (over x), expert: 16 (over z, y, core).
Axes of the slice: x: 2, y: 2, z: 4, core: 2. Of those that a mesh axis runs over, the one named last changes fastest.
Arguments:
- residual: bfloat16 [4096, 3584], P(('groups', 'expert')), parts along dimension 0, may hold values from -24 to 24
- norm_gain: float32 [3584], replicated, may hold values from 0.25 to 1.75
- router: bfloat16 [3584, 4], replicated, may hold values from -0.09375 to 0.09375
- w_gate: bfloat16 [3584, 4096], P(None, 'expert'), may hold values from -0.09375 to 0.09375
- w_up: bfloat16 [3584, 4096], P(None, 'expert'), may hold values from -0.09375 to 0.09375
- w_down: bfloat16 [4096, 3584], P('expert'), may hold values from -0.1875 to 0.1875
- expert_ids: int32 [4096, 2], P(('groups', 'expert')), parts along dimension 0, may hold values from 0 to 3, all different within a row; in each aligned block of 128 rows (0 to 127, 128 to 255, ...) at most 96 rows name the same one
Outputs:
- layer_out: bfloat16 [4096, 3584], P(('groups', 'expert')), parts along dimension 0
There are 2 independent parts, one for each index of `groups`. A program takes and returns all parts, laid end to end along the dimension named above; an argument that names none is the same for every part. Nothing has to cross between parts.
Inputs may be any that keep to these rules, and one draw needn't show every extreme that they name: `expert_ids`: each row names 2 different experts. Within the rows of one device no expert is named by more than 96 rows, and in every draw some device's rows name some expert exactly 96 times.
All inputs are finite; a program needn't handle non-finite values.
Results may differ from a plain program's by a relative error of at most 0.0054.
Values may be sent and summed in bfloat16 or wider, within the bound.
No kernel may reach another device: no remote copies, remote signals or barrier semaphores. Data moves between devices by JAX's collectives and lax.ppermute only.
A program may use at most 128 MiB of HBM per device.

v0:
```python
import jax
import jax.numpy as jnp
from jax import lax
from jax.sharding import PartitionSpec as P

route_scale = 2.5
norm_eps = 1e-06


def swapped(value, axis, distance):
    mask = 2**distance
    pairs = [(source, source ^ mask) for source in range(lax.axis_size(axis))]
    return lax.ppermute(value, axis, pairs)


def shards(residual, norm_gain, router, w_gate, w_up, w_down, expert_ids):
    tok_rows, model_width = residual.shape
    top_count = expert_ids.shape[1]
    expert_count = router.shape[1]
    device_count = lax.axis_size("expert")
    span_size = device_count // expert_count
    capacity = 3 * tok_rows * top_count // (2 * expert_count)
    quarter = capacity // span_size
    residual_wide = residual.astype(jnp.float32)
    mean_square = jnp.mean(residual_wide * residual_wide, axis=1, keepdims=True)
    normed = (residual_wide * lax.rsqrt(mean_square + norm_eps) * norm_gain).astype(jnp.bfloat16)
    logits = jnp.dot(normed, router, preferred_element_type=jnp.float32)
    affinity = jax.nn.sigmoid(logits)
    picked = expert_ids[:, :, None] == lax.iota(jnp.int32, expert_count)[None, None, :]
    chosen = jnp.sum(jnp.where(picked, affinity[:, None, :], 0.0), axis=2)
    gate_values = route_scale * chosen / jnp.sum(chosen, axis=1, keepdims=True)
    flat_pick = picked.reshape(tok_rows * top_count, expert_count).astype(jnp.int32)
    before = jnp.cumsum(flat_pick, axis=0) - flat_pick
    target = expert_ids.reshape(tok_rows * top_count) * capacity + jnp.sum(
        before * flat_pick, axis=1
    )
    places = lax.iota(jnp.int32, expert_count * capacity)
    matches = (target[None, :] == places[:, None]).reshape(
        expert_count * capacity, tok_rows, top_count
    )
    assignment = jnp.sum(matches.astype(jnp.float32), axis=2).astype(jnp.bfloat16)
    packed = jnp.dot(assignment, normed, preferred_element_type=jnp.float32).astype(jnp.bfloat16)
    member = lax.axis_index("expert") % span_size
    outgoing = packed.reshape(device_count, quarter, model_width)
    arrived = lax.all_to_all(outgoing, "expert", split_axis=0, concat_axis=0, tiled=True)
    current = arrived.reshape(device_count, 1, quarter, model_width)
    for level_index in range(span_size.bit_length() - 1):
        incoming = swapped(current, "expert", level_index)
        lower_first = (member >> level_index) % 2 == 0
        first_part = jnp.where(lower_first, current, incoming)
        second_part = jnp.where(lower_first, incoming, current)
        current = jnp.concatenate((first_part, second_part), axis=1)
    arrived = current.reshape(device_count, capacity, model_width)
    sources, slot_rows, unused_width = arrived.shape
    flat_rows = arrived.reshape(sources * slot_rows, model_width)
    gate_proj = jnp.dot(flat_rows, w_gate, preferred_element_type=jnp.float32)
    up_proj = jnp.dot(flat_rows, w_up, preferred_element_type=jnp.float32)
    activated = (jax.nn.silu(gate_proj) * up_proj).astype(jnp.bfloat16)
    partial_value = jnp.dot(activated, w_down, preferred_element_type=jnp.float32).astype(
        jnp.bfloat16
    )
    partials = partial_value.reshape(sources, slot_rows, model_width)
    returned = lax.all_to_all(partials, "expert", split_axis=0, concat_axis=0, tiled=True)
    summed = jnp.sum(
        returned.reshape(expert_count, span_size, capacity, model_width), axis=1, dtype=jnp.float32
    )
    flat_sums = summed.reshape(expert_count * capacity, model_width)
    gathered = jnp.take(flat_sums, target, axis=0).reshape(tok_rows, top_count, model_width)
    branch = jnp.sum(gathered * gate_values[:, :, None], axis=1)
    return (residual_wide + branch).astype(jnp.bfloat16)


def solution(mesh):
    in_specs = (
        P(("groups", "expert"), None),
        P(),
        P(),
        P(None, "expert"),
        P(None, "expert"),
        P("expert", None),
        P(("groups", "expert"), None),
    )
    out_specs = P(("groups", "expert"), None)
    return jax.shard_map(shards, mesh=mesh, in_specs=in_specs, out_specs=out_specs, check_vma=False)
```

profile of v0, /device:TPU:16, one launch (start us, length us, event | category | flops | bytes accessed | tf_op | source)
XLA Modules:
  0.0 517.7 jit_solution(12100820611355460152)
XLA Ops:
  0.0 0.0 copy-start
  0.0 0.9 copy.28
  0.9 0.1 eq.57
  1.1 0.1 reshape.124
  1.2 1.2 reduce-window.6
  2.4 0.1 slice.10
  2.5 0.1 copy.30
  2.7 0.1 copy.31
  2.8 0.1 add_bitcast_fusion
  2.9 0.1 reduce_sum.68
  3.0 0.1 copy.32
  3.1 0.7 compare_and_fusion
  3.8 1.4 fusion
  5.3 2.1 convolution_convert_fusion.1
  7.4 67.7 %all_to_all.10 = bf16[16,24,3584]{2,1,0:T(8,128)(2,1)} all-to-all(bf16[16,24,3584]{2,1,0:T(8,128)(2,1)S(1)} %bitcast.42), channel_id=1, replica_groups=mesh['groups'=2,'expert'=16] {'expert'}, dimensions={0} | all-to-all | bytes 5505024 | tf_op jit(solution)/shard_map/all_to_all | solution.py:45
  75.2 0.0 collective-permute-start
  75.2 5.4 %collective-permute-done = bf16[16,1,24,3584]{3,2,1,0:T(8,128)(2,1)} collective-permute-done((bf16[16,1,24,3584]{3,2,1,0:T(8,128)(2,1)}, bf16[16,1,24,3584]{3,2,1,0:T(8,128)(2,1)}, u32[]{:S(2)}, u32[]{:S(2)}) %collective-permute-start) | collective-permute-done | bytes 2752544 | tf_op jit(solution)/shard_map/ppermute | solution.py:13
  80.6 3.0 broadcast_select_fusion.3
  83.6 0.0 copy-start.2
  83.6 0.0 copy-start.3
  83.6 3.3 pad_maximum_fusion.1
  86.9 0.0 copy-done.2
  86.9 0.8 copy-done.3
  87.7 0.2 collective-permute-start.1
  87.9 120.8 %collective-permute-done.1 = bf16[16,2,24,3584]{3,2,1,0:T(8,128)(2,1)} collective-permute-done((bf16[16,2,24,3584]{3,2,1,0:T(8,128)(2,1)}, bf16[16,2,24,3584]{3,2,1,0:T(8,128)(2,1)}, u32[]{:S(2)}, u32[]{:S(2)}) %collective-permute-start.1) | collective-permute-done | bytes 5505056 | tf_op jit(solution)/shard_map/ppermute | solution.py:13
  208.7 4.7 broadcast_select_fusion.1
  213.4 0.0 copy-start.8
  213.4 1.1 pad_maximum_fusion
  214.5 0.0 copy-start.4
  214.5 4.0 copy-done.4
  218.5 0.0 copy-done.8
  218.5 4.2 fusion.19
  222.8 0.0 copy-done
  222.8 17.4 %convolution_convert_fusion = bf16[1536,3584]{1,0:T(8,128)(2,1)} fusion(bf16[256,3584]{1,0:T(8,128)(2,1)S(1)} %copy-done, f32[1536,256]{1,0:T(8,128)} %fusion.19, bf16[1536,3584]{1,0:T(8,128)(2,1)} %bitcast.41, bf16[3584,256]{1,0:T(8,128)(2,1)} %param.11), kind=kOutput, calls=%fused_computation.2 | convolution fusion | flops 5645008896 | bytes 27262976 | tf_op jit(solution)/shard_map/dot_general | solution.py:59
  240.1 0.0 copy-start.9
  240.2 6.6 %all-to-all-start.1 = ((bf16[16,96,3584]{2,1,0:T(8,128)(2,1)}), bf16[16,96,3584]{2,1,0:T(8,128)(2,1)}, u32[]{:S(2)}, u32[]{:S(2)}) async-start(bf16[16,96,3584]{2,1,0:T(8,128)(2,1)} %bitcast.39), calls=%async_computation.1 | async-start | bytes 22020096 | tf_op jit(solution)/shard_map/all_to_all | solution.py:63
  246.8 0.0 copy-done.7
  246.8 0.1 copy.34
  246.9 0.1 mul.80
  247.0 0.1 copy.33
  247.2 0.4 fusion.6
  247.7 0.1 copy.35
  247.8 237.7 %all-to-all-done.1 = bf16[16,96,3584]{2,1,0:T(8,128)(2,1)} async-done(((bf16[16,96,3584]{2,1,0:T(8,128)(2,1)}), bf16[16,96,3584]{2,1,0:T(8,128)(2,1)}, u32[]{:S(2)}, u32[]{:S(2)}) %all-to-all-start.1) | async-done | bytes 11010080 | tf_op jit(solution)/shard_map/all_to_all | solution.py:63
  485.5 8.8 %convert_reduce_fusion = f32[4,96,3584]{2,1,0:T(8,128)} fusion(bf16[16,96,3584]{2,1,0:T(8,128)(2,1)} %all-to-all-done.1), kind=kLoop, calls=%fused_computation.1 | loop fusion | flops 9633792 | bytes 16515072 | tf_op jit(solution)/shard_map/reduce_sum | solution.py:64
  494.3 7.8 %gather_fusion = f32[256,3584]{1,0:T(8,128)} fusion(f32[384,3584]{1,0:T(8,128)} %bitcast.38, s32[1024]{0:T(1024)S(1)} %pad_clamp_fusion), kind=kCustom, calls=%fused_computation | custom fusion | bytes 7341056 | tf_op jit(solution)/shard_map/jit(_take)/gather | solution.py:68
  502.1 5.5 %gather.7 = f32[128,2,3584]{2,1,0:T(2,128)} reshape(f32[256,3584]{1,0:T(8,128)} %gather_fusion) | data formatting | bytes 7340032 | tf_op jit(solution)/shard_map/jit(_take)/gather | solution.py:68
  507.6 9.0 %multiply_reduce_fusion = f32[128,3584]{1,0:T(8,128)S(1)} fusion(f32[128,2,3584]{2,1,0:T(2,128)} %gather.7, pred[128,2]{1,0:T(8,128)(4,1)S(1)} %copy.33, f32[128,2]{1,0:T(8,128)S(1)} %copy.35), kind=kLoop, calls=%fused_computation.8 | loop fusion | flops 2293760 | bytes 5506304 | tf_op jit(solution)/shard_map/reduce_sum | solution.py:69
  516.6 1.1 fusion.3
  (19 shorter events, 0.2 us)
Async XLA Ops:
  0.0 222.8 %copy-start = (bf16[256,3584]{1,0:T(8,128)(2,1)S(1)}, bf16[256,3584]{1,0:T(8,128)(2,1)}, u32[]{:S(2)}) copy-start(bf16[256,3584]{1,0:T(8,128)(2,1)} %param.12) | copy-start | bytes 5505028
  75.2 5.4 %collective-permute-start = (bf16[16,1,24,3584]{3,2,1,0:T(8,128)(2,1)}, bf16[16,1,24,3584]{3,2,1,0:T(8,128)(2,1)}, u32[]{:S(2)}, u32[]{:S(2)}) collective-permute-start(bf16[16,1,24,3584]{3,2,1,0:T(8,128)(2,1)} %bitcast.3), channel_id=1, source_target_pairs={{0,1},{1,0},{2,3},{3,2},{4,5},{5,4},{6,7},{7,6},{8,9},{9,8},{10,11... | collective-permute-start | bytes 8257544 | tf_op jit(solution)/shard_map/ppermute | solution.py:13
  83.6 3.3 copy-start.2
  83.6 4.1 copy-start.3
  87.7 121.0 %collective-permute-start.1 = (bf16[16,2,24,3584]{3,2,1,0:T(8,128)(2,1)}, bf16[16,2,24,3584]{3,2,1,0:T(8,128)(2,1)}, u32[]{:S(2)}, u32[]{:S(2)}) collective-permute-start(bf16[16,2,24,3584]{3,2,1,0:T(8,128)(2,1)} %pad_maximum_fusion.1), channel_id=1, source_target_pairs={{0,2},{1,3},{2,0},{3,1},{4,6},{5,7},{6,4},{7,5},{8,10},{9,11},{10,... | collective-permute-start | bytes 16515080 | tf_op jit(solution)/shard_map/ppermute | solution.py:13
  213.4 5.1 copy-start.8
  214.5 4.0 copy-start.4
  240.1 6.6 %copy-start.7 = (s32[128,2]{0,1:T(2,128)S(1)}, s32[128,2]{0,1:T(2,128)}, u32[]{:S(2)}) copy-start(s32[128,2]{0,1:T(2,128)} %param.13) | copy-start | bytes 3076
  240.1 7.1 %copy-start.5 = (bf16[128,3584]{1,0:T(8,128)(2,1)S(1)}, bf16[128,3584]{1,0:T(8,128)(2,1)}, u32[]{:S(2)}) copy-start(bf16[128,3584]{1,0:T(8,128)(2,1)} %param.7) | copy-start | bytes 2752516
  240.1 7.1 %copy-start.6 = (f32[3584]{0:T(1024)S(1)}, f32[3584]{0:T(1024)}, u32[]{:S(2)}) copy-start(f32[3584]{0:T(1024)} %param.8) | copy-start | bytes 43012
  240.1 7.1 %copy-start.9 = (bf16[3584,4]{0,1:T(4,128)(2,1)S(1)}, bf16[3584,4]{0,1:T(4,128)(2,1)}, u32[]{:S(2)}) copy-start(bf16[3584,4]{0,1:T(4,128)(2,1)} %param.9) | copy-start | bytes 86020
  240.2 245.4 %all-to-all-start.1 = ((bf16[16,96,3584]{2,1,0:T(8,128)(2,1)}), bf16[16,96,3584]{2,1,0:T(8,128)(2,1)}, u32[]{:S(2)}, u32[]{:S(2)}) async-start(bf16[16,96,3584]{2,1,0:T(8,128)(2,1)} %bitcast.39), calls=%async_computation.1 | async-start | bytes 22020096 | tf_op jit(solution)/shard_map/all_to_all | solution.py:63
  507.6 10.1 %copy-start.1 = (bf16[256,3584]{1,0:T(8,128)(2,1)S(1)}, bf16[256,3584]{1,0:T(8,128)(2,1)}, u32[]{:S(2)}) copy-start(bf16[256,3584]{1,0:T(8,128)(2,1)} %param.12) | copy-start | bytes 5505028
where the time goes:
time: 518 us
  waiting for transfers between devices  364 us (70%)
  blocking collectives  67.7 us (13%)
  other arithmetic  34.5 us (7%)
  matrix products  24.2 us (5%)
  local copies, waits for them, and re-layouts  20.4 us (4%)
  starting transfers between devices  6.84 us (1%)
    all_to_all x1, waiting for transfers between devices, shards(): lax.all_to_all(partials, 'expert', split_axis=0, concat_axis=0, tiled=True)  238 us
    ppermute x2, waiting for transfers between devices, swapped(): return lax.ppermute(value, axis, pairs)  126 us
    all_to_all x1, blocking collectives, shards(): lax.all_to_all(outgoing, 'expert', split_axis=0, concat_axis=0, tiled=True)  67.7 us
    dot_general x1, matrix products, shards(): jnp.dot(activated, w_down, preferred_element_type=jnp.float32)  17.4 us
    gather x2, local copies, waits for them, and re-layouts, shards(): jnp.take(flat_sums, target, axis=0)  13.3 us
  transfers between devices with their start and end apart: 3, of which 3 were waited for; matrix products, arithmetic and copies ran while one was open for 0% of the time, Pallas kernels for 0%

commit v1 on v0

v1 whole, which is shorter than its diff:
```python
import jax
import jax.numpy as jnp
from jax import lax
from jax.sharding import PartitionSpec as P

route_scale = 2.5
norm_eps = 1e-06


def flipped(value, distance):
    pairs = [(source, source ^ distance) for source in range(lax.axis_size("expert"))]
    return lax.ppermute(value, "expert", pairs)


def turned(value, shift):
    count = lax.axis_size("groups")
    pairs = [(source, (source + shift) % count) for source in range(count)]
    return lax.ppermute(value, "groups", pairs)


def shards(residual, norm_gain, router, w_gate, w_up, w_down, expert_ids):
    tok_rows, model_width = residual.shape
    top_count = expert_ids.shape[1]
    expert_count = router.shape[1]
    device_count = lax.axis_size("expert")
    groups = lax.axis_size("groups")
    span_size = device_count // expert_count
    capacity = 3 * tok_rows * top_count // (2 * expert_count)
    hidden = w_gate.shape[1]
    part = hidden // groups
    my_group = lax.axis_index("groups")
    lines = [[e * span_size + m for e in range(expert_count)] for m in range(span_size)]

    def cut(start):
        gate_up = jnp.concatenate(
            [
                lax.dynamic_slice_in_dim(w_gate, start, part, 1),
                lax.dynamic_slice_in_dim(w_up, start, part, 1),
            ],
            axis=1,
        )
        return gate_up, lax.dynamic_slice_in_dim(w_down, start, part, 0)

    sent_gate_up, sent_down = cut(my_group * part)
    gate_up_parts = [cut(g * part)[0] for g in range(groups)]
    down_parts = [cut(g * part)[1] for g in range(groups)]

    def span(parts, sent):
        all_parts = list(parts)
        for distance in range(2, span_size, 2):
            first = flipped(sent, distance)
            all_parts += [first] + [turned(first, shift) for shift in range(1, groups)]
        return all_parts + [flipped(p, 1) for p in all_parts]

    gate_up_all = span(gate_up_parts, sent_gate_up)
    down_all = span(down_parts, sent_down)

    residual_wide = residual.astype(jnp.float32)
    mean_square = jnp.mean(residual_wide * residual_wide, axis=1, keepdims=True)
    normed = (residual_wide * lax.rsqrt(mean_square + norm_eps) * norm_gain).astype(jnp.bfloat16)
    picked = expert_ids[:, :, None] == lax.iota(jnp.int32, expert_count)[None, None, :]
    flat_pick = picked.reshape(tok_rows * top_count, expert_count).astype(jnp.int32)
    before = jnp.cumsum(flat_pick, axis=0) - flat_pick
    target = expert_ids.reshape(tok_rows * top_count) * capacity + jnp.sum(
        before * flat_pick, axis=1
    )
    target = target.reshape(tok_rows, top_count)
    places = lax.iota(jnp.int32, expert_count * capacity)
    matches = target[:, :, None] == places[None, None, :]
    assignment = jnp.any(matches, axis=1).astype(jnp.bfloat16)
    packed = lax.dot_general(
        assignment, normed, (((0,), (0,)), ((), ())), preferred_element_type=jnp.float32
    ).astype(jnp.bfloat16)
    rows = lax.all_to_all(
        packed, "expert", split_axis=0, concat_axis=0, axis_index_groups=lines, tiled=True
    )

    logits = jnp.dot(normed, router, preferred_element_type=jnp.float32)
    affinity = jax.nn.sigmoid(logits)
    chosen = jnp.sum(jnp.where(picked, affinity[:, None, :], 0.0), axis=2)
    gate_values = route_scale * chosen / jnp.sum(chosen, axis=1, keepdims=True)

    activated = []
    for gate_up in gate_up_all:
        both = jnp.dot(rows, gate_up, preferred_element_type=jnp.float32)
        activated.append(
            (jax.nn.silu(both[:, :part]) * both[:, part:]).astype(jnp.bfloat16)
        )
    activated = jnp.concatenate(activated, axis=1)
    down = jnp.concatenate(down_all, axis=0)
    expert_out = jnp.dot(activated, down, preferred_element_type=jnp.float32).astype(jnp.bfloat16)
    returned = lax.all_to_all(
        expert_out, "expert", split_axis=0, concat_axis=0, axis_index_groups=lines, tiled=True
    )
    branch = jnp.zeros((tok_rows, model_width), jnp.float32)
    for k in range(top_count):
        found = jnp.dot(
            matches[:, k].astype(jnp.bfloat16), returned, preferred_element_type=jnp.float32
        )
        branch = branch + found * gate_values[:, k : k + 1]
    return (residual_wide + branch).astype(jnp.bfloat16)


def solution(mesh):
    in_specs = (
        P(("groups", "expert"), None),
        P(),
        P(),
        P(None, "expert"),
        P(None, "expert"),
        P("expert", None),
        P(("groups", "expert"), None),
    )
    out_specs = P(("groups", "expert"), None)
    return jax.shard_map(shards, mesh=mesh, in_specs=in_specs, out_specs=out_specs, check_vma=False)
```

time: 518 us -> 247 us (0.48)
  the two profiles are of different devices: /device:TPU:16 before, /device:TPU:0 now
where the time goes in v1:
time: 247 us; the launch traced here: 246 us
  waiting for transfers between devices  171 us (69%)
  matrix products  39.4 us (16%)
  starting transfers between devices  18.8 us (8%)
  local copies, waits for them, and re-layouts  8.93 us (4%)
  other arithmetic  7.4 us (3%)
    all_to_all x1, waiting for transfers between devices, shards(): lax.all_to_all(expert_out, 'expert', split_axis=0, concat_axis=0, axis_in...  61.2 us
    ppermute x10, waiting for transfers between devices, flipped(): return lax.ppermute(value, 'expert', pairs)  56.1 us
    ppermute x2, waiting for transfers between devices, turned(): return lax.ppermute(value, 'groups', pairs)  54 us
    dot_general x8, matrix products, shards(): both = jnp.dot(rows, gate_up, preferred_element_type=jnp.float32)  27.4 us
    all_to_all x1, starting transfers between devices, shards(): lax.all_to_all(packed, 'expert', split_axis=0, concat_axis=0, axis_index_...  6.45 us
    unnamed x37, local copies, waits for them, and re-layouts  5.4 us
  transfers between devices with their start and end apart: 14, of which 7 were waited for; matrix products, arithmetic and copies ran while one was open for 13% of the time, Pallas kernels for 0%

profile of v1, /device:TPU:0, one launch (start us, length us, event | category | flops | bytes accessed | tf_op | source)
XLA Modules:
  0.0 246.4 jit_solution(12098171140893377324)
XLA Ops:
  0.0 0.8 copy.29
  0.8 0.1 eq.49
  0.9 0.1 eq.45
  1.1 1.2 reduce-window.6
  2.4 0.1 copy.31
  2.7 0.1 reduce_sum.39
  2.9 0.7 multiply_add_fusion
  3.6 0.1 iota_compare_fusion
  3.8 1.4 fusion.3
  5.3 3.7 %convolution_convert_fusion = bf16[384,3584]{1,0:T(8,128)(2,1)} fusion(pred[128,384]{1,0:T(8,128)(4,1)S(1)} %get-tuple-element.19, bf16[128,3584]{1,0:T(8,128)(2,1)} %param.7, f32[3584]{0:T(1024)} %param.8, f32[128]{0:T(128)S(1)} %add_rsqrt_fusion), kind=kOutput, calls=%fused_computation | convolution fusion | flops 355532800 | bytes 3734016 | tf_op jit(solution)/shard_map/dot_general | solution.py:71
  9.0 6.5 %all-to-all-start = ((bf16[4,96,3584]{2,1,0:T(8,128)(2,1)}), bf16[4,96,3584]{2,1,0:T(8,128)(2,1)}, u32[]{:S(2)}, u32[]{:S(2)}) async-start(bf16[4,96,3584]{2,1,0:T(8,128)(2,1)} %bitcast.3), calls=%async_computation | async-start | bytes 5505024 | tf_op jit(solution)/shard_map/all_to_all | solution.py:74
  15.4 2.5 %constant_dynamic-slice_fusion = (bf16[3584,128]{1,0:T(8,128)(2,1)S(1)}, bf16[3584,128]{1,0:T(8,128)(2,1)S(1)}, bf16[3584,128]{1,0:T(8,128)(2,1)S(1)}, bf16[3584...) fusion(bf16[3584,256]{1,0:T(8,128)(2,1)S(1)} %copy-done.3, s32[]{:T(128)S(6)} %select_n.9, ...), kind=kLoop, calls=%fused_computation.66 | loop fusion | bytes 11010052 | tf_op jit(solution)/shard_map/dynamic_slice | solution.py:38
  18.0 0.2 pad_maximum_fusion.2
  18.2 1.6 collective-permute-start
  19.8 0.7 copy-done.1
  20.4 0.2 fusion.33
  20.7 1.6 collective-permute-start.6
  22.3 1.4 pad_maximum_fusion
  23.7 1.5 pad_maximum_fusion.1
  25.2 0.5 collective-permute-start.3
  25.7 53.7 %collective-permute-done.6 = bf16[128,3584]{1,0:T(8,128)(2,1)S(1)} collective-permute-done((bf16[128,3584]{1,0:T(8,128)(2,1)S(1)}, bf16[128,3584]{1,0:T(8,128)(2,1)S(1)}, u32[]{:S(2)}, u32[]{:S(2)}) %collective-permute-start.6) | collective-permute-done | bytes 917536 | tf_op jit(solution)/shard_map/ppermute | solution.py:12
  79.4 1.5 collective-permute-start.7
  80.9 0.1 constant_dynamic-update-slice_fusion.6
  81.1 19.2 %collective-permute-done.7 = bf16[128,3584]{1,0:T(8,128)(2,1)S(1)} collective-permute-done((bf16[128,3584]{1,0:T(8,128)(2,1)S(1)}, bf16[128,3584]{1,0:T(8,128)(2,1)S(1)}, u32[]{:S(2)}, u32[]{:S(2)}) %collective-permute-start.7) | collective-permute-done | bytes 917536 | tf_op jit(solution)/shard_map/ppermute | solution.py:18
  100.4 0.6 collective-permute-start.10
  100.9 1.5 collective-permute-start.1
  102.6 0.2 collective-permute-done.9
  102.8 0.1 collective-permute-start.11
  103.0 1.1 collective-permute-done.10
  104.1 0.1 collective-permute-start.4
  104.3 1.1 collective-permute-done.11
  105.4 2.9 %copy-done.10 = bf16[1024,3584]{1,0:T(8,128)(2,1)} copy-done((bf16[1024,3584]{1,0:T(8,128)(2,1)}, bf16[1024,3584]{1,0:T(8,128)(2,1)S(1)}, u32[]{:S(2)}) %copy-start.10) | copy-done | bytes 7340056
  108.4 34.9 %collective-permute-done.1 = bf16[3584,256]{1,0:T(8,128)(2,1)} collective-permute-done((bf16[3584,256]{1,0:T(8,128)(2,1)}, bf16[3584,256]{1,0:T(8,128)(2,1)}, u32[]{:S(2)}, u32[]{:S(2)}) %collective-permute-start.1) | collective-permute-done | bytes 1835040 | tf_op jit(solution)/shard_map/ppermute | solution.py:18
  143.3 3.0 %fusion.32 = f32[384,256]{0,1:T(8,128)S(1)} fusion(bf16[384,3584]{1,0:T(8,128)(2,1)} %bitcast.4, bf16[3584,128]{1,0:T(8,128)(2,1)S(1)} %copy-done.7, bf16[3584,128]{1,0:T(8,128)(2,1)S(1)} %copy-done.9), kind=kOutput, calls=%fused_computation.73 | convolution fusion | flops 708313088 | bytes 4980736 | tf_op jit(solution)/shard_map/dot_general | solution.py:85
  146.4 2.9 %fusion.31 = f32[384,256]{0,1:T(8,128)S(1)} fusion(bf16[384,3584]{1,0:T(8,128)(2,1)} %bitcast.4, bf16[3584,128]{1,0:T(8,128)(2,1)S(1)} %get-tuple-element.15, bf16[3584,128]{1,0:T(8,128)(2,1)S(1)} %copy-done.5), kind=kOutput, calls=%fused_computation.72 | convolution fusion | flops 708313088 | bytes 4980736 | tf_op jit(solution)/shard_map/dot_general | solution.py:85
  149.4 3.5 %fusion.34 = f32[384,256]{0,1:T(8,128)S(1)} fusion(bf16[384,3584]{1,0:T(8,128)(2,1)} %bitcast.4, bf16[3584,256]{1,0:T(8,128)(2,1)} %collective-permute-done), kind=kOutput, calls=%fused_computation.75 | convolution fusion | flops 704643072 | bytes 4980736 | tf_op jit(solution)/shard_map/dot_general | solution.py:85
  153.0 3.5 %fusion.35 = f32[384,256]{0,1:T(8,128)S(1)} fusion(bf16[384,3584]{1,0:T(8,128)(2,1)} %bitcast.4, bf16[3584,256]{1,0:T(8,128)(2,1)} %collective-permute-done.1), kind=kOutput, calls=%fused_computation.76 | convolution fusion | flops 704643072 | bytes 4980736 | tf_op jit(solution)/shard_map/dot_general | solution.py:85
  156.6 3.5 %fusion.36 = f32[384,256]{0,1:T(8,128)S(1)} fusion(bf16[384,3584]{1,0:T(8,128)(2,1)} %bitcast.4, bf16[3584,256]{1,0:T(8,128)(2,1)} %collective-permute-done.2), kind=kOutput, calls=%fused_computation.77 | convolution fusion | flops 704643072 | bytes 4980736 | tf_op jit(solution)/shard_map/dot_general | solution.py:85
  160.2 3.6 %fusion.37 = f32[384,256]{0,1:T(8,128)S(1)} fusion(bf16[384,3584]{1,0:T(8,128)(2,1)} %bitcast.4, bf16[3584,256]{1,0:T(8,128)(2,1)} %collective-permute-done.3), kind=kOutput, calls=%fused_computation.78 | convolution fusion | flops 704643072 | bytes 4980736 | tf_op jit(solution)/shard_map/dot_general | solution.py:85
  163.9 3.6 %fusion.38 = f32[384,256]{0,1:T(8,128)S(1)} fusion(bf16[384,3584]{1,0:T(8,128)(2,1)} %bitcast.4, bf16[3584,256]{1,0:T(8,128)(2,1)} %collective-permute-done.4), kind=kOutput, calls=%fused_computation.79 | convolution fusion | flops 704643072 | bytes 4980736 | tf_op jit(solution)/shard_map/dot_general | solution.py:85
  167.6 3.7 %fusion.39 = f32[384,256]{0,1:T(8,128)S(1)} fusion(bf16[384,3584]{1,0:T(8,128)(2,1)} %bitcast.4, bf16[3584,256]{1,0:T(8,128)(2,1)} %collective-permute-done.5), kind=kOutput, calls=%fused_computation.80 | convolution fusion | flops 704643072 | bytes 4980736 | tf_op jit(solution)/shard_map/dot_general | solution.py:85
  171.4 4.4 %convolution_convert_fusion.1 = bf16[384,3584]{1,0:T(8,128)(2,1)} fusion(bf16[384,1024]{0,1:T(8,128)(2,1)S(1)} %fusion.26, bf16[1024,3584]{1,0:T(8,128)(2,1)S(1)} %bitcast.57), kind=kOutput, calls=%fused_computation.1 | convolution fusion | flops 2819948544 | bytes 10878976 | tf_op jit(solution)/shard_map/dot_general | solution.py:91
  175.8 4.8 %all-to-all-start.1 = ((bf16[4,96,3584]{2,1,0:T(8,128)(2,1)}), bf16[4,96,3584]{2,1,0:T(8,128)(2,1)S(1)}, u32[]{:S(2)}, u32[]{:S(2)}) async-start(bf16[4,96,3584]{2,1,0:T(8,128)(2,1)} %bitcast.55), calls=%async_computation.1 | async-start | bytes 5505024 | tf_op jit(solution)/shard_map/all_to_all | solution.py:92
  180.6 1.6 fusion.8
  182.3 61.2 %all-to-all-done.1 = bf16[4,96,3584]{2,1,0:T(8,128)(2,1)S(1)} async-done(((bf16[4,96,3584]{2,1,0:T(8,128)(2,1)}), bf16[4,96,3584]{2,1,0:T(8,128)(2,1)S(1)}, u32[]{:S(2)}, u32[]{:S(2)}) %all-to-all-start.1) | async-done | bytes 2752544 | tf_op jit(solution)/shard_map/all_to_all | solution.py:92
  243.5 0.7 convolution_multiply_fusion
  244.2 0.5 copy-done.2
  244.7 1.7 fusion.2
  (65 shorter events, 1.5 us)
Async XLA Ops:
  0.0 180.6 %copy-start = (bf16[3584,4]{0,1:T(4,128)(2,1)S(1)}, bf16[3584,4]{0,1:T(4,128)(2,1)}, u32[]{:S(2)}) copy-start(bf16[3584,4]{0,1:T(4,128)(2,1)} %param.9) | copy-start | bytes 86020
  9.0 6.5 %copy-start.3 = (bf16[3584,256]{1,0:T(8,128)(2,1)S(1)}, bf16[3584,256]{1,0:T(8,128)(2,1)}, u32[]{:S(2)}) copy-start(bf16[3584,256]{1,0:T(8,128)(2,1)} %param.11) | copy-start | bytes 5505028
  9.0 134.3 %all-to-all-start = ((bf16[4,96,3584]{2,1,0:T(8,128)(2,1)}), bf16[4,96,3584]{2,1,0:T(8,128)(2,1)}, u32[]{:S(2)}, u32[]{:S(2)}) async-start(bf16[4,96,3584]{2,1,0:T(8,128)(2,1)} %bitcast.3), calls=%async_computation | async-start | bytes 5505024 | tf_op jit(solution)/shard_map/all_to_all | solution.py:74
  17.9 4.3 %copy-start.6 = (bf16[3584,128]{1,0:T(8,128)(2,1)}, bf16[3584,128]{1,0:T(8,128)(2,1)S(1)}, u32[]{:S(2)}) copy-start(bf16[3584,128]{1,0:T(8,128)(2,1)S(1)} %get-tuple-element.14) | copy-start | bytes 2752516
  17.9 4.3 %copy-start.8 = (bf16[3584,128]{1,0:T(8,128)(2,1)}, bf16[3584,128]{1,0:T(8,128)(2,1)S(1)}, u32[]{:S(2)}) copy-start(bf16[3584,128]{1,0:T(8,128)(2,1)S(1)} %get-tuple-element.21) | copy-start | bytes 2752516
  18.0 5.7 %copy-start.4 = (bf16[3584,128]{1,0:T(8,128)(2,1)}, bf16[3584,128]{1,0:T(8,128)(2,1)S(1)}, u32[]{:S(2)}) copy-start(bf16[3584,128]{1,0:T(8,128)(2,1)S(1)} %get-tuple-element.20) | copy-start | bytes 2752516
  18.0 2.5 %copy-start.1 = (bf16[256,3584]{1,0:T(8,128)(2,1)S(1)}, bf16[256,3584]{1,0:T(8,128)(2,1)}, u32[]{:S(2)}) copy-start(bf16[256,3584]{1,0:T(8,128)(2,1)} %param.12) | copy-start | bytes 5505028
  18.2 82.7 %collective-permute-start = (bf16[3584,256]{1,0:T(8,128)(2,1)S(1)}, bf16[3584,256]{1,0:T(8,128)(2,1)}, u32[]{:S(2)}, u32[]{:S(2)}) collective-permute-start(bf16[3584,256]{1,0:T(8,128)(2,1)S(1)} %pad_maximum_fusion.2), channel_id=1, source_target_pairs={{0,2},{1,3},{2,0},{3,1},{4,6},{5,7},{6,4},{7,5},{8,10},{9,11},{10,... | collective-permute-start | bytes 5505032 | tf_op jit(solution)/shard_map/ppermute | solution.py:12
  20.7 58.7 %collective-permute-start.6 = (bf16[128,3584]{1,0:T(8,128)(2,1)S(1)}, bf16[128,3584]{1,0:T(8,128)(2,1)S(1)}, u32[]{:S(2)}, u32[]{:S(2)}) collective-permute-start(bf16[128,3584]{1,0:T(8,128)(2,1)S(1)} %get-tuple-element.9), channel_id=1, source_target_pairs={{0,2},{1,3},{2,0},{3,1},{4,6},{5,7},{6,4},{7,5},{8,10},{9,11},{10,... | collective-permute-start | bytes 2752520 | tf_op jit(solution)/shard_map/ppermute | solution.py:12
  23.7 132.9 %collective-permute-start.2 = (bf16[3584,256]{1,0:T(8,128)(2,1)}, bf16[3584,256]{1,0:T(8,128)(2,1)}, u32[]{:S(2)}, u32[]{:S(2)}) collective-permute-start(bf16[3584,256]{1,0:T(8,128)(2,1)} %pad_maximum_fusion), channel_id=1, source_target_pairs={{0,1},{1,0},{2,3},{3,2},{4,5},{5,4},{6,7},{7,6},{8,9},{9,8},{10,11... | collective-permute-start | bytes 5505032 | tf_op jit(solution)/shard_map/ppermute | solution.py:12
  25.2 135.0 %collective-permute-start.3 = (bf16[3584,256]{1,0:T(8,128)(2,1)}, bf16[3584,256]{1,0:T(8,128)(2,1)}, u32[]{:S(2)}, u32[]{:S(2)}) collective-permute-start(bf16[3584,256]{1,0:T(8,128)(2,1)} %pad_maximum_fusion.1), channel_id=1, source_target_pairs={{0,1},{1,0},{2,3},{3,2},{4,5},{5,4},{6,7},{7,6},{8,9},{9,8},{10,11... | collective-permute-start | bytes 5505032 | tf_op jit(solution)/shard_map/ppermute | solution.py:12
  25.7 74.7 %collective-permute-start.8 = (bf16[128,3584]{1,0:T(8,128)(2,1)S(1)}, bf16[128,3584]{1,0:T(8,128)(2,1)S(1)}, u32[]{:S(2)}, u32[]{:S(2)}) collective-permute-start(bf16[128,3584]{1,0:T(8,128)(2,1)S(1)} %get-tuple-element.8), channel_id=1, source_target_pairs={{0,1},{1,0},{2,3},{3,2},{4,5},{5,4},{6,7},{7,6},{8,9},{9,8},{10,11... | collective-permute-start | bytes 2752520 | tf_op jit(solution)/shard_map/ppermute | solution.py:12
  79.4 20.9 %collective-permute-start.7 = (bf16[128,3584]{1,0:T(8,128)(2,1)S(1)}, bf16[128,3584]{1,0:T(8,128)(2,1)S(1)}, u32[]{:S(2)}, u32[]{:S(2)}) collective-permute-start(bf16[128,3584]{1,0:T(8,128)(2,1)S(1)} %collective-permute-done.6), channel_id=1, source_target_pairs={{0,16},{16,0},{1,17},{17,1},{2,18},{18,2},{3,19},{19,3},{4,20},{20... | collective-permute-start | bytes 2752520 | tf_op jit(solution)/shard_map/ppermute | solution.py:18
  100.3 2.5 %collective-permute-start.9 = (bf16[128,3584]{1,0:T(8,128)(2,1)S(1)}, bf16[128,3584]{1,0:T(8,128)(2,1)S(1)}, u32[]{:S(2)}, u32[]{:S(2)}) collective-permute-start(bf16[128,3584]{1,0:T(8,128)(2,1)S(1)} %get-tuple-element.7), channel_id=1, source_target_pairs={{0,1},{1,0},{2,3},{3,2},{4,5},{5,4},{6,7},{7,6},{8,9},{9,8},{10,11... | collective-permute-start | bytes 2752520 | tf_op jit(solution)/shard_map/ppermute | solution.py:12
  100.4 3.7 %collective-permute-start.10 = (bf16[128,3584]{1,0:T(8,128)(2,1)S(1)}, bf16[128,3584]{1,0:T(8,128)(2,1)S(1)}, u32[]{:S(2)}, u32[]{:S(2)}) collective-permute-start(bf16[128,3584]{1,0:T(8,128)(2,1)S(1)} %collective-permute-done.6), channel_id=1, source_target_pairs={{0,1},{1,0},{2,3},{3,2},{4,5},{5,4},{6,7},{7,6},{8,9},{9,8},{10,11... | collective-permute-start | bytes 2752520 | tf_op jit(solution)/shard_map/ppermute | solution.py:12
  100.9 42.3 %collective-permute-start.1 = (bf16[3584,256]{1,0:T(8,128)(2,1)}, bf16[3584,256]{1,0:T(8,128)(2,1)}, u32[]{:S(2)}, u32[]{:S(2)}) collective-permute-start(bf16[3584,256]{1,0:T(8,128)(2,1)} %collective-permute-done), channel_id=1, source_target_pairs={{0,16},{16,0},{1,17},{17,1},{2,18},{18,2},{3,19},{19,3},{4,20},{20... | collective-permute-start | bytes 5505032 | tf_op jit(solution)/shard_map/ppermute | solution.py:18
  102.5 40.7 %copy-start.7 = (bf16[3584,128]{1,0:T(8,128)(2,1)S(1)}, bf16[3584,128]{1,0:T(8,128)(2,1)}, u32[]{:S(2)}) copy-start(bf16[3584,128]{1,0:T(8,128)(2,1)} %copy-done.6) | copy-start | bytes 2752516
  102.5 40.7 %copy-start.9 = (bf16[3584,128]{1,0:T(8,128)(2,1)S(1)}, bf16[3584,128]{1,0:T(8,128)(2,1)}, u32[]{:S(2)}) copy-start(bf16[3584,128]{1,0:T(8,128)(2,1)} %copy-done.8) | copy-start | bytes 2752516
  102.8 2.6 %collective-permute-start.11 = (bf16[128,3584]{1,0:T(8,128)(2,1)S(1)}, bf16[128,3584]{1,0:T(8,128)(2,1)S(1)}, u32[]{:S(2)}, u32[]{:S(2)}) collective-permute-start(bf16[128,3584]{1,0:T(8,128)(2,1)S(1)} %collective-permute-done.7), channel_id=1, source_target_pairs={{0,1},{1,0},{2,3},{3,2},{4,5},{5,4},{6,7},{7,6},{8,9},{9,8},{10,11... | collective-permute-start | bytes 2752520 | tf_op jit(solution)/shard_map/ppermute | solution.py:12
  104.1 59.8 %collective-permute-start.4 = (bf16[3584,256]{1,0:T(8,128)(2,1)}, bf16[3584,256]{1,0:T(8,128)(2,1)}, u32[]{:S(2)}, u32[]{:S(2)}) collective-permute-start(bf16[3584,256]{1,0:T(8,128)(2,1)} %collective-permute-done), channel_id=1, source_target_pairs={{0,1},{1,0},{2,3},{3,2},{4,5},{5,4},{6,7},{7,6},{8,9},{9,8},{10,11... | collective-permute-start | bytes 5505032 | tf_op jit(solution)/shard_map/ppermute | solution.py:12
  105.4 2.9 %copy-start.10 = (bf16[1024,3584]{1,0:T(8,128)(2,1)}, bf16[1024,3584]{1,0:T(8,128)(2,1)S(1)}, u32[]{:S(2)}) copy-start(bf16[1024,3584]{1,0:T(8,128)(2,1)S(1)} %constant_dynamic-update-slice_fusion) | copy-start | bytes 22020100
  143.2 24.4 %collective-permute-start.5 = (bf16[3584,256]{1,0:T(8,128)(2,1)}, bf16[3584,256]{1,0:T(8,128)(2,1)}, u32[]{:S(2)}, u32[]{:S(2)}) collective-permute-start(bf16[3584,256]{1,0:T(8,128)(2,1)} %collective-permute-done.1), channel_id=1, source_target_pairs={{0,1},{1,0},{2,3},{3,2},{4,5},{5,4},{6,7},{7,6},{8,9},{9,8},{10,11... | collective-permute-start | bytes 5505032 | tf_op jit(solution)/shard_map/ppermute | solution.py:12
  143.3 3.1 %copy-start.5 = (bf16[3584,128]{1,0:T(8,128)(2,1)S(1)}, bf16[3584,128]{1,0:T(8,128)(2,1)}, u32[]{:S(2)}) copy-start(bf16[3584,128]{1,0:T(8,128)(2,1)} %copy-done.4) | copy-start | bytes 2752516
  160.2 11.2 %slice-start = ((s8[7340032]{0:T(1024)(128)(4,1)}), s8[4194304]{0:T(1024)(128)(4,1)S(1)}, s32[]{:S(2)}) async-start(s8[7340032]{0:T(1024)(128)(4,1)} %bitcast.56), calls=%async_computation.2 | async-start | bytes 8388608
  163.9 7.5 %slice-start.1 = ((s8[7340032]{0:T(1024)(128)(4,1)}), s8[3145728]{0:T(1024)(128)(4,1)S(1)}, s32[]{:S(2)}) async-start(s8[7340032]{0:T(1024)(128)(4,1)} %bitcast.56), calls=%async_computation.3 | async-start | bytes 6291456
  175.8 4.8 %copy-start.11 = (f32[3584]{0:T(1024)S(1)}, f32[3584]{0:T(1024)}, u32[]{:S(2)}) copy-start(f32[3584]{0:T(1024)} %param.8) | copy-start | bytes 43012
  175.8 6.4 %copy-start.12 = (s32[128,2]{0,1:T(2,128)S(1)}, s32[128,2]{0,1:T(2,128)}, u32[]{:S(2)}) copy-start(s32[128,2]{0,1:T(2,128)} %param.13) | copy-start | bytes 3076
  175.8 67.7 %all-to-all-start.1 = ((bf16[4,96,3584]{2,1,0:T(8,128)(2,1)}), bf16[4,96,3584]{2,1,0:T(8,128)(2,1)S(1)}, u32[]{:S(2)}, u32[]{:S(2)}) async-start(bf16[4,96,3584]{2,1,0:T(8,128)(2,1)} %bitcast.55), calls=%async_computation.1 | async-start | bytes 5505024 | tf_op jit(solution)/shard_map/all_to_all | solution.py:92
  243.5 1.2 copy-start.2

commit v2 on v1

v2 whole, which is shorter than its diff:
```python
import functools

import jax
import jax.numpy as jnp
from jax import lax
from jax.experimental import pallas as pl
from jax.experimental.pallas import tpu as pltpu
from jax.sharding import PartitionSpec as P

route_scale = 2.5
norm_eps = 1e-06
first_share = 2
down_chunks = 2
vmem_bytes = 56 * 1024 * 1024
late_vmem_bytes = 24 * 1024 * 1024


def flipped(value, distance):
    pairs = [(source, source ^ distance) for source in range(lax.axis_size("expert"))]
    return lax.ppermute(value, "expert", pairs)


def turned(value, shift):
    count = lax.axis_size("groups")
    pairs = [(source, (source + shift) % count) for source in range(count)]
    return lax.ppermute(value, "groups", pairs)


def cuts(total, count, unit):
    marks = [total // unit * i // count * unit for i in range(count)] + [total]
    return [(low, high - low) for low, high in zip(marks[:-1], marks[1:])]


def prepare_kernel(block_rows, station, residual, gain, router_t, ids_t, table, packed):
    rows, width = residual.shape
    experts = router_t.shape[0]
    wide = residual[...].astype(jnp.float32)
    mean_square = jnp.mean(wide * wide, axis=1, keepdims=True)
    scale = gain[...].reshape(1, width)
    normed = (wide * lax.rsqrt(mean_square + norm_eps) * scale).astype(jnp.bfloat16)
    here = station[0]
    lane_expert = lax.broadcasted_iota(jnp.int32, (experts, rows), 0) ^ here
    named_t = jnp.zeros((experts, rows), jnp.float32)
    for k in range(ids_t.shape[0]):
        named_t += jnp.where(ids_t[k : k + 1, :] == lane_expert, 1.0, 0.0)
    named_16 = named_t.astype(jnp.bfloat16)
    one = lax.broadcasted_iota(jnp.int32, (rows, rows), 0)
    two = lax.broadcasted_iota(jnp.int32, (rows, rows), 1)
    earlier_t = jnp.where(one < two, 1.0, 0.0).astype(jnp.bfloat16)
    slot_t = jnp.dot(named_16, earlier_t, preferred_element_type=jnp.float32)
    slot_t = jnp.where(named_t > 0.0, slot_t, -1.0)
    place = lax.broadcasted_iota(jnp.int32, (block_rows, rows), 0).astype(jnp.float32)
    for e in range(experts):
        hit = jnp.where(place == slot_t[e : e + 1, :], 1.0, 0.0).astype(jnp.bfloat16)
        block = jnp.dot(hit, normed, preferred_element_type=jnp.float32).astype(jnp.bfloat16)
        start = pl.multiple_of((here ^ e) * block_rows, 16)
        packed[pl.ds(start, block_rows), :] = block
    across = (((1,), (1,)), ((), ()))
    same = jnp.where(one == two, 1.0, 0.0).astype(jnp.bfloat16)
    earlier = jnp.where(two < one, 1.0, 0.0).astype(jnp.bfloat16)
    named = lax.dot_general(same, named_16, across, preferred_element_type=jnp.float32)
    slot = lax.dot_general(earlier, named_16, across, preferred_element_type=jnp.float32)
    slot = jnp.where(named > 0.0, slot, -1.0)
    logits = lax.dot_general(normed, router_t[...], across, preferred_element_type=jnp.float32)
    affinity = jax.nn.sigmoid(logits)
    column = lax.broadcasted_iota(jnp.int32, (rows, experts), 1)
    chosen = []
    for e in range(experts):
        value = jnp.sum(jnp.where(column == (here ^ e), affinity, 0.0), axis=1, keepdims=True)
        chosen.append(jnp.where(named[:, e : e + 1] > 0.0, value, 0.0))
    total = sum(chosen[1:], chosen[0])
    lanes = lax.broadcasted_iota(jnp.int32, (rows, table.shape[1]), 1)
    filled = jnp.zeros((rows, table.shape[1]), jnp.float32)
    for e in range(experts):
        filled = jnp.where(lanes == e, slot[:, e : e + 1], filled)
        filled = jnp.where(lanes == experts + e, route_scale * chosen[e] / total, filled)
    table[pl.ds(0, rows), :] = filled
    table[pl.ds(rows, experts), :] = slot_t


def prepare(residual, norm_gain, router, expert_ids, station, block_rows):
    rows, width = residual.shape
    experts = router.shape[1]
    whole = pl.BlockSpec(memory_space=pltpu.VMEM)
    return pl.pallas_call(
        functools.partial(prepare_kernel, block_rows),
        out_shape=[
            jax.ShapeDtypeStruct((rows + experts, rows), jnp.float32),
            jax.ShapeDtypeStruct((experts * block_rows, width), jnp.bfloat16),
        ],
        in_specs=[pl.BlockSpec(memory_space=pltpu.SMEM)] + [whole] * 4,
        out_specs=[whole] * 2,
        compiler_params=pltpu.CompilerParams(vmem_limit_bytes=vmem_bytes),
    )(station[None], residual, norm_gain, router.T, expert_ids.T)


def moved(copies, sems):
    return [pltpu.make_async_copy(a, b, sems.at[i]) for i, (a, b) in enumerate(copies)]


def down_pieces(refs, target, copies, group, hidden, groups):
    pieces = []
    for ref, (member, shift, rows, column, columns) in zip(refs, copies):
        start = member * hidden
        if shift is not None:
            part = lax.rem(group + groups - shift, groups)
            start = pl.multiple_of(part * (hidden // groups) + start, 16)
        pieces.append((ref.at[:, pl.ds(column, columns)], target.at[pl.ds(start, rows), :]))
    return pieces


def down_product(act, wd, outs):
    block_rows = outs[0].shape[0]
    width = wd.shape[1]
    step = 256 if width % 256 == 0 else 128
    for base in range(0, width, step):
        span = pl.ds(base, step)
        value = jnp.dot(act[...], wd[:, span], preferred_element_type=jnp.float32)
        value = value.astype(jnp.bfloat16)
        for i, out in enumerate(outs):
            out[:, span] = value[i * block_rows : (i + 1) * block_rows, :]


def expert_kernel(plan, group, station, rows, *refs):
    block_rows, hidden, width, groups, weight_copies, down_copies = plan
    weight_refs, refs = refs[: len(weight_copies)], refs[len(weight_copies) :]
    down_refs, refs = refs[: len(down_copies)], refs[len(down_copies) :]
    act, outs, (x, w, wd, row_sems, weight_sems, down_sems) = refs[0], refs[1:-6], refs[-6:]
    members = w.shape[0]
    g = group[0]
    row_pieces = []
    for r in range(x.shape[0] // block_rows):
        start = pl.multiple_of((station[0] ^ r) * block_rows, 16)
        row_pieces.append(
            (rows.at[pl.ds(start, block_rows), :], x.at[pl.ds(r * block_rows, block_rows), :])
        )
    row_waits = moved(row_pieces, row_sems)
    stages = [[] for _ in range(members)]
    pieces = []
    for ref, (member, shift, base, size, column) in zip(weight_refs, weight_copies):
        start = base
        if shift is not None:
            part = lax.rem(g + groups - shift, groups)
            start = pl.multiple_of(part * (width // groups) + base, 16)
        pieces.append((ref, w.at[member, pl.ds(start, size), pl.ds(column, hidden)]))
    for copy, (member, *_) in zip(moved(pieces, weight_sems), weight_copies):
        stages[member].append(copy)
    stages.append(moved(down_pieces(down_refs, wd, down_copies, g, hidden, groups), down_sems))

    for copy in row_waits + stages[0]:
        copy.start()
    for copy in row_waits:
        copy.wait()
    for copy in stages[1]:
        copy.start()
    for member in range(members):
        for copy in stages[member]:
            copy.wait()
        if member + 2 <= members:
            for copy in stages[member + 2]:
                copy.start()
        gate = jnp.dot(x[...], w[member, :, :hidden], preferred_element_type=jnp.float32)
        up = jnp.dot(x[...], w[member, :, hidden:], preferred_element_type=jnp.float32)
        act[:, member * hidden : (member + 1) * hidden] = (
            gate / (1.0 + jnp.exp(-gate)) * up
        ).astype(jnp.bfloat16)
    for copy in stages[members]:
        copy.wait()
    down_product(act, wd, outs)


def expert_first(group, station, rows, weights, copies, downs, down_copies, sizes, members):
    block_rows, hidden, groups = sizes
    total_rows, width = rows.shape
    columns = down_copies[0][-1]
    blocks = total_rows // block_rows
    plan = (block_rows, hidden, width, groups, copies, down_copies)
    out = pl.pallas_call(
        functools.partial(expert_kernel, plan),
        out_shape=[jax.ShapeDtypeStruct((total_rows, members * hidden), jnp.bfloat16)]
        + [jax.ShapeDtypeStruct((block_rows, columns), jnp.bfloat16)] * blocks,
        in_specs=[pl.BlockSpec(memory_space=pltpu.SMEM)] * 2
        + [pl.BlockSpec(memory_space=pl.ANY)] * (1 + len(copies) + len(down_copies)),
        out_specs=[pl.BlockSpec(memory_space=pltpu.VMEM)] * (1 + blocks),
        scratch_shapes=[
            pltpu.VMEM((total_rows, width), jnp.bfloat16),
            pltpu.VMEM((members, width, 2 * hidden), jnp.bfloat16),
            pltpu.VMEM((members * hidden, columns), jnp.bfloat16),
            pltpu.SemaphoreType.DMA((blocks,)),
            pltpu.SemaphoreType.DMA((len(copies),)),
            pltpu.SemaphoreType.DMA((len(down_copies),)),
        ],
        compiler_params=pltpu.CompilerParams(vmem_limit_bytes=vmem_bytes),
    )(group, station, rows, *weights, *downs)
    return out[0], out[1:]


def down_kernel(plan, group, act, *refs):
    hidden, groups, copies = plan
    down_refs, outs, (wd, sems) = refs[: len(copies)], refs[len(copies) : -2], refs[-2:]
    waits = moved(down_pieces(down_refs, wd, copies, group[0], hidden, groups), sems)
    for copy in waits:
        copy.start()
    for copy in waits:
        copy.wait()
    down_product(act, wd, outs)


def expert_later(group, act, downs, copies, sizes):
    block_rows, hidden, groups = sizes
    blocks = act.shape[0] // block_rows
    columns = copies[0][-1]
    whole = pl.BlockSpec(memory_space=pltpu.VMEM)
    return pl.pallas_call(
        functools.partial(down_kernel, (hidden, groups, copies)),
        out_shape=[jax.ShapeDtypeStruct((block_rows, columns), jnp.bfloat16)] * blocks,
        in_specs=[pl.BlockSpec(memory_space=pltpu.SMEM), whole]
        + [pl.BlockSpec(memory_space=pl.ANY)] * len(downs),
        out_specs=[whole] * blocks,
        scratch_shapes=[
            pltpu.VMEM((act.shape[1], columns), jnp.bfloat16),
            pltpu.SemaphoreType.DMA((len(copies),)),
        ],
        compiler_params=pltpu.CompilerParams(vmem_limit_bytes=late_vmem_bytes),
    )(group, act, *downs)


def weighted_sum(classes, is_hub, table, blocks, high, low):
    block_rows = blocks[0].shape[0]
    rows = table.shape[1]
    experts = table.shape[0] - rows
    place = lax.broadcasted_iota(jnp.int32, (rows, block_rows), 1).astype(jnp.float32)
    for i, (e, at_hub) in enumerate(classes):
        gate = table[pl.ds(0, rows), experts + e : experts + e + 1]
        if not at_hub:
            gate = jnp.where(is_hub[0] == 1, 0.0, gate)
        weight = jnp.where(place == table[pl.ds(0, rows), e : e + 1], gate, 0.0)
        upper = weight.astype(jnp.bfloat16)
        columns = pl.ds(i * block_rows, block_rows)
        high[:, columns] = upper
        low[:, columns] = (weight - upper.astype(jnp.float32)).astype(jnp.bfloat16)
    stacked = jnp.concatenate([block[...] for block in blocks], axis=0)
    total = jnp.dot(high[...], stacked, preferred_element_type=jnp.float32)
    return total + jnp.dot(low[...], stacked, preferred_element_type=jnp.float32)


def partner_kernel(classes, is_hub, table, *refs):
    blocks, (out, high, low) = refs[:-3], refs[-3:]
    out[...] = weighted_sum(classes, is_hub, table, blocks, high, low).astype(jnp.bfloat16)


def partner_sum(classes, is_hub, table, blocks):
    block_rows, width = blocks[0].shape
    rows = table.shape[1]
    whole = pl.BlockSpec(memory_space=pltpu.VMEM)
    return pl.pallas_call(
        functools.partial(partner_kernel, classes),
        out_shape=jax.ShapeDtypeStruct((rows, width), jnp.bfloat16),
        in_specs=[pl.BlockSpec(memory_space=pltpu.SMEM)] + [whole] * (1 + len(blocks)),
        out_specs=whole,
        scratch_shapes=[pltpu.VMEM((rows, block_rows * len(blocks)), jnp.bfloat16)] * 2,
        compiler_params=pltpu.CompilerParams(vmem_limit_bytes=late_vmem_bytes),
    )(is_hub, table, *blocks)


def result_kernel(plan, is_hub, table, *refs):
    classes, base, size, first = plan
    count = len(classes)
    blocks = refs[:count]
    hub_sum, residual = refs[count : count + 2]
    out, high, low, held, result, sems = refs[-6:]
    span = pl.ds(base, size)
    fetch = pltpu.make_async_copy(residual.at[:, span], held, sems.at[0])
    fetch.start()
    total = weighted_sum(classes, is_hub, table, blocks, high, low)
    fetch.wait()
    total += held[...].astype(jnp.float32) + hub_sum[...].astype(jnp.float32)
    result[...] = total.astype(jnp.bfloat16)
    store = pltpu.make_async_copy(result, out.at[:, span], sems.at[1])
    store.start()
    store.wait()


def result(classes, is_hub, table, blocks, hub_sum, residual, base, size, so_far):
    block_rows = blocks[0].shape[0]
    rows, width = residual.shape
    whole = pl.BlockSpec(memory_space=pltpu.VMEM)
    anywhere = pl.BlockSpec(memory_space=pl.ANY)
    first = so_far is None
    earlier = [] if first else [so_far]
    return pl.pallas_call(
        functools.partial(result_kernel, (classes, base, size, first)),
        out_shape=jax.ShapeDtypeStruct((rows, width), jnp.bfloat16),
        in_specs=[pl.BlockSpec(memory_space=pltpu.SMEM)]
        + [whole] * (2 + len(blocks))
        + [anywhere] * (1 + len(earlier)),
        out_specs=anywhere,
        scratch_shapes=[pltpu.VMEM((rows, block_rows * len(blocks)), jnp.bfloat16)] * 2
        + [pltpu.VMEM((rows, size), jnp.bfloat16)] * 2
        + [pltpu.SemaphoreType.DMA((2,))],
        input_output_aliases={} if first else {len(blocks) + 4: 0},
        compiler_params=pltpu.CompilerParams(vmem_limit_bytes=late_vmem_bytes),
    )(is_hub, table, *blocks, hub_sum, residual, *earlier)


def named(name, function, *args):
    with jax.named_scope(name):
        return function(*args)


def after(value, *others):
    return lax.optimization_barrier((value,) + others)[0]


def shards(residual, norm_gain, router, w_gate, w_up, w_down, expert_ids):
    tok_rows, width = residual.shape
    top = expert_ids.shape[1]
    experts = router.shape[1]
    device_count = lax.axis_size("expert")
    groups = lax.axis_size("groups")
    members = device_count // experts
    hidden = w_gate.shape[1]
    capacity = 3 * tok_rows * top // (2 * experts)
    block_rows = -(-capacity // 16) * 16
    my_group = lax.axis_index("groups")
    station = (lax.axis_index("expert") // members).astype(jnp.int32)
    half = experts // 2
    last = experts - 1
    hubs = (half - 1, half)
    is_hub = jnp.logical_or(station == hubs[0], station == hubs[1]).astype(jnp.int32)[None]

    def along(value, route):
        pairs = [
            (a * members + m, b * members + m) for a, b in route.items() for m in range(members)
        ]
        return lax.ppermute(value, "expert", pairs)

    near = {r: {z: z ^ r for z in range(experts)} for r in range(1, half)}
    mixed = {
        r: {z: z ^ (r ^ last if z in hubs else r) for z in range(experts)}
        for r in range(half, last)
    }
    far = {z: z ^ last for z in range(experts) if z not in hubs}
    between = {hubs[0]: hubs[1], hubs[1]: hubs[0]}

    part_width, part_hidden = width // groups, hidden // groups
    jobs = []
    for distance in range(2, members, 2):
        for i, w in enumerate((w_gate, w_up)):
            early = part_width // ((first_share if i == 0 else 2) * 16) * 16
            for base, size in ((0, early), (early, part_width - early)):
                sent = lax.dynamic_slice_in_dim(w, my_group * part_width + base, size, 0)
                jobs.append((sent, distance, (base, size, i * hidden), None))
    columns = cuts(width, down_chunks, 128)
    for c, (base, size) in enumerate(columns):
        for distance in range(2, members, 2):
            sent = lax.dynamic_slice(w_down, (my_group * part_hidden, base), (part_hidden, size))
            jobs.append((sent, distance, None, c))
    table, packed = prepare(after(residual, jobs[0][0]), norm_gain, router, expert_ids, station, block_rows)
    lines = [[e * members + m for e in range(experts)] for m in range(members)]
    hub_table = named("table", along, table, between)

    last_job = len(jobs) - 1
    group = my_group[None].astype(jnp.int32)
    weights = [w_gate, w_up] + [named("own", flipped, w, 1) for w in (w_gate, w_up)]
    copies = [(m, None, 0, width, i * hidden) for m in range(2) for i in range(2)]
    own_down = named("own", flipped, w_down, 1)
    downs = [[w_down, own_down] for _ in columns]
    down_copies = [[(m, None, hidden, base, size) for m in range(2)] for base, size in columns]
    Y, X = [], []
    rows = None
    for n, (sent, distance, gate_up, chunk) in enumerate(jobs):
        Y.append(named(f"Y{n}", flipped, after(sent, *Y[-1:], *(X[-2] if n > 1 else [])), distance))
        if n == 0:
            packed = after(packed, Y[0], hub_table)
            rows = lax.all_to_all(packed, "expert", 0, 0, axis_index_groups=lines, tiled=True)
        ready = after(Y[n], *X[-1]) if X else Y[n]
        X.append([named(f"X{n}", turned, ready, shift) for shift in range(1, groups)])
    sizes = (block_rows, hidden, groups)
    first_jobs = sum(1 for job in jobs if job[3] in (None, 0))
    act = None
    for n, (sent, distance, gate_up, chunk) in enumerate(jobs):
        if n == first_jobs:
            act, first_outs = expert_first(
                group, station[None], rows, weights, copies, downs[0], down_copies[0], sizes, members
            )
        for offset in range(2):
            for shift, part in enumerate([Y[n]] + X[n]):
                if offset:
                    part = named(f"C{n}", flipped, part if act is None else after(part, act), 1)
                if gate_up is not None:
                    base, size, column = gate_up
                    weights.append(part)
                    copies.append((distance + offset, shift, base, size, column))
                else:
                    downs[chunk].append(part)
                    down_copies[chunk].append(
                        (distance + offset, shift, part_hidden, 0, columns[chunk][1])
                    )

    partner = [(r, True) for r in mixed] + [(last, True)]
    classes = [(r, r < half) for r in range(experts)]
    layer_out = None
    for c, (base, size) in enumerate(columns):
        outs = first_outs if c == 0 else expert_later(group, act, downs[c], down_copies[c], sizes)
        back = [outs[0]] + [None] * last
        for r in mixed:
            route = {b: a for a, b in mixed[r].items()}
            back[r] = named(f"mixed_back{c}", along, outs[r], route)
        back[last] = named(f"far_back{c}", along, outs[last], far)
        for r in near:
            back[r] = named(f"near_back{c}", along, outs[r], near[r])
        held = [back[r] for r in mixed] + [outs[last]]
        hub_sum = partner_sum(partner, is_hub, hub_table, held)
        hub_sum = named(f"sum_back{c}", along, hub_sum, between)
        layer_out = result(
            classes, is_hub, table, back, hub_sum, residual, base, size, layer_out
        )
    return layer_out


def solution(mesh):
    in_specs = (
        P(("groups", "expert"), None),
        P(),
        P(),
        P(None, "expert"),
        P(None, "expert"),
        P("expert", None),
        P(("groups", "expert"), None),
    )
    out_specs = P(("groups", "expert"), None)
    return jax.shard_map(shards, mesh=mesh, in_specs=in_specs, out_specs=out_specs, check_vma=False)
```

time: 247 us -> 153 us (0.62)
  the two profiles are of different devices: /device:TPU:0 before, /device:TPU:16 now
where the time goes in v2:
time: 153 us
  waiting for transfers between devices  84.2 us (55%)
  starting transfers between devices  36.5 us (24%)
  Pallas kernels  25.5 us (17%)
  local copies, waits for them, and re-layouts  6.17 us (4%)
    ppermute x9, waiting for transfers between devices, along(): return lax.ppermute(value, 'expert', pairs)  35.8 us
    ppermute x21, waiting for transfers between devices, flipped(): return lax.ppermute(value, 'expert', pairs)  35.3 us
    ppermute x9, starting transfers between devices, along(): return lax.ppermute(value, 'expert', pairs)  13.7 us
    ppermute x6, waiting for transfers between devices, turned(): return lax.ppermute(value, 'groups', pairs)  13.1 us
    pallas_call x1, Pallas kernels, expert_first(): pl.pallas_call(functools.partial(expert_kernel, plan), out_shape=[jax.Sha...  12.9 us
    ppermute x6, starting transfers between devices, turned(): return lax.ppermute(value, 'groups', pairs)  9 us
    ppermute x21, starting transfers between devices, flipped(): return lax.ppermute(value, 'expert', pairs)  8.69 us
    all_to_all x1, starting transfers between devices, shards(): lax.all_to_all(packed, 'expert', 0, 0, axis_index_groups=lines, tiled=True)  5.2 us
  transfers between devices with their start and end apart: 37, of which 22 were waited for; matrix products, arithmetic and copies ran while one was open for 1% of the time, Pallas kernels for 15%

profile of v2, /device:TPU:16, one launch (start us, length us, event | category | flops | bytes accessed | tf_op | source)
XLA Modules:
  0.0 152.8 jit_solution(4910615525233998288)
XLA Ops:
  0.0 1.2 constant_dynamic-slice_fusion.3
  1.2 1.6 %collective-permute-start = (bf16[896,256]{1,0:T(8,128)(2,1)S(1)}, bf16[896,256]{1,0:T(8,128)(2,1)}, u32[]{:S(2)}, u32[]{:S(2)}) collective-permute-start(bf16[896,256]{1,0:T(8,128)(2,1)S(1)} %get-tuple-element.60), channel_id=1, source_target_pairs={{0,2},{1,3},{2,0},{3,1},{4,6},{5,7},{6,4},{7,5},{8,10},{9,11},{10,... | collective-permute-start | bytes 1376264 | tf_op jit(solution)/shard_map/Y0/ppermute | solution.py:20
  2.8 3.9 %shard_map.73 = (f32[132,128]{1,0:T(8,128)}, bf16[384,3584]{1,0:T(8,128)(2,1)}) custom-call(s32[1]{0:T(128)} %bitcast.1.station, bf16[128,3584]{1,0:T(8,128)(2,1)} %refs_5_.3, f32[3584]{0:T(1024)} %gain.1, bf16[4,3584]{1,0:T(4,128)(2,1)} %bitcast.8, s32[2,128]{1,0:T(2,128)} %bitcast.9), custom_call_target="tpu_custom_call" | custom-call | tf_op jit(solution)/shard_map/pallas_call | solution.py:85
  6.7 2.3 %collective-permute-start.1 = (f32[132,128]{1,0:T(8,128)}, f32[132,128]{1,0:T(8,128)S(1)}, u32[]{:S(2)}, u32[]{:S(2)}) collective-permute-start(f32[132,128]{1,0:T(8,128)} %get-tuple-element.31.table), channel_id=1, source_target_pairs={{4,8},{5,9},{6,10},{7,11},{8,4},{9,5},{10,6},{11,7},{20,24},{21,25... | collective-permute-start | bytes 202760 | tf_op jit(solution)/shard_map/table/ppermute | solution.py:336
  9.1 4.0 %collective-permute-done.1.table = f32[132,128]{1,0:T(8,128)S(1)} collective-permute-done((f32[132,128]{1,0:T(8,128)}, f32[132,128]{1,0:T(8,128)S(1)}, u32[]{:S(2)}, u32[]{:S(2)}) %collective-permute-start.1) | collective-permute-done | bytes 67616 | tf_op jit(solution)/shard_map/table/ppermute | solution.py:336
  13.7 5.2 %all-to-all-start = ((bf16[4,96,3584]{2,1,0:T(8,128)(2,1)}), bf16[4,96,3584]{2,1,0:T(8,128)(2,1)}, u32[]{:S(2)}, u32[]{:S(2)}) async-start(bf16[4,96,3584]{2,1,0:T(8,128)(2,1)} %bitcast.7), calls=%async_computation | async-start | bytes 5505024 | tf_op jit(solution)/shard_map/all_to_all | solution.py:376
  18.9 1.5 collective-permute-start.7
  20.4 1.5 collective-permute-start.4
  21.9 1.2 constant_dynamic-slice_fusion.1
  23.1 6.8 %collective-permute-done.7.refs_8_ = bf16[896,256]{1,0:T(8,128)(2,1)} collective-permute-done((bf16[896,256]{1,0:T(8,128)(2,1)S(1)}, bf16[896,256]{1,0:T(8,128)(2,1)}, u32[]{:S(2)}, u32[]{:S(2)}) %collective-permute-start.7) | collective-permute-done | bytes 458784 | tf_op jit(solution)/shard_map/Y1/ppermute | solution.py:20
  29.9 1.4 collective-permute-done.4.refs_5_
  31.2 0.6 collective-permute-start.11
  31.8 1.4 collective-permute-start.8
  33.2 8.2 %collective-permute-done.11.refs_12_ = bf16[896,256]{1,0:T(8,128)(2,1)S(1)} collective-permute-done((bf16[896,256]{1,0:T(8,128)(2,1)S(1)}, bf16[896,256]{1,0:T(8,128)(2,1)S(1)}, u32[]{:S(2)}, u32[]{:S(2)}) %collective-permute-start.11) | collective-permute-done | bytes 458784 | tf_op jit(solution)/shard_map/Y2/ppermute | solution.py:20
  41.6 1.9 %collective-permute-start.15 = (bf16[896,256]{1,0:T(8,128)(2,1)S(1)}, bf16[896,256]{1,0:T(8,128)(2,1)S(1)}, u32[]{:S(2)}, u32[]{:S(2)}) collective-permute-start(bf16[896,256]{1,0:T(8,128)(2,1)S(1)} %get-tuple-element.38), channel_id=1, source_target_pairs={{0,2},{1,3},{2,0},{3,1},{4,6},{5,7},{6,4},{7,5},{8,10},{9,11},{10,... | collective-permute-start | bytes 1376264 | tf_op jit(solution)/shard_map/Y3/ppermute | solution.py:20
  43.6 1.8 %collective-permute-start.12 = (bf16[896,256]{1,0:T(8,128)(2,1)S(1)}, bf16[896,256]{1,0:T(8,128)(2,1)S(1)}, u32[]{:S(2)}, u32[]{:S(2)}) collective-permute-start(bf16[896,256]{1,0:T(8,128)(2,1)S(1)} %collective-permute-done.11.refs_12_), channel_id=1, source_target_pairs={{0,16},{16,0},{1,17},{17,1},{2,18},{18,2},{3,19},{19,3},{4,20},{20... | collective-permute-start | bytes 1376264 | tf_op jit(solution)/shard_map/X2/ppermute | solution.py:26
  45.9 4.8 %collective-permute-done.15.refs_16_ = bf16[896,256]{1,0:T(8,128)(2,1)S(1)} collective-permute-done((bf16[896,256]{1,0:T(8,128)(2,1)S(1)}, bf16[896,256]{1,0:T(8,128)(2,1)S(1)}, u32[]{:S(2)}, u32[]{:S(2)}) %collective-permute-start.15) | collective-permute-done | bytes 458784 | tf_op jit(solution)/shard_map/Y3/ppermute | solution.py:20
  50.7 1.3 collective-permute-done.12.refs_13_
  52.1 0.8 copy-done.14
  52.9 0.7 collective-permute-start.20
  53.6 1.7 %collective-permute-start.16 = (bf16[896,256]{1,0:T(8,128)(2,1)S(1)}, bf16[896,256]{1,0:T(8,128)(2,1)S(1)}, u32[]{:S(2)}, u32[]{:S(2)}) collective-permute-start(bf16[896,256]{1,0:T(8,128)(2,1)S(1)} %collective-permute-done.15.refs_16_), channel_id=1, source_target_pairs={{0,16},{16,0},{1,17},{17,1},{2,18},{18,2},{3,19},{19,3},{4,20},{20... | collective-permute-start | bytes 1376264 | tf_op jit(solution)/shard_map/X3/ppermute | solution.py:26
  55.3 10.7 %collective-permute-done.20.refs_22_ = bf16[128,1792]{1,0:T(8,128)(2,1)S(1)} collective-permute-done((bf16[128,1792]{1,0:T(8,128)(2,1)S(1)}, bf16[128,1792]{1,0:T(8,128)(2,1)S(1)}, u32[]{:S(2)}, u32[]{:S(2)}) %collective-permute-start.20) | collective-permute-done | bytes 458784 | tf_op jit(solution)/shard_map/Y4/ppermute | solution.py:20
  66.5 1.2 collective-permute-done.13.refs_14_
  67.8 1.8 %collective-permute-start.21 = (bf16[128,1792]{1,0:T(8,128)(2,1)S(1)}, bf16[128,1792]{1,0:T(8,128)(2,1)S(1)}, u32[]{:S(2)}, u32[]{:S(2)}) collective-permute-start(bf16[128,1792]{1,0:T(8,128)(2,1)S(1)} %collective-permute-done.20.refs_22_), channel_id=1, source_target_pairs={{0,16},{16,0},{1,17},{17,1},{2,18},{18,2},{3,19},{19,3},{4,20},{20... | collective-permute-start | bytes 1376264 | tf_op jit(solution)/shard_map/X4/ppermute | solution.py:26
  70.5 9.8 %collective-permute-done.21.refs_23_ = bf16[128,1792]{1,0:T(8,128)(2,1)S(1)} collective-permute-done((bf16[128,1792]{1,0:T(8,128)(2,1)S(1)}, bf16[128,1792]{1,0:T(8,128)(2,1)S(1)}, u32[]{:S(2)}, u32[]{:S(2)}) %collective-permute-start.21) | collective-permute-done | bytes 458784 | tf_op jit(solution)/shard_map/X4/ppermute | solution.py:26
  80.3 1.5 collective-permute-done.24.refs_2_
  81.9 0.9 collective-permute-start.25
  82.9 0.9 copy-done.24
  83.9 12.9 %shard_map.74 = (bf16[384,1024]{1,0:T(8,128)(2,1)}, bf16[96,1792]{1,0:T(8,128)(2,1)}, bf16[96,1792]{1,0:T(8,128)(2,1)}, bf16[96,1792]{1,0:T(8,128)(2,1)}, bf16[96,1792]{1,0:T(8,128)(2,1)}) custom-call(s32[1]{0:T(128)} %bitcast.4.group, s32[1]{0:T(128)} %bitcast.1.station, bf16[384,3584]{1,0:T(8,128)(2,1)} %bitcast.6.rows, bf16[3584,256]{1,0:T(8,128)(2,1)} %refs_0_.2, ...), custom_call_target="tpu_custom_call" | custom-call | tf_op jit(solution)/shard_map/pallas_call | solution.py:178
  97.8 0.9 collective-permute-done.27.refs_5_
  98.7 0.7 collective-permute-done.26.refs_4_
  99.4 1.1 copy-done.3
  100.5 3.7 %shard_map.75 = (bf16[96,1792]{1,0:T(8,128)(2,1)S(1)}, bf16[96,1792]{1,0:T(8,128)(2,1)S(1)}, bf16[96,1792]{1,0:T(8,128)(2,1)}, bf16[96,1792]{1,0:T(8,128)(2,1)S(1)}) custom-call(s32[1]{0:T(128)} %bitcast.4.group, bf16[384,1024]{1,0:T(8,128)(2,1)S(1)} %copy-done.3, bf16[256,3584]{1,0:T(8,128)(2,1)S(1)} %copy-done.1, ...), custom_call_target="tpu_custom_call" | custom-call | tf_op jit(solution)/shard_map/pallas_call | solution.py:214
  104.2 0.7 copy-done.7
  105.3 1.6 %collective-permute-start.32 = (bf16[96,1792]{1,0:T(8,128)(2,1)}, bf16[96,1792]{1,0:T(8,128)(2,1)S(1)}, u32[]{:S(2)}, u32[]{:S(2)}) collective-permute-start(bf16[96,1792]{1,0:T(8,128)(2,1)} %get-tuple-element.52), channel_id=1, source_target_pairs={{0,4},{1,5},{2,6},{3,7},{4,0},{5,1},{6,2},{7,3},{8,12},{9,13},{10,... | collective-permute-start | bytes 1032200 | tf_op jit(solution)/shard_map/near_back0/ppermute | solution.py:336
  107.0 0.8 collective-permute-done.33.refs_0_.refs_2_
  108.3 2.8 %collective-permute-start.35 = (bf16[128,1792]{1,0:T(8,128)(2,1)S(1)}, bf16[128,1792]{1,0:T(8,128)(2,1)S(1)}, u32[]{:S(2)}, u32[]{:S(2)}) collective-permute-start(bf16[128,1792]{1,0:T(8,128)(2,1)S(1)} %shard_map.77), channel_id=1, source_target_pairs={{4,8},{5,9},{6,10},{7,11},{8,4},{9,5},{10,6},{11,7},{20,24},{21,25... | collective-permute-start | bytes 1376264 | tf_op jit(solution)/shard_map/sum_back0/ppermute | solution.py:336
  111.1 5.0 %collective-permute-done.29.refs_0_.refs_2_ = bf16[96,1792]{1,0:T(8,128)(2,1)S(1)} collective-permute-done((bf16[96,1792]{1,0:T(8,128)(2,1)}, bf16[96,1792]{1,0:T(8,128)(2,1)S(1)}, u32[]{:S(2)}, u32[]{:S(2)}) %collective-permute-start.29) | collective-permute-done | bytes 344096 | tf_op jit(solution)/shard_map/mixed_back1/ppermute | solution.py:336
  116.6 3.0 %collective-permute-start.31 = (bf16[128,1792]{1,0:T(8,128)(2,1)S(1)}, bf16[128,1792]{1,0:T(8,128)(2,1)S(1)}, u32[]{:S(2)}, u32[]{:S(2)}) collective-permute-start(bf16[128,1792]{1,0:T(8,128)(2,1)S(1)} %shard_map.76), channel_id=1, source_target_pairs={{4,8},{5,9},{6,10},{7,11},{8,4},{9,5},{10,6},{11,7},{20,24},{21,25... | collective-permute-start | bytes 1376264 | tf_op jit(solution)/shard_map/sum_back1/ppermute | solution.py:336
  119.7 0.7 collective-permute-start.34
  120.4 1.7 %collective-permute-start.28 = (bf16[96,1792]{1,0:T(8,128)(2,1)S(1)}, bf16[96,1792]{1,0:T(8,128)(2,1)S(1)}, u32[]{:S(2)}, u32[]{:S(2)}) collective-permute-start(bf16[96,1792]{1,0:T(8,128)(2,1)S(1)} %copy-done.8), channel_id=1, source_target_pairs={{0,4},{1,5},{2,6},{3,7},{4,0},{5,1},{6,2},{7,3},{8,12},{9,13},{10,... | collective-permute-start | bytes 1032200 | tf_op jit(solution)/shard_map/near_back1/ppermute | solution.py:336
  122.1 5.6 %collective-permute-done.32.refs_1_ = bf16[96,1792]{1,0:T(8,128)(2,1)S(1)} collective-permute-done((bf16[96,1792]{1,0:T(8,128)(2,1)}, bf16[96,1792]{1,0:T(8,128)(2,1)S(1)}, u32[]{:S(2)}, u32[]{:S(2)}) %collective-permute-start.32) | collective-permute-done | bytes 344096 | tf_op jit(solution)/shard_map/near_back0/ppermute | solution.py:336
  127.7 0.7 collective-permute-start.30
  128.4 5.9 %collective-permute-done.35.refs_4_ = bf16[128,1792]{1,0:T(8,128)(2,1)S(1)} collective-permute-done((bf16[128,1792]{1,0:T(8,128)(2,1)S(1)}, bf16[128,1792]{1,0:T(8,128)(2,1)S(1)}, u32[]{:S(2)}, u32[]{:S(2)}) %collective-permute-start.35) | collective-permute-done | bytes 458784 | tf_op jit(solution)/shard_map/sum_back0/ppermute | solution.py:336
  134.3 1.9 %shard_map.78.refs_6_ = bf16[128,3584]{1,0:T(8,128)(2,1)} custom-call(s32[1]{0:T(128)} %bitcast.is_hub, f32[132,128]{1,0:T(8,128)S(1)} %copy-done.6, bf16[96,1792]{1,0:T(8,128)(2,1)S(1)} %copy-done.4, bf16[96,1792]{1,0:T(8,128)(2,1)S(1)} %collective-permute-done.32.refs_1_, bf16[96,1792]{1,0:T(8,128)(2,1)S(1)} %collective-permute-done.33.refs_0_.refs_2_, ...), custom_call_target="tpu_custom_call" | custom-call | tf_op jit(solution)/shard_map/pallas_call | solution.py:291
  136.2 3.9 %collective-permute-done.28.refs_1_ = bf16[96,1792]{1,0:T(8,128)(2,1)S(1)} collective-permute-done((bf16[96,1792]{1,0:T(8,128)(2,1)S(1)}, bf16[96,1792]{1,0:T(8,128)(2,1)S(1)}, u32[]{:S(2)}, u32[]{:S(2)}) %collective-permute-start.28) | collective-permute-done | bytes 344096 | tf_op jit(solution)/shard_map/near_back1/ppermute | solution.py:336
  140.1 10.6 %collective-permute-done.31.refs_4_ = bf16[128,1792]{1,0:T(8,128)(2,1)S(1)} collective-permute-done((bf16[128,1792]{1,0:T(8,128)(2,1)S(1)}, bf16[128,1792]{1,0:T(8,128)(2,1)S(1)}, u32[]{:S(2)}, u32[]{:S(2)}) %collective-permute-start.31) | collective-permute-done | bytes 458784 | tf_op jit(solution)/shard_map/sum_back1/ppermute | solution.py:336
  150.7 1.9 %shard_map.79 = bf16[128,3584]{1,0:T(8,128)(2,1)} custom-call(s32[1]{0:T(128)} %bitcast.is_hub, f32[132,128]{1,0:T(8,128)S(1)} %copy-done.6, bf16[96,1792]{1,0:T(8,128)(2,1)S(1)} %get-tuple-element.47.refs_0_, bf16[96,1792]{1,0:T(8,128)(2,1)S(1)} %collective-permute-done.28.refs_1_, ...), custom_call_target="tpu_custom_call", output_to_operand_aliasing={{}: (8, {})} | custom-call | tf_op jit(solution)/shard_map/pallas_call | solution.py:291
  (86 shorter events, 5.7 us)
Async XLA Ops:
  1.2 12.4 %collective-permute-start = (bf16[896,256]{1,0:T(8,128)(2,1)S(1)}, bf16[896,256]{1,0:T(8,128)(2,1)}, u32[]{:S(2)}, u32[]{:S(2)}) collective-permute-start(bf16[896,256]{1,0:T(8,128)(2,1)S(1)} %get-tuple-element.60), channel_id=1, source_target_pairs={{0,2},{1,3},{2,0},{3,1},{4,6},{5,7},{6,4},{7,5},{8,10},{9,11},{10,... | collective-permute-start | bytes 1376264 | tf_op jit(solution)/shard_map/Y0/ppermute | solution.py:20
  6.7 6.4 %collective-permute-start.1 = (f32[132,128]{1,0:T(8,128)}, f32[132,128]{1,0:T(8,128)S(1)}, u32[]{:S(2)}, u32[]{:S(2)}) collective-permute-start(f32[132,128]{1,0:T(8,128)} %get-tuple-element.31.table), channel_id=1, source_target_pairs={{4,8},{5,9},{6,10},{7,11},{8,4},{9,5},{10,6},{11,7},{20,24},{21,25... | collective-permute-start | bytes 202760 | tf_op jit(solution)/shard_map/table/ppermute | solution.py:336
  13.7 70.2 %all-to-all-start = ((bf16[4,96,3584]{2,1,0:T(8,128)(2,1)}), bf16[4,96,3584]{2,1,0:T(8,128)(2,1)}, u32[]{:S(2)}, u32[]{:S(2)}) async-start(bf16[4,96,3584]{2,1,0:T(8,128)(2,1)} %bitcast.7), calls=%async_computation | async-start | bytes 5505024 | tf_op jit(solution)/shard_map/all_to_all | solution.py:376
  18.9 26.5 %copy-start = (bf16[256,3584]{1,0:T(8,128)(2,1)S(1)}, bf16[256,3584]{1,0:T(8,128)(2,1)}, u32[]{:S(2)}) copy-start(bf16[256,3584]{1,0:T(8,128)(2,1)} %refs_0_.3) | copy-start | bytes 5505028
  18.9 11.0 %collective-permute-start.7 = (bf16[896,256]{1,0:T(8,128)(2,1)S(1)}, bf16[896,256]{1,0:T(8,128)(2,1)}, u32[]{:S(2)}, u32[]{:S(2)}) collective-permute-start(bf16[896,256]{1,0:T(8,128)(2,1)S(1)} %get-tuple-element.34), channel_id=1, source_target_pairs={{0,2},{1,3},{2,0},{3,1},{4,6},{5,7},{6,4},{7,5},{8,10},{9,11},{10,... | collective-permute-start | bytes 1376264 | tf_op jit(solution)/shard_map/Y1/ppermute | solution.py:20
  20.4 10.9 %collective-permute-start.4 = (bf16[896,256]{1,0:T(8,128)(2,1)}, bf16[896,256]{1,0:T(8,128)(2,1)}, u32[]{:S(2)}, u32[]{:S(2)}) collective-permute-start(bf16[896,256]{1,0:T(8,128)(2,1)} %collective-permute-done.refs_4_), channel_id=1, source_target_pairs={{0,16},{16,0},{1,17},{17,1},{2,18},{18,2},{3,19},{19,3},{4,20},{20... | collective-permute-start | bytes 1376264 | tf_op jit(solution)/shard_map/X0/ppermute | solution.py:26
  31.2 10.2 %collective-permute-start.11 = (bf16[896,256]{1,0:T(8,128)(2,1)S(1)}, bf16[896,256]{1,0:T(8,128)(2,1)S(1)}, u32[]{:S(2)}, u32[]{:S(2)}) collective-permute-start(bf16[896,256]{1,0:T(8,128)(2,1)S(1)} %get-tuple-element.36), channel_id=1, source_target_pairs={{0,2},{1,3},{2,0},{3,1},{4,6},{5,7},{6,4},{7,5},{8,10},{9,11},{10,... | collective-permute-start | bytes 1376264 | tf_op jit(solution)/shard_map/Y2/ppermute | solution.py:20
  31.8 9.8 %collective-permute-start.8 = (bf16[896,256]{1,0:T(8,128)(2,1)}, bf16[896,256]{1,0:T(8,128)(2,1)S(1)}, u32[]{:S(2)}, u32[]{:S(2)}) collective-permute-start(bf16[896,256]{1,0:T(8,128)(2,1)} %collective-permute-done.7.refs_8_), channel_id=1, source_target_pairs={{0,16},{16,0},{1,17},{17,1},{2,18},{18,2},{3,19},{19,3},{4,20},{20... | collective-permute-start | bytes 1376264 | tf_op jit(solution)/shard_map/X1/ppermute | solution.py:26
  33.2 12.6 %collective-permute-start.5 = (bf16[896,256]{1,0:T(8,128)(2,1)}, bf16[896,256]{1,0:T(8,128)(2,1)S(1)}, u32[]{:S(2)}, u32[]{:S(2)}) collective-permute-start(bf16[896,256]{1,0:T(8,128)(2,1)} %collective-permute-done.refs_4_), channel_id=1, source_target_pairs={{0,1},{1,0},{2,3},{3,2},{4,5},{5,4},{6,7},{7,6},{8,9},{9,8},{10,11... | collective-permute-start | bytes 1376264 | tf_op jit(solution)/shard_map/C0/ppermute | solution.py:20
  41.4 28.1 %copy-start.9 = (bf16[896,256]{1,0:T(8,128)(2,1)}, bf16[896,256]{1,0:T(8,128)(2,1)S(1)}, u32[]{:S(2)}) copy-start(bf16[896,256]{1,0:T(8,128)(2,1)S(1)} %collective-permute-done.11.refs_12_) | copy-start | bytes 1376260
  41.6 9.1 %collective-permute-start.15 = (bf16[896,256]{1,0:T(8,128)(2,1)S(1)}, bf16[896,256]{1,0:T(8,128)(2,1)S(1)}, u32[]{:S(2)}, u32[]{:S(2)}) collective-permute-start(bf16[896,256]{1,0:T(8,128)(2,1)S(1)} %get-tuple-element.38), channel_id=1, source_target_pairs={{0,2},{1,3},{2,0},{3,1},{4,6},{5,7},{6,4},{7,5},{8,10},{9,11},{10,... | collective-permute-start | bytes 1376264 | tf_op jit(solution)/shard_map/Y3/ppermute | solution.py:20
  43.6 8.5 %collective-permute-start.12 = (bf16[896,256]{1,0:T(8,128)(2,1)S(1)}, bf16[896,256]{1,0:T(8,128)(2,1)S(1)}, u32[]{:S(2)}, u32[]{:S(2)}) collective-permute-start(bf16[896,256]{1,0:T(8,128)(2,1)S(1)} %collective-permute-done.11.refs_12_), channel_id=1, source_target_pairs={{0,16},{16,0},{1,17},{17,1},{2,18},{18,2},{3,19},{19,3},{4,20},{20... | collective-permute-start | bytes 1376264 | tf_op jit(solution)/shard_map/X2/ppermute | solution.py:26
  45.3 24.6 %collective-permute-start.19 = (bf16[256,3584]{1,0:T(8,128)(2,1)S(1)}, bf16[256,3584]{1,0:T(8,128)(2,1)}, u32[]{:S(2)}, u32[]{:S(2)}) collective-permute-start(bf16[256,3584]{1,0:T(8,128)(2,1)S(1)} %copy-done), channel_id=1, source_target_pairs={{0,1},{1,0},{2,3},{3,2},{4,5},{5,4},{6,7},{7,6},{8,9},{9,8},{10,11... | collective-permute-start | bytes 5505032 | tf_op jit(solution)/shard_map/own/ppermute | solution.py:20
  45.3 24.6 %collective-permute-start.2 = (bf16[3584,256]{1,0:T(8,128)(2,1)}, bf16[3584,256]{1,0:T(8,128)(2,1)}, u32[]{:S(2)}, u32[]{:S(2)}) collective-permute-start(bf16[3584,256]{1,0:T(8,128)(2,1)} %refs_0_.2), channel_id=1, source_target_pairs={{0,1},{1,0},{2,3},{3,2},{4,5},{5,4},{6,7},{7,6},{8,9},{9,8},{10,11... | collective-permute-start | bytes 5505032 | tf_op jit(solution)/shard_map/own/ppermute | solution.py:20
  45.8 7.1 %collective-permute-start.9 = (bf16[896,256]{1,0:T(8,128)(2,1)}, bf16[896,256]{1,0:T(8,128)(2,1)}, u32[]{:S(2)}, u32[]{:S(2)}) collective-permute-start(bf16[896,256]{1,0:T(8,128)(2,1)} %collective-permute-done.7.refs_8_), channel_id=1, source_target_pairs={{0,1},{1,0},{2,3},{3,2},{4,5},{5,4},{6,7},{7,6},{8,9},{9,8},{10,11... | collective-permute-start | bytes 1376264 | tf_op jit(solution)/shard_map/C1/ppermute | solution.py:20
  50.7 33.1 %copy-start.13 = (bf16[896,256]{1,0:T(8,128)(2,1)}, bf16[896,256]{1,0:T(8,128)(2,1)S(1)}, u32[]{:S(2)}) copy-start(bf16[896,256]{1,0:T(8,128)(2,1)S(1)} %collective-permute-done.15.refs_16_) | copy-start | bytes 1376260
  50.7 2.9 %collective-permute-start.6 = (bf16[896,256]{1,0:T(8,128)(2,1)}, bf16[896,256]{1,0:T(8,128)(2,1)}, u32[]{:S(2)}, u32[]{:S(2)}) collective-permute-start(bf16[896,256]{1,0:T(8,128)(2,1)} %collective-permute-done.4.refs_5_), channel_id=1, source_target_pairs={{0,1},{1,0},{2,3},{3,2},{4,5},{5,4},{6,7},{7,6},{8,9},{9,8},{10,11... | collective-permute-start | bytes 1376264 | tf_op jit(solution)/shard_map/C0/ppermute | solution.py:20
  52.9 17.6 %collective-permute-start.3 = (bf16[3584,256]{1,0:T(8,128)(2,1)}, bf16[3584,256]{1,0:T(8,128)(2,1)}, u32[]{:S(2)}, u32[]{:S(2)}) collective-permute-start(bf16[3584,256]{1,0:T(8,128)(2,1)} %refs_1_.1), channel_id=1, source_target_pairs={{0,1},{1,0},{2,3},{3,2},{4,5},{5,4},{6,7},{7,6},{8,9},{9,8},{10,11... | collective-permute-start | bytes 5505032 | tf_op jit(solution)/shard_map/own/ppermute | solution.py:20
  52.9 17.1 %copy-start.15 = (bf16[896,256]{1,0:T(8,128)(2,1)S(1)}, bf16[896,256]{1,0:T(8,128)(2,1)}, u32[]{:S(2)}) copy-start(bf16[896,256]{1,0:T(8,128)(2,1)} %copy-done.14) | copy-start | bytes 1376260
  52.9 13.0 %collective-permute-start.20 = (bf16[128,1792]{1,0:T(8,128)(2,1)S(1)}, bf16[128,1792]{1,0:T(8,128)(2,1)S(1)}, u32[]{:S(2)}, u32[]{:S(2)}) collective-permute-start(bf16[128,1792]{1,0:T(8,128)(2,1)S(1)} %get-tuple-element.40), channel_id=1, source_target_pairs={{0,2},{1,3},{2,0},{3,1},{4,6},{5,7},{6,4},{7,5},{8,10},{9,11},{10,... | collective-permute-start | bytes 1376264 | tf_op jit(solution)/shard_map/Y4/ppermute | solution.py:20
  53.6 12.7 %collective-permute-start.16 = (bf16[896,256]{1,0:T(8,128)(2,1)S(1)}, bf16[896,256]{1,0:T(8,128)(2,1)S(1)}, u32[]{:S(2)}, u32[]{:S(2)}) collective-permute-start(bf16[896,256]{1,0:T(8,128)(2,1)S(1)} %collective-permute-done.15.refs_16_), channel_id=1, source_target_pairs={{0,16},{16,0},{1,17},{17,1},{2,18},{18,2},{3,19},{19,3},{4,20},{20... | collective-permute-start | bytes 1376264 | tf_op jit(solution)/shard_map/X3/ppermute | solution.py:26
  65.9 16.9 %copy-start.16 = (bf16[128,1792]{1,0:T(8,128)(2,1)}, bf16[128,1792]{1,0:T(8,128)(2,1)S(1)}, u32[]{:S(2)}) copy-start(bf16[128,1792]{1,0:T(8,128)(2,1)S(1)} %collective-permute-done.20.refs_22_) | copy-start | bytes 1376260
  65.9 1.8 %collective-permute-start.13 = (bf16[896,256]{1,0:T(8,128)(2,1)S(1)}, bf16[896,256]{1,0:T(8,128)(2,1)S(1)}, u32[]{:S(2)}, u32[]{:S(2)}) collective-permute-start(bf16[896,256]{1,0:T(8,128)(2,1)S(1)} %collective-permute-done.11.refs_12_), channel_id=1, source_target_pairs={{0,1},{1,0},{2,3},{3,2},{4,5},{5,4},{6,7},{7,6},{8,9},{9,8},{10,11... | collective-permute-start | bytes 1376264 | tf_op jit(solution)/shard_map/C2/ppermute | solution.py:20
  66.3 16.6 %copy-start.17 = (bf16[896,256]{1,0:T(8,128)(2,1)}, bf16[896,256]{1,0:T(8,128)(2,1)S(1)}, u32[]{:S(2)}) copy-start(bf16[896,256]{1,0:T(8,128)(2,1)S(1)} %collective-permute-done.16.refs_17_) | copy-start | bytes 1376260
  66.3 3.2 %collective-permute-start.10 = (bf16[896,256]{1,0:T(8,128)(2,1)S(1)}, bf16[896,256]{1,0:T(8,128)(2,1)S(1)}, u32[]{:S(2)}, u32[]{:S(2)}) collective-permute-start(bf16[896,256]{1,0:T(8,128)(2,1)S(1)} %copy-done.11), channel_id=1, source_target_pairs={{0,1},{1,0},{2,3},{3,2},{4,5},{5,4},{6,7},{7,6},{8,9},{9,8},{10,11... | collective-permute-start | bytes 1376264 | tf_op jit(solution)/shard_map/C1/ppermute | solution.py:20
  67.7 15.1 %copy-start.18 = (bf16[896,256]{1,0:T(8,128)(2,1)}, bf16[896,256]{1,0:T(8,128)(2,1)S(1)}, u32[]{:S(2)}) copy-start(bf16[896,256]{1,0:T(8,128)(2,1)S(1)} %collective-permute-done.13.refs_14_) | copy-start | bytes 1376260
  67.8 12.6 %collective-permute-start.21 = (bf16[128,1792]{1,0:T(8,128)(2,1)S(1)}, bf16[128,1792]{1,0:T(8,128)(2,1)S(1)}, u32[]{:S(2)}, u32[]{:S(2)}) collective-permute-start(bf16[128,1792]{1,0:T(8,128)(2,1)S(1)} %collective-permute-done.20.refs_22_), channel_id=1, source_target_pairs={{0,16},{16,0},{1,17},{17,1},{2,18},{18,2},{3,19},{19,3},{4,20},{20... | collective-permute-start | bytes 1376264 | tf_op jit(solution)/shard_map/X4/ppermute | solution.py:26
  69.5 12.3 %collective-permute-start.24 = (bf16[128,1792]{1,0:T(8,128)(2,1)S(1)}, bf16[128,1792]{1,0:T(8,128)(2,1)S(1)}, u32[]{:S(2)}, u32[]{:S(2)}) collective-permute-start(bf16[128,1792]{1,0:T(8,128)(2,1)S(1)} %get-tuple-element.43), channel_id=1, source_target_pairs={{0,2},{1,3},{2,0},{3,1},{4,6},{5,7},{6,4},{7,5},{8,10},{9,11},{10,... | collective-permute-start | bytes 1376264 | tf_op jit(solution)/shard_map/Y5/ppermute | solution.py:20
  69.9 11.9 %collective-permute-start.17 = (bf16[896,256]{1,0:T(8,128)(2,1)S(1)}, bf16[896,256]{1,0:T(8,128)(2,1)S(1)}, u32[]{:S(2)}, u32[]{:S(2)}) collective-permute-start(bf16[896,256]{1,0:T(8,128)(2,1)S(1)} %collective-permute-done.15.refs_16_), channel_id=1, source_target_pairs={{0,1},{1,0},{2,3},{3,2},{4,5},{5,4},{6,7},{7,6},{8,9},{9,8},{10,11... | collective-permute-start | bytes 1376264 | tf_op jit(solution)/shard_map/C3/ppermute | solution.py:20
  69.9 12.9 %collective-permute-start.14 = (bf16[896,256]{1,0:T(8,128)(2,1)S(1)}, bf16[896,256]{1,0:T(8,128)(2,1)S(1)}, u32[]{:S(2)}, u32[]{:S(2)}) collective-permute-start(bf16[896,256]{1,0:T(8,128)(2,1)S(1)} %copy-done.15), channel_id=1, source_target_pairs={{0,1},{1,0},{2,3},{3,2},{4,5},{5,4},{6,7},{7,6},{8,9},{9,8},{10,11... | collective-permute-start | bytes 1376264 | tf_op jit(solution)/shard_map/C2/ppermute | solution.py:20
  70.4 12.4 %collective-permute-start.22 = (bf16[128,1792]{1,0:T(8,128)(2,1)S(1)}, bf16[128,1792]{1,0:T(8,128)(2,1)S(1)}, u32[]{:S(2)}, u32[]{:S(2)}) collective-permute-start(bf16[128,1792]{1,0:T(8,128)(2,1)S(1)} %collective-permute-done.20.refs_22_), channel_id=1, source_target_pairs={{0,1},{1,0},{2,3},{3,2},{4,5},{5,4},{6,7},{7,6},{8,9},{9,8},{10,11... | collective-permute-start | bytes 1376264 | tf_op jit(solution)/shard_map/C4/ppermute | solution.py:20
  80.3 2.5 %collective-permute-start.18 = (bf16[896,256]{1,0:T(8,128)(2,1)S(1)}, bf16[896,256]{1,0:T(8,128)(2,1)S(1)}, u32[]{:S(2)}, u32[]{:S(2)}) collective-permute-start(bf16[896,256]{1,0:T(8,128)(2,1)S(1)} %collective-permute-done.16.refs_17_), channel_id=1, source_target_pairs={{0,1},{1,0},{2,3},{3,2},{4,5},{5,4},{6,7},{7,6},{8,9},{9,8},{10,11... | collective-permute-start | bytes 1376264 | tf_op jit(solution)/shard_map/C3/ppermute | solution.py:20
  81.9 1.9 %collective-permute-start.23 = (bf16[128,1792]{1,0:T(8,128)(2,1)S(1)}, bf16[128,1792]{1,0:T(8,128)(2,1)}, u32[]{:S(2)}, u32[]{:S(2)}) collective-permute-start(bf16[128,1792]{1,0:T(8,128)(2,1)S(1)} %collective-permute-done.21.refs_23_), channel_id=1, source_target_pairs={{0,1},{1,0},{2,3},{3,2},{4,5},{5,4},{6,7},{7,6},{8,9},{9,8},{10,11... | collective-permute-start | bytes 1376264 | tf_op jit(solution)/shard_map/C4/ppermute | solution.py:20
  81.9 15.0 %collective-permute-start.25 = (bf16[128,1792]{1,0:T(8,128)(2,1)S(1)}, bf16[128,1792]{1,0:T(8,128)(2,1)S(1)}, u32[]{:S(2)}, u32[]{:S(2)}) collective-permute-start(bf16[128,1792]{1,0:T(8,128)(2,1)S(1)} %collective-permute-done.24.refs_2_), channel_id=1, source_target_pairs={{0,16},{16,0},{1,17},{17,1},{2,18},{18,2},{3,19},{19,3},{4,20},{20... | collective-permute-start | bytes 1376264 | tf_op jit(solution)/shard_map/X5/ppermute | solution.py:26
  83.9 15.5 %copy-start.1 = (bf16[256,3584]{1,0:T(8,128)(2,1)S(1)}, bf16[256,3584]{1,0:T(8,128)(2,1)}, u32[]{:S(2)}) copy-start(bf16[256,3584]{1,0:T(8,128)(2,1)} %refs_0_.3) | copy-start | bytes 5505028
  96.9 1.9 %collective-permute-start.27 = (bf16[128,1792]{1,0:T(8,128)(2,1)S(1)}, bf16[128,1792]{1,0:T(8,128)(2,1)S(1)}, u32[]{:S(2)}, u32[]{:S(2)}) collective-permute-start(bf16[128,1792]{1,0:T(8,128)(2,1)S(1)} %collective-permute-done.25.refs_3_), channel_id=1, source_target_pairs={{0,1},{1,0},{2,3},{3,2},{4,5},{5,4},{6,7},{7,6},{8,9},{9,8},{10,11... | collective-permute-start | bytes 1376264 | tf_op jit(solution)/shard_map/C5/ppermute | solution.py:20
  97.1 2.3 %collective-permute-start.26 = (bf16[128,1792]{1,0:T(8,128)(2,1)S(1)}, bf16[128,1792]{1,0:T(8,128)(2,1)S(1)}, u32[]{:S(2)}, u32[]{:S(2)}) collective-permute-start(bf16[128,1792]{1,0:T(8,128)(2,1)S(1)} %collective-permute-done.24.refs_2_), channel_id=1, source_target_pairs={{0,1},{1,0},{2,3},{3,2},{4,5},{5,4},{6,7},{7,6},{8,9},{9,8},{10,11... | collective-permute-start | bytes 1376264 | tf_op jit(solution)/shard_map/C5/ppermute | solution.py:20
  97.4 10.3 %collective-permute-start.33 = (bf16[96,1792]{1,0:T(8,128)(2,1)}, bf16[96,1792]{1,0:T(8,128)(2,1)S(1)}, u32[]{:S(2)}, u32[]{:S(2)}) collective-permute-start(bf16[96,1792]{1,0:T(8,128)(2,1)} %get-tuple-element.53), channel_id=1, source_target_pairs={{8,0},{9,1},{10,2},{11,3},{0,4},{1,5},{2,6},{3,7},{12,8},{13,9},{1... | collective-permute-start | bytes 1032200 | tf_op jit(solution)/shard_map/mixed_back0/ppermute | solution.py:336
  104.9 29.4 %copy-start.2 = (bf16[128,3584]{1,0:T(8,128)(2,1)S(1)}, bf16[128,3584]{1,0:T(8,128)(2,1)}, u32[]{:S(2)}) copy-start(bf16[128,3584]{1,0:T(8,128)(2,1)} %refs_5_.3) | copy-start | bytes 2752516
  104.9 29.4 %copy-start.4 = (bf16[96,1792]{1,0:T(8,128)(2,1)S(1)}, bf16[96,1792]{1,0:T(8,128)(2,1)}, u32[]{:S(2)}) copy-start(bf16[96,1792]{1,0:T(8,128)(2,1)} %get-tuple-element.51.refs_0_) | copy-start | bytes 1032196
  104.9 29.4 %copy-start.6 = (f32[132,128]{1,0:T(8,128)S(1)}, f32[132,128]{1,0:T(8,128)}, u32[]{:S(2)}) copy-start(f32[132,128]{1,0:T(8,128)} %get-tuple-element.31.table) | copy-start | bytes 202756
  104.9 11.1 %collective-permute-start.29 = (bf16[96,1792]{1,0:T(8,128)(2,1)}, bf16[96,1792]{1,0:T(8,128)(2,1)S(1)}, u32[]{:S(2)}, u32[]{:S(2)}) collective-permute-start(bf16[96,1792]{1,0:T(8,128)(2,1)} %get-tuple-element.49), channel_id=1, source_target_pairs={{8,0},{9,1},{10,2},{11,3},{0,4},{1,5},{2,6},{3,7},{12,8},{13,9},{1... | collective-permute-start | bytes 1032200 | tf_op jit(solution)/shard_map/mixed_back1/ppermute | solution.py:336
  105.3 22.4 %collective-permute-start.32 = (bf16[96,1792]{1,0:T(8,128)(2,1)}, bf16[96,1792]{1,0:T(8,128)(2,1)S(1)}, u32[]{:S(2)}, u32[]{:S(2)}) collective-permute-start(bf16[96,1792]{1,0:T(8,128)(2,1)} %get-tuple-element.52), channel_id=1, source_target_pairs={{0,4},{1,5},{2,6},{3,7},{4,0},{5,1},{6,2},{7,3},{8,12},{9,13},{10,... | collective-permute-start | bytes 1032200 | tf_op jit(solution)/shard_map/near_back0/ppermute | solution.py:336
  108.3 26.0 %collective-permute-start.35 = (bf16[128,1792]{1,0:T(8,128)(2,1)S(1)}, bf16[128,1792]{1,0:T(8,128)(2,1)S(1)}, u32[]{:S(2)}, u32[]{:S(2)}) collective-permute-start(bf16[128,1792]{1,0:T(8,128)(2,1)S(1)} %shard_map.77), channel_id=1, source_target_pairs={{4,8},{5,9},{6,10},{7,11},{8,4},{9,5},{10,6},{11,7},{20,24},{21,25... | collective-permute-start | bytes 1376264 | tf_op jit(solution)/shard_map/sum_back0/ppermute | solution.py:336
  116.6 34.1 %collective-permute-start.31 = (bf16[128,1792]{1,0:T(8,128)(2,1)S(1)}, bf16[128,1792]{1,0:T(8,128)(2,1)S(1)}, u32[]{:S(2)}, u32[]{:S(2)}) collective-permute-start(bf16[128,1792]{1,0:T(8,128)(2,1)S(1)} %shard_map.76), channel_id=1, source_target_pairs={{4,8},{5,9},{6,10},{7,11},{8,4},{9,5},{10,6},{11,7},{20,24},{21,25... | collective-permute-start | bytes 1376264 | tf_op jit(solution)/shard_map/sum_back1/ppermute | solution.py:336
  119.7 8.7 %collective-permute-start.34 = (bf16[96,1792]{1,0:T(8,128)(2,1)S(1)}, bf16[96,1792]{1,0:T(8,128)(2,1)S(1)}, u32[]{:S(2)}, u32[]{:S(2)}) collective-permute-start(bf16[96,1792]{1,0:T(8,128)(2,1)S(1)} %copy-done.5), channel_id=1, source_target_pairs={{0,12},{1,13},{2,14},{3,15},{12,0},{13,1},{14,2},{15,3},{16,28},{1... | collective-permute-start | bytes 1032200 | tf_op jit(solution)/shard_map/far_back0/ppermute | solution.py:336
  120.4 19.8 %collective-permute-start.28 = (bf16[96,1792]{1,0:T(8,128)(2,1)S(1)}, bf16[96,1792]{1,0:T(8,128)(2,1)S(1)}, u32[]{:S(2)}, u32[]{:S(2)}) collective-permute-start(bf16[96,1792]{1,0:T(8,128)(2,1)S(1)} %copy-done.8), channel_id=1, source_target_pairs={{0,4},{1,5},{2,6},{3,7},{4,0},{5,1},{6,2},{7,3},{8,12},{9,13},{10,... | collective-permute-start | bytes 1032200 | tf_op jit(solution)/shard_map/near_back1/ppermute | solution.py:336
  127.7 12.4 %collective-permute-start.30 = (bf16[96,1792]{1,0:T(8,128)(2,1)S(1)}, bf16[96,1792]{1,0:T(8,128)(2,1)S(1)}, u32[]{:S(2)}, u32[]{:S(2)}) collective-permute-start(bf16[96,1792]{1,0:T(8,128)(2,1)S(1)} %get-tuple-element.50.refs_1_), channel_id=1, source_target_pairs={{0,12},{1,13},{2,14},{3,15},{12,0},{13,1},{14,2},{15,3},{16,28},{1... | collective-permute-start | bytes 1032200 | tf_op jit(solution)/shard_map/far_back1/ppermute | solution.py:336
  (14 other events, 74.1 us)

commit v3 on v2

--- a/solution.py
+++ b/solution.py
@@ -74,8 +74,7 @@
     for e in range(experts):
         filled = jnp.where(lanes == e, slot[:, e : e + 1], filled)
         filled = jnp.where(lanes == experts + e, route_scale * chosen[e] / total, filled)
-    table[pl.ds(0, rows), :] = filled
-    table[pl.ds(rows, experts), :] = slot_t
+    table[...] = filled
 
 
 def prepare(residual, norm_gain, router, expert_ids, station, block_rows):
@@ -85,7 +84,7 @@
     return pl.pallas_call(
         functools.partial(prepare_kernel, block_rows),
         out_shape=[
-            jax.ShapeDtypeStruct((rows + experts, rows), jnp.float32),
+            jax.ShapeDtypeStruct((rows, 128), jnp.float32),
             jax.ShapeDtypeStruct((experts * block_rows, width), jnp.bfloat16),
         ],
         in_specs=[pl.BlockSpec(memory_space=pltpu.SMEM)] + [whole] * 4,
@@ -225,54 +224,59 @@
     )(group, act, *downs)
 
 
-def weighted_sum(classes, is_hub, table, blocks, high, low):
+def lanes_for(count):
+    return -(-count // 128) * 128
+
+
+def weighted_sum(plan, is_hub, table, blocks, high, low):
+    classes, experts = plan
     block_rows = blocks[0].shape[0]
-    rows = table.shape[1]
-    experts = table.shape[0] - rows
+    rows = table.shape[0]
+    used = pl.ds(0, block_rows * len(blocks))
     place = lax.broadcasted_iota(jnp.int32, (rows, block_rows), 1).astype(jnp.float32)
     for i, (e, at_hub) in enumerate(classes):
-        gate = table[pl.ds(0, rows), experts + e : experts + e + 1]
+        gate = table[:, experts + e : experts + e + 1]
         if not at_hub:
             gate = jnp.where(is_hub[0] == 1, 0.0, gate)
-        weight = jnp.where(place == table[pl.ds(0, rows), e : e + 1], gate, 0.0)
+        weight = jnp.where(place == table[:, e : e + 1], gate, 0.0)
         upper = weight.astype(jnp.bfloat16)
         columns = pl.ds(i * block_rows, block_rows)
         high[:, columns] = upper
         low[:, columns] = (weight - upper.astype(jnp.float32)).astype(jnp.bfloat16)
     stacked = jnp.concatenate([block[...] for block in blocks], axis=0)
-    total = jnp.dot(high[...], stacked, preferred_element_type=jnp.float32)
-    return total + jnp.dot(low[...], stacked, preferred_element_type=jnp.float32)
-
-
-def partner_kernel(classes, is_hub, table, *refs):
+    total = jnp.dot(high[:, used], stacked, preferred_element_type=jnp.float32)
+    return total + jnp.dot(low[:, used], stacked, preferred_element_type=jnp.float32)
+
+
+def partner_kernel(plan, is_hub, table, *refs):
     blocks, (out, high, low) = refs[:-3], refs[-3:]
-    out[...] = weighted_sum(classes, is_hub, table, blocks, high, low).astype(jnp.bfloat16)
-
-
-def partner_sum(classes, is_hub, table, blocks):
+    out[...] = weighted_sum(plan, is_hub, table, blocks, high, low).astype(jnp.bfloat16)
+
+
+def partner_sum(plan, is_hub, table, blocks):
     block_rows, width = blocks[0].shape
-    rows = table.shape[1]
+    rows = table.shape[0]
     whole = pl.BlockSpec(memory_space=pltpu.VMEM)
     return pl.pallas_call(
-        functools.partial(partner_kernel, classes),
+        functools.partial(partner_kernel, plan),
         out_shape=jax.ShapeDtypeStruct((rows, width), jnp.bfloat16),
         in_specs=[pl.BlockSpec(memory_space=pltpu.SMEM)] + [whole] * (1 + len(blocks)),
         out_specs=whole,
-        scratch_shapes=[pltpu.VMEM((rows, block_rows * len(blocks)), jnp.bfloat16)] * 2,
+        scratch_shapes=[pltpu.VMEM((rows, lanes_for(block_rows * len(blocks))), jnp.bfloat16)] * 2,
         compiler_params=pltpu.CompilerParams(vmem_limit_bytes=late_vmem_bytes),
     )(is_hub, table, *blocks)
 
 
 def result_kernel(plan, is_hub, table, *refs):
-    classes, base, size, first = plan
-    count = len(classes)
+    sum_plan, base, size = plan
+    count = len(sum_plan[0])
     blocks = refs[:count]
     hub_sum, residual = refs[count : count + 2]
     out, high, low, held, result, sems = refs[-6:]
     span = pl.ds(base, size)
     fetch = pltpu.make_async_copy(residual.at[:, span], held, sems.at[0])
     fetch.start()
-    total = weighted_sum(classes, is_hub, table, blocks, high, low)
+    total = weighted_sum(sum_plan, is_hub, table, blocks, high, low)
     fetch.wait()
     total += held[...].astype(jnp.float32) + hub_sum[...].astype(jnp.float32)
     result[...] = total.astype(jnp.bfloat16)
@@ -281,7 +285,7 @@
     store.wait()
 
 
-def result(classes, is_hub, table, blocks, hub_sum, residual, base, size, so_far):
+def result(plan, is_hub, table, blocks, hub_sum, residual, base, size, so_far):
     block_rows = blocks[0].shape[0]
     rows, width = residual.shape
     whole = pl.BlockSpec(memory_space=pltpu.VMEM)
@@ -289,13 +293,13 @@
     first = so_far is None
     earlier = [] if first else [so_far]
     return pl.pallas_call(
-        functools.partial(result_kernel, (classes, base, size, first)),
+        functools.partial(result_kernel, (plan, base, size)),
         out_shape=jax.ShapeDtypeStruct((rows, width), jnp.bfloat16),
         in_specs=[pl.BlockSpec(memory_space=pltpu.SMEM)]
         + [whole] * (2 + len(blocks))
         + [anywhere] * (1 + len(earlier)),
         out_specs=anywhere,
-        scratch_shapes=[pltpu.VMEM((rows, block_rows * len(blocks)), jnp.bfloat16)] * 2
+        scratch_shapes=[pltpu.VMEM((rows, lanes_for(block_rows * len(blocks))), jnp.bfloat16)] * 2
         + [pltpu.VMEM((rows, size), jnp.bfloat16)] * 2
         + [pltpu.SemaphoreType.DMA((2,))],
         input_output_aliases={} if first else {len(blocks) + 4: 0},
@@ -411,10 +415,10 @@
         for r in near:
             back[r] = named(f"near_back{c}", along, outs[r], near[r])
         held = [back[r] for r in mixed] + [outs[last]]
-        hub_sum = partner_sum(partner, is_hub, hub_table, held)
+        hub_sum = partner_sum((partner, experts), is_hub, hub_table, held)
         hub_sum = named(f"sum_back{c}", along, hub_sum, between)
         layer_out = result(
-            classes, is_hub, table, back, hub_sum, residual, base, size, layer_out
+            (classes, experts), is_hub, table, back, hub_sum, residual, base, size, layer_out
         )
     return layer_out
 

time: 153 us -> 153 us (level)
  no operation moved by 1% of the time
where the time goes in v3:
time: 153 us
  waiting for transfers between devices  84.2 us (55%)
  starting transfers between devices  36.5 us (24%)
  Pallas kernels  25.5 us (17%)
  local copies, waits for them, and re-layouts  6.17 us (4%)
    ppermute x9, waiting for transfers between devices, along(): return lax.ppermute(value, 'expert', pairs)  35.7 us
    ppermute x21, waiting for transfers between devices, flipped(): return lax.ppermute(value, 'expert', pairs)  35.4 us
    ppermute x9, starting transfers between devices, along(): return lax.ppermute(value, 'expert', pairs)  13.7 us
    ppermute x6, waiting for transfers between devices, turned(): return lax.ppermute(value, 'groups', pairs)  13.1 us
    pallas_call x1, Pallas kernels, expert_first(): pl.pallas_call(functools.partial(expert_kernel, plan), out_shape=[jax.Sha...  12.9 us
    ppermute x6, starting transfers between devices, turned(): return lax.ppermute(value, 'groups', pairs)  9 us
    ppermute x21, starting transfers between devices, flipped(): return lax.ppermute(value, 'expert', pairs)  8.69 us
    all_to_all x1, starting transfers between devices, shards(): lax.all_to_all(packed, 'expert', 0, 0, axis_index_groups=lines, tiled=True)  5.2 us
  transfers between devices with their start and end apart: 37, of which 22 were waited for; matrix products, arithmetic and copies ran while one was open for 1% of the time, Pallas kernels for 15%

profile of v3, /device:TPU:16, one launch (start us, length us, event | category | flops | bytes accessed | tf_op | source)
XLA Modules:
  0.0 152.8 jit_solution(17004619299763933707)
XLA Ops:
  0.0 1.2 constant_dynamic-slice_fusion.3
  1.2 1.6 %collective-permute-start = (bf16[896,256]{1,0:T(8,128)(2,1)S(1)}, bf16[896,256]{1,0:T(8,128)(2,1)}, u32[]{:S(2)}, u32[]{:S(2)}) collective-permute-start(bf16[896,256]{1,0:T(8,128)(2,1)S(1)} %get-tuple-element.60), channel_id=1, source_target_pairs={{0,2},{1,3},{2,0},{3,1},{4,6},{5,7},{6,4},{7,5},{8,10},{9,11},{10,... | collective-permute-start | bytes 1376264 | tf_op jit(solution)/shard_map/Y0/ppermute | solution.py:20
  2.8 3.9 %shard_map.73 = (f32[128,128]{1,0:T(8,128)}, bf16[384,3584]{1,0:T(8,128)(2,1)}) custom-call(s32[1]{0:T(128)} %bitcast.1.station, bf16[128,3584]{1,0:T(8,128)(2,1)} %refs_5_.3, f32[3584]{0:T(1024)} %gain.1, bf16[4,3584]{1,0:T(4,128)(2,1)} %bitcast.8, s32[2,128]{1,0:T(2,128)} %bitcast.9), custom_call_target="tpu_custom_call" | custom-call | tf_op jit(solution)/shard_map/pallas_call | solution.py:84
  6.7 2.3 %collective-permute-start.1 = (f32[128,128]{1,0:T(8,128)}, f32[128,128]{1,0:T(8,128)S(1)}, u32[]{:S(2)}, u32[]{:S(2)}) collective-permute-start(f32[128,128]{1,0:T(8,128)} %get-tuple-element.31.table), channel_id=1, source_target_pairs={{4,8},{5,9},{6,10},{7,11},{8,4},{9,5},{10,6},{11,7},{20,24},{21,25... | collective-permute-start | bytes 196616 | tf_op jit(solution)/shard_map/table/ppermute | solution.py:340
  9.1 4.0 %collective-permute-done.1.table = f32[128,128]{1,0:T(8,128)S(1)} collective-permute-done((f32[128,128]{1,0:T(8,128)}, f32[128,128]{1,0:T(8,128)S(1)}, u32[]{:S(2)}, u32[]{:S(2)}) %collective-permute-start.1) | collective-permute-done | bytes 65568 | tf_op jit(solution)/shard_map/table/ppermute | solution.py:340
  13.7 5.2 %all-to-all-start = ((bf16[4,96,3584]{2,1,0:T(8,128)(2,1)}), bf16[4,96,3584]{2,1,0:T(8,128)(2,1)}, u32[]{:S(2)}, u32[]{:S(2)}) async-start(bf16[4,96,3584]{2,1,0:T(8,128)(2,1)} %bitcast.7), calls=%async_computation | async-start | bytes 5505024 | tf_op jit(solution)/shard_map/all_to_all | solution.py:380
  18.9 1.5 collective-permute-start.7
  20.4 1.5 collective-permute-start.4
  21.9 1.2 constant_dynamic-slice_fusion.1
  23.1 6.8 %collective-permute-done.7.refs_8_ = bf16[896,256]{1,0:T(8,128)(2,1)} collective-permute-done((bf16[896,256]{1,0:T(8,128)(2,1)S(1)}, bf16[896,256]{1,0:T(8,128)(2,1)}, u32[]{:S(2)}, u32[]{:S(2)}) %collective-permute-start.7) | collective-permute-done | bytes 458784 | tf_op jit(solution)/shard_map/Y1/ppermute | solution.py:20
  29.9 1.4 collective-permute-done.4.refs_5_
  31.2 0.6 collective-permute-start.11
  31.8 1.4 collective-permute-start.8
  33.2 8.2 %collective-permute-done.11.refs_12_ = bf16[896,256]{1,0:T(8,128)(2,1)S(1)} collective-permute-done((bf16[896,256]{1,0:T(8,128)(2,1)S(1)}, bf16[896,256]{1,0:T(8,128)(2,1)S(1)}, u32[]{:S(2)}, u32[]{:S(2)}) %collective-permute-start.11) | collective-permute-done | bytes 458784 | tf_op jit(solution)/shard_map/Y2/ppermute | solution.py:20
  41.6 1.9 %collective-permute-start.15 = (bf16[896,256]{1,0:T(8,128)(2,1)S(1)}, bf16[896,256]{1,0:T(8,128)(2,1)S(1)}, u32[]{:S(2)}, u32[]{:S(2)}) collective-permute-start(bf16[896,256]{1,0:T(8,128)(2,1)S(1)} %get-tuple-element.38), channel_id=1, source_target_pairs={{0,2},{1,3},{2,0},{3,1},{4,6},{5,7},{6,4},{7,5},{8,10},{9,11},{10,... | collective-permute-start | bytes 1376264 | tf_op jit(solution)/shard_map/Y3/ppermute | solution.py:20
  43.6 1.8 %collective-permute-start.12 = (bf16[896,256]{1,0:T(8,128)(2,1)S(1)}, bf16[896,256]{1,0:T(8,128)(2,1)S(1)}, u32[]{:S(2)}, u32[]{:S(2)}) collective-permute-start(bf16[896,256]{1,0:T(8,128)(2,1)S(1)} %collective-permute-done.11.refs_12_), channel_id=1, source_target_pairs={{0,16},{16,0},{1,17},{17,1},{2,18},{18,2},{3,19},{19,3},{4,20},{20... | collective-permute-start | bytes 1376264 | tf_op jit(solution)/shard_map/X2/ppermute | solution.py:26
  45.9 4.8 %collective-permute-done.15.refs_16_ = bf16[896,256]{1,0:T(8,128)(2,1)S(1)} collective-permute-done((bf16[896,256]{1,0:T(8,128)(2,1)S(1)}, bf16[896,256]{1,0:T(8,128)(2,1)S(1)}, u32[]{:S(2)}, u32[]{:S(2)}) %collective-permute-start.15) | collective-permute-done | bytes 458784 | tf_op jit(solution)/shard_map/Y3/ppermute | solution.py:20
  50.7 1.3 collective-permute-done.12.refs_13_
  52.1 0.8 copy-done.14
  52.9 0.7 collective-permute-start.20
  53.6 1.7 %collective-permute-start.16 = (bf16[896,256]{1,0:T(8,128)(2,1)S(1)}, bf16[896,256]{1,0:T(8,128)(2,1)S(1)}, u32[]{:S(2)}, u32[]{:S(2)}) collective-permute-start(bf16[896,256]{1,0:T(8,128)(2,1)S(1)} %collective-permute-done.15.refs_16_), channel_id=1, source_target_pairs={{0,16},{16,0},{1,17},{17,1},{2,18},{18,2},{3,19},{19,3},{4,20},{20... | collective-permute-start | bytes 1376264 | tf_op jit(solution)/shard_map/X3/ppermute | solution.py:26
  55.3 10.7 %collective-permute-done.20.refs_22_ = bf16[128,1792]{1,0:T(8,128)(2,1)S(1)} collective-permute-done((bf16[128,1792]{1,0:T(8,128)(2,1)S(1)}, bf16[128,1792]{1,0:T(8,128)(2,1)S(1)}, u32[]{:S(2)}, u32[]{:S(2)}) %collective-permute-start.20) | collective-permute-done | bytes 458784 | tf_op jit(solution)/shard_map/Y4/ppermute | solution.py:20
  66.5 1.2 collective-permute-done.13.refs_14_
  67.8 1.8 %collective-permute-start.21 = (bf16[128,1792]{1,0:T(8,128)(2,1)S(1)}, bf16[128,1792]{1,0:T(8,128)(2,1)S(1)}, u32[]{:S(2)}, u32[]{:S(2)}) collective-permute-start(bf16[128,1792]{1,0:T(8,128)(2,1)S(1)} %collective-permute-done.20.refs_22_), channel_id=1, source_target_pairs={{0,16},{16,0},{1,17},{17,1},{2,18},{18,2},{3,19},{19,3},{4,20},{20... | collective-permute-start | bytes 1376264 | tf_op jit(solution)/shard_map/X4/ppermute | solution.py:26
  70.5 9.8 %collective-permute-done.21.refs_23_ = bf16[128,1792]{1,0:T(8,128)(2,1)S(1)} collective-permute-done((bf16[128,1792]{1,0:T(8,128)(2,1)S(1)}, bf16[128,1792]{1,0:T(8,128)(2,1)S(1)}, u32[]{:S(2)}, u32[]{:S(2)}) %collective-permute-start.21) | collective-permute-done | bytes 458784 | tf_op jit(solution)/shard_map/X4/ppermute | solution.py:26
  80.3 1.5 collective-permute-done.24.refs_2_
  81.9 0.9 collective-permute-start.25
  82.9 0.9 copy-done.24
  83.9 12.9 %shard_map.74 = (bf16[384,1024]{1,0:T(8,128)(2,1)}, bf16[96,1792]{1,0:T(8,128)(2,1)}, bf16[96,1792]{1,0:T(8,128)(2,1)}, bf16[96,1792]{1,0:T(8,128)(2,1)}, bf16[96,1792]{1,0:T(8,128)(2,1)}) custom-call(s32[1]{0:T(128)} %bitcast.4.group, s32[1]{0:T(128)} %bitcast.1.station, bf16[384,3584]{1,0:T(8,128)(2,1)} %bitcast.6.rows, bf16[3584,256]{1,0:T(8,128)(2,1)} %refs_0_.2, ...), custom_call_target="tpu_custom_call" | custom-call | tf_op jit(solution)/shard_map/pallas_call | solution.py:177
  97.8 0.9 collective-permute-done.27.refs_5_
  98.7 0.7 collective-permute-done.26.refs_4_
  99.4 1.1 copy-done.3
  100.5 3.7 %shard_map.75 = (bf16[96,1792]{1,0:T(8,128)(2,1)S(1)}, bf16[96,1792]{1,0:T(8,128)(2,1)S(1)}, bf16[96,1792]{1,0:T(8,128)(2,1)}, bf16[96,1792]{1,0:T(8,128)(2,1)S(1)}) custom-call(s32[1]{0:T(128)} %bitcast.4.group, bf16[384,1024]{1,0:T(8,128)(2,1)S(1)} %copy-done.3, bf16[256,3584]{1,0:T(8,128)(2,1)S(1)} %copy-done.1, ...), custom_call_target="tpu_custom_call" | custom-call | tf_op jit(solution)/shard_map/pallas_call | solution.py:213
  104.2 0.7 copy-done.7
  105.3 1.6 %collective-permute-start.32 = (bf16[96,1792]{1,0:T(8,128)(2,1)}, bf16[96,1792]{1,0:T(8,128)(2,1)S(1)}, u32[]{:S(2)}, u32[]{:S(2)}) collective-permute-start(bf16[96,1792]{1,0:T(8,128)(2,1)} %get-tuple-element.52), channel_id=1, source_target_pairs={{0,4},{1,5},{2,6},{3,7},{4,0},{5,1},{6,2},{7,3},{8,12},{9,13},{10,... | collective-permute-start | bytes 1032200 | tf_op jit(solution)/shard_map/near_back0/ppermute | solution.py:340
  107.0 0.8 collective-permute-done.33.refs_0_.refs_2_
  108.3 2.8 %collective-permute-start.35 = (bf16[128,1792]{1,0:T(8,128)(2,1)S(1)}, bf16[128,1792]{1,0:T(8,128)(2,1)S(1)}, u32[]{:S(2)}, u32[]{:S(2)}) collective-permute-start(bf16[128,1792]{1,0:T(8,128)(2,1)S(1)} %shard_map.77), channel_id=1, source_target_pairs={{4,8},{5,9},{6,10},{7,11},{8,4},{9,5},{10,6},{11,7},{20,24},{21,25... | collective-permute-start | bytes 1376264 | tf_op jit(solution)/shard_map/sum_back0/ppermute | solution.py:340
  111.1 5.0 %collective-permute-done.29.refs_0_.refs_2_ = bf16[96,1792]{1,0:T(8,128)(2,1)S(1)} collective-permute-done((bf16[96,1792]{1,0:T(8,128)(2,1)}, bf16[96,1792]{1,0:T(8,128)(2,1)S(1)}, u32[]{:S(2)}, u32[]{:S(2)}) %collective-permute-start.29) | collective-permute-done | bytes 344096 | tf_op jit(solution)/shard_map/mixed_back1/ppermute | solution.py:340
  116.6 3.0 %collective-permute-start.31 = (bf16[128,1792]{1,0:T(8,128)(2,1)S(1)}, bf16[128,1792]{1,0:T(8,128)(2,1)S(1)}, u32[]{:S(2)}, u32[]{:S(2)}) collective-permute-start(bf16[128,1792]{1,0:T(8,128)(2,1)S(1)} %shard_map.76), channel_id=1, source_target_pairs={{4,8},{5,9},{6,10},{7,11},{8,4},{9,5},{10,6},{11,7},{20,24},{21,25... | collective-permute-start | bytes 1376264 | tf_op jit(solution)/shard_map/sum_back1/ppermute | solution.py:340
  119.7 0.7 collective-permute-start.34
  120.4 1.7 %collective-permute-start.28 = (bf16[96,1792]{1,0:T(8,128)(2,1)S(1)}, bf16[96,1792]{1,0:T(8,128)(2,1)S(1)}, u32[]{:S(2)}, u32[]{:S(2)}) collective-permute-start(bf16[96,1792]{1,0:T(8,128)(2,1)S(1)} %copy-done.8), channel_id=1, source_target_pairs={{0,4},{1,5},{2,6},{3,7},{4,0},{5,1},{6,2},{7,3},{8,12},{9,13},{10,... | collective-permute-start | bytes 1032200 | tf_op jit(solution)/shard_map/near_back1/ppermute | solution.py:340
  122.1 5.6 %collective-permute-done.32.refs_1_ = bf16[96,1792]{1,0:T(8,128)(2,1)S(1)} collective-permute-done((bf16[96,1792]{1,0:T(8,128)(2,1)}, bf16[96,1792]{1,0:T(8,128)(2,1)S(1)}, u32[]{:S(2)}, u32[]{:S(2)}) %collective-permute-start.32) | collective-permute-done | bytes 344096 | tf_op jit(solution)/shard_map/near_back0/ppermute | solution.py:340
  127.7 0.7 collective-permute-start.30
  128.4 5.9 %collective-permute-done.35.refs_4_ = bf16[128,1792]{1,0:T(8,128)(2,1)S(1)} collective-permute-done((bf16[128,1792]{1,0:T(8,128)(2,1)S(1)}, bf16[128,1792]{1,0:T(8,128)(2,1)S(1)}, u32[]{:S(2)}, u32[]{:S(2)}) %collective-permute-start.35) | collective-permute-done | bytes 458784 | tf_op jit(solution)/shard_map/sum_back0/ppermute | solution.py:340
  134.3 2.0 %shard_map.78.refs_6_ = bf16[128,3584]{1,0:T(8,128)(2,1)} custom-call(s32[1]{0:T(128)} %bitcast.is_hub, f32[128,128]{1,0:T(8,128)S(1)} %copy-done.6, bf16[96,1792]{1,0:T(8,128)(2,1)S(1)} %copy-done.5, bf16[96,1792]{1,0:T(8,128)(2,1)S(1)} %collective-permute-done.32.refs_1_, bf16[96,1792]{1,0:T(8,128)(2,1)S(1)} %collective-permute-done.33.refs_0_.refs_2_, ...), custom_call_target="tpu_custom_call" | custom-call | tf_op jit(solution)/shard_map/pallas_call | solution.py:295
  136.3 3.9 %collective-permute-done.28.refs_1_ = bf16[96,1792]{1,0:T(8,128)(2,1)S(1)} collective-permute-done((bf16[96,1792]{1,0:T(8,128)(2,1)S(1)}, bf16[96,1792]{1,0:T(8,128)(2,1)S(1)}, u32[]{:S(2)}, u32[]{:S(2)}) %collective-permute-start.28) | collective-permute-done | bytes 344096 | tf_op jit(solution)/shard_map/near_back1/ppermute | solution.py:340
  140.1 10.6 %collective-permute-done.31.refs_4_ = bf16[128,1792]{1,0:T(8,128)(2,1)S(1)} collective-permute-done((bf16[128,1792]{1,0:T(8,128)(2,1)S(1)}, bf16[128,1792]{1,0:T(8,128)(2,1)S(1)}, u32[]{:S(2)}, u32[]{:S(2)}) %collective-permute-start.31) | collective-permute-done | bytes 458784 | tf_op jit(solution)/shard_map/sum_back1/ppermute | solution.py:340
  150.7 1.9 %shard_map.79 = bf16[128,3584]{1,0:T(8,128)(2,1)} custom-call(s32[1]{0:T(128)} %bitcast.is_hub, f32[128,128]{1,0:T(8,128)S(1)} %copy-done.6, bf16[96,1792]{1,0:T(8,128)(2,1)S(1)} %get-tuple-element.47.refs_0_, bf16[96,1792]{1,0:T(8,128)(2,1)S(1)} %collective-permute-done.28.refs_1_, ...), custom_call_target="tpu_custom_call", output_to_operand_aliasing={{}: (8, {})} | custom-call | tf_op jit(solution)/shard_map/pallas_call | solution.py:295
  (86 shorter events, 5.8 us)
Async XLA Ops:
  1.2 12.4 %collective-permute-start = (bf16[896,256]{1,0:T(8,128)(2,1)S(1)}, bf16[896,256]{1,0:T(8,128)(2,1)}, u32[]{:S(2)}, u32[]{:S(2)}) collective-permute-start(bf16[896,256]{1,0:T(8,128)(2,1)S(1)} %get-tuple-element.60), channel_id=1, source_target_pairs={{0,2},{1,3},{2,0},{3,1},{4,6},{5,7},{6,4},{7,5},{8,10},{9,11},{10,... | collective-permute-start | bytes 1376264 | tf_op jit(solution)/shard_map/Y0/ppermute | solution.py:20
  6.7 6.4 %collective-permute-start.1 = (f32[128,128]{1,0:T(8,128)}, f32[128,128]{1,0:T(8,128)S(1)}, u32[]{:S(2)}, u32[]{:S(2)}) collective-permute-start(f32[128,128]{1,0:T(8,128)} %get-tuple-element.31.table), channel_id=1, source_target_pairs={{4,8},{5,9},{6,10},{7,11},{8,4},{9,5},{10,6},{11,7},{20,24},{21,25... | collective-permute-start | bytes 196616 | tf_op jit(solution)/shard_map/table/ppermute | solution.py:340
  13.7 70.2 %all-to-all-start = ((bf16[4,96,3584]{2,1,0:T(8,128)(2,1)}), bf16[4,96,3584]{2,1,0:T(8,128)(2,1)}, u32[]{:S(2)}, u32[]{:S(2)}) async-start(bf16[4,96,3584]{2,1,0:T(8,128)(2,1)} %bitcast.7), calls=%async_computation | async-start | bytes 5505024 | tf_op jit(solution)/shard_map/all_to_all | solution.py:380
  18.9 26.5 %copy-start = (bf16[256,3584]{1,0:T(8,128)(2,1)S(1)}, bf16[256,3584]{1,0:T(8,128)(2,1)}, u32[]{:S(2)}) copy-start(bf16[256,3584]{1,0:T(8,128)(2,1)} %refs_0_.3) | copy-start | bytes 5505028
  18.9 11.0 %collective-permute-start.7 = (bf16[896,256]{1,0:T(8,128)(2,1)S(1)}, bf16[896,256]{1,0:T(8,128)(2,1)}, u32[]{:S(2)}, u32[]{:S(2)}) collective-permute-start(bf16[896,256]{1,0:T(8,128)(2,1)S(1)} %get-tuple-element.34), channel_id=1, source_target_pairs={{0,2},{1,3},{2,0},{3,1},{4,6},{5,7},{6,4},{7,5},{8,10},{9,11},{10,... | collective-permute-start | bytes 1376264 | tf_op jit(solution)/shard_map/Y1/ppermute | solution.py:20
  20.4 10.9 %collective-permute-start.4 = (bf16[896,256]{1,0:T(8,128)(2,1)}, bf16[896,256]{1,0:T(8,128)(2,1)}, u32[]{:S(2)}, u32[]{:S(2)}) collective-permute-start(bf16[896,256]{1,0:T(8,128)(2,1)} %collective-permute-done.refs_4_), channel_id=1, source_target_pairs={{0,16},{16,0},{1,17},{17,1},{2,18},{18,2},{3,19},{19,3},{4,20},{20... | collective-permute-start | bytes 1376264 | tf_op jit(solution)/shard_map/X0/ppermute | solution.py:26
  31.2 10.2 %collective-permute-start.11 = (bf16[896,256]{1,0:T(8,128)(2,1)S(1)}, bf16[896,256]{1,0:T(8,128)(2,1)S(1)}, u32[]{:S(2)}, u32[]{:S(2)}) collective-permute-start(bf16[896,256]{1,0:T(8,128)(2,1)S(1)} %get-tuple-element.36), channel_id=1, source_target_pairs={{0,2},{1,3},{2,0},{3,1},{4,6},{5,7},{6,4},{7,5},{8,10},{9,11},{10,... | collective-permute-start | bytes 1376264 | tf_op jit(solution)/shard_map/Y2/ppermute | solution.py:20
  31.8 9.8 %collective-permute-start.8 = (bf16[896,256]{1,0:T(8,128)(2,1)}, bf16[896,256]{1,0:T(8,128)(2,1)S(1)}, u32[]{:S(2)}, u32[]{:S(2)}) collective-permute-start(bf16[896,256]{1,0:T(8,128)(2,1)} %collective-permute-done.7.refs_8_), channel_id=1, source_target_pairs={{0,16},{16,0},{1,17},{17,1},{2,18},{18,2},{3,19},{19,3},{4,20},{20... | collective-permute-start | bytes 1376264 | tf_op jit(solution)/shard_map/X1/ppermute | solution.py:26
  33.2 12.6 %collective-permute-start.5 = (bf16[896,256]{1,0:T(8,128)(2,1)}, bf16[896,256]{1,0:T(8,128)(2,1)S(1)}, u32[]{:S(2)}, u32[]{:S(2)}) collective-permute-start(bf16[896,256]{1,0:T(8,128)(2,1)} %collective-permute-done.refs_4_), channel_id=1, source_target_pairs={{0,1},{1,0},{2,3},{3,2},{4,5},{5,4},{6,7},{7,6},{8,9},{9,8},{10,11... | collective-permute-start | bytes 1376264 | tf_op jit(solution)/shard_map/C0/ppermute | solution.py:20
  41.4 28.1 %copy-start.9 = (bf16[896,256]{1,0:T(8,128)(2,1)}, bf16[896,256]{1,0:T(8,128)(2,1)S(1)}, u32[]{:S(2)}) copy-start(bf16[896,256]{1,0:T(8,128)(2,1)S(1)} %collective-permute-done.11.refs_12_) | copy-start | bytes 1376260
  41.6 9.1 %collective-permute-start.15 = (bf16[896,256]{1,0:T(8,128)(2,1)S(1)}, bf16[896,256]{1,0:T(8,128)(2,1)S(1)}, u32[]{:S(2)}, u32[]{:S(2)}) collective-permute-start(bf16[896,256]{1,0:T(8,128)(2,1)S(1)} %get-tuple-element.38), channel_id=1, source_target_pairs={{0,2},{1,3},{2,0},{3,1},{4,6},{5,7},{6,4},{7,5},{8,10},{9,11},{10,... | collective-permute-start | bytes 1376264 | tf_op jit(solution)/shard_map/Y3/ppermute | solution.py:20
  43.6 8.5 %collective-permute-start.12 = (bf16[896,256]{1,0:T(8,128)(2,1)S(1)}, bf16[896,256]{1,0:T(8,128)(2,1)S(1)}, u32[]{:S(2)}, u32[]{:S(2)}) collective-permute-start(bf16[896,256]{1,0:T(8,128)(2,1)S(1)} %collective-permute-done.11.refs_12_), channel_id=1, source_target_pairs={{0,16},{16,0},{1,17},{17,1},{2,18},{18,2},{3,19},{19,3},{4,20},{20... | collective-permute-start | bytes 1376264 | tf_op jit(solution)/shard_map/X2/ppermute | solution.py:26
  45.3 24.6 %collective-permute-start.19 = (bf16[256,3584]{1,0:T(8,128)(2,1)S(1)}, bf16[256,3584]{1,0:T(8,128)(2,1)}, u32[]{:S(2)}, u32[]{:S(2)}) collective-permute-start(bf16[256,3584]{1,0:T(8,128)(2,1)S(1)} %copy-done), channel_id=1, source_target_pairs={{0,1},{1,0},{2,3},{3,2},{4,5},{5,4},{6,7},{7,6},{8,9},{9,8},{10,11... | collective-permute-start | bytes 5505032 | tf_op jit(solution)/shard_map/own/ppermute | solution.py:20
  45.3 24.6 %collective-permute-start.2 = (bf16[3584,256]{1,0:T(8,128)(2,1)}, bf16[3584,256]{1,0:T(8,128)(2,1)}, u32[]{:S(2)}, u32[]{:S(2)}) collective-permute-start(bf16[3584,256]{1,0:T(8,128)(2,1)} %refs_0_.2), channel_id=1, source_target_pairs={{0,1},{1,0},{2,3},{3,2},{4,5},{5,4},{6,7},{7,6},{8,9},{9,8},{10,11... | collective-permute-start | bytes 5505032 | tf_op jit(solution)/shard_map/own/ppermute | solution.py:20
  45.8 7.1 %collective-permute-start.9 = (bf16[896,256]{1,0:T(8,128)(2,1)}, bf16[896,256]{1,0:T(8,128)(2,1)}, u32[]{:S(2)}, u32[]{:S(2)}) collective-permute-start(bf16[896,256]{1,0:T(8,128)(2,1)} %collective-permute-done.7.refs_8_), channel_id=1, source_target_pairs={{0,1},{1,0},{2,3},{3,2},{4,5},{5,4},{6,7},{7,6},{8,9},{9,8},{10,11... | collective-permute-start | bytes 1376264 | tf_op jit(solution)/shard_map/C1/ppermute | solution.py:20
  50.7 33.1 %copy-start.13 = (bf16[896,256]{1,0:T(8,128)(2,1)}, bf16[896,256]{1,0:T(8,128)(2,1)S(1)}, u32[]{:S(2)}) copy-start(bf16[896,256]{1,0:T(8,128)(2,1)S(1)} %collective-permute-done.15.refs_16_) | copy-start | bytes 1376260
  50.7 2.9 %collective-permute-start.6 = (bf16[896,256]{1,0:T(8,128)(2,1)}, bf16[896,256]{1,0:T(8,128)(2,1)}, u32[]{:S(2)}, u32[]{:S(2)}) collective-permute-start(bf16[896,256]{1,0:T(8,128)(2,1)} %collective-permute-done.4.refs_5_), channel_id=1, source_target_pairs={{0,1},{1,0},{2,3},{3,2},{4,5},{5,4},{6,7},{7,6},{8,9},{9,8},{10,11... | collective-permute-start | bytes 1376264 | tf_op jit(solution)/shard_map/C0/ppermute | solution.py:20
  52.9 17.6 %collective-permute-start.3 = (bf16[3584,256]{1,0:T(8,128)(2,1)}, bf16[3584,256]{1,0:T(8,128)(2,1)}, u32[]{:S(2)}, u32[]{:S(2)}) collective-permute-start(bf16[3584,256]{1,0:T(8,128)(2,1)} %refs_1_.1), channel_id=1, source_target_pairs={{0,1},{1,0},{2,3},{3,2},{4,5},{5,4},{6,7},{7,6},{8,9},{9,8},{10,11... | collective-permute-start | bytes 5505032 | tf_op jit(solution)/shard_map/own/ppermute | solution.py:20
  52.9 17.1 %copy-start.15 = (bf16[896,256]{1,0:T(8,128)(2,1)S(1)}, bf16[896,256]{1,0:T(8,128)(2,1)}, u32[]{:S(2)}) copy-start(bf16[896,256]{1,0:T(8,128)(2,1)} %copy-done.14) | copy-start | bytes 1376260
  52.9 13.0 %collective-permute-start.20 = (bf16[128,1792]{1,0:T(8,128)(2,1)S(1)}, bf16[128,1792]{1,0:T(8,128)(2,1)S(1)}, u32[]{:S(2)}, u32[]{:S(2)}) collective-permute-start(bf16[128,1792]{1,0:T(8,128)(2,1)S(1)} %get-tuple-element.40), channel_id=1, source_target_pairs={{0,2},{1,3},{2,0},{3,1},{4,6},{5,7},{6,4},{7,5},{8,10},{9,11},{10,... | collective-permute-start | bytes 1376264 | tf_op jit(solution)/shard_map/Y4/ppermute | solution.py:20
  53.6 12.7 %collective-permute-start.16 = (bf16[896,256]{1,0:T(8,128)(2,1)S(1)}, bf16[896,256]{1,0:T(8,128)(2,1)S(1)}, u32[]{:S(2)}, u32[]{:S(2)}) collective-permute-start(bf16[896,256]{1,0:T(8,128)(2,1)S(1)} %collective-permute-done.15.refs_16_), channel_id=1, source_target_pairs={{0,16},{16,0},{1,17},{17,1},{2,18},{18,2},{3,19},{19,3},{4,20},{20... | collective-permute-start | bytes 1376264 | tf_op jit(solution)/shard_map/X3/ppermute | solution.py:26
  65.9 16.9 %copy-start.16 = (bf16[128,1792]{1,0:T(8,128)(2,1)}, bf16[128,1792]{1,0:T(8,128)(2,1)S(1)}, u32[]{:S(2)}) copy-start(bf16[128,1792]{1,0:T(8,128)(2,1)S(1)} %collective-permute-done.20.refs_22_) | copy-start | bytes 1376260
  65.9 1.8 %collective-permute-start.13 = (bf16[896,256]{1,0:T(8,128)(2,1)S(1)}, bf16[896,256]{1,0:T(8,128)(2,1)S(1)}, u32[]{:S(2)}, u32[]{:S(2)}) collective-permute-start(bf16[896,256]{1,0:T(8,128)(2,1)S(1)} %collective-permute-done.11.refs_12_), channel_id=1, source_target_pairs={{0,1},{1,0},{2,3},{3,2},{4,5},{5,4},{6,7},{7,6},{8,9},{9,8},{10,11... | collective-permute-start | bytes 1376264 | tf_op jit(solution)/shard_map/C2/ppermute | solution.py:20
  66.3 16.6 %copy-start.17 = (bf16[896,256]{1,0:T(8,128)(2,1)}, bf16[896,256]{1,0:T(8,128)(2,1)S(1)}, u32[]{:S(2)}) copy-start(bf16[896,256]{1,0:T(8,128)(2,1)S(1)} %collective-permute-done.16.refs_17_) | copy-start | bytes 1376260
  66.3 3.2 %collective-permute-start.10 = (bf16[896,256]{1,0:T(8,128)(2,1)S(1)}, bf16[896,256]{1,0:T(8,128)(2,1)S(1)}, u32[]{:S(2)}, u32[]{:S(2)}) collective-permute-start(bf16[896,256]{1,0:T(8,128)(2,1)S(1)} %copy-done.11), channel_id=1, source_target_pairs={{0,1},{1,0},{2,3},{3,2},{4,5},{5,4},{6,7},{7,6},{8,9},{9,8},{10,11... | collective-permute-start | bytes 1376264 | tf_op jit(solution)/shard_map/C1/ppermute | solution.py:20
  67.7 15.1 %copy-start.18 = (bf16[896,256]{1,0:T(8,128)(2,1)}, bf16[896,256]{1,0:T(8,128)(2,1)S(1)}, u32[]{:S(2)}) copy-start(bf16[896,256]{1,0:T(8,128)(2,1)S(1)} %collective-permute-done.13.refs_14_) | copy-start | bytes 1376260
  67.8 12.6 %collective-permute-start.21 = (bf16[128,1792]{1,0:T(8,128)(2,1)S(1)}, bf16[128,1792]{1,0:T(8,128)(2,1)S(1)}, u32[]{:S(2)}, u32[]{:S(2)}) collective-permute-start(bf16[128,1792]{1,0:T(8,128)(2,1)S(1)} %collective-permute-done.20.refs_22_), channel_id=1, source_target_pairs={{0,16},{16,0},{1,17},{17,1},{2,18},{18,2},{3,19},{19,3},{4,20},{20... | collective-permute-start | bytes 1376264 | tf_op jit(solution)/shard_map/X4/ppermute | solution.py:26
  69.5 12.3 %collective-permute-start.24 = (bf16[128,1792]{1,0:T(8,128)(2,1)S(1)}, bf16[128,1792]{1,0:T(8,128)(2,1)S(1)}, u32[]{:S(2)}, u32[]{:S(2)}) collective-permute-start(bf16[128,1792]{1,0:T(8,128)(2,1)S(1)} %get-tuple-element.43), channel_id=1, source_target_pairs={{0,2},{1,3},{2,0},{3,1},{4,6},{5,7},{6,4},{7,5},{8,10},{9,11},{10,... | collective-permute-start | bytes 1376264 | tf_op jit(solution)/shard_map/Y5/ppermute | solution.py:20
  69.9 11.9 %collective-permute-start.17 = (bf16[896,256]{1,0:T(8,128)(2,1)S(1)}, bf16[896,256]{1,0:T(8,128)(2,1)S(1)}, u32[]{:S(2)}, u32[]{:S(2)}) collective-permute-start(bf16[896,256]{1,0:T(8,128)(2,1)S(1)} %collective-permute-done.15.refs_16_), channel_id=1, source_target_pairs={{0,1},{1,0},{2,3},{3,2},{4,5},{5,4},{6,7},{7,6},{8,9},{9,8},{10,11... | collective-permute-start | bytes 1376264 | tf_op jit(solution)/shard_map/C3/ppermute | solution.py:20
  69.9 12.9 %collective-permute-start.14 = (bf16[896,256]{1,0:T(8,128)(2,1)S(1)}, bf16[896,256]{1,0:T(8,128)(2,1)S(1)}, u32[]{:S(2)}, u32[]{:S(2)}) collective-permute-start(bf16[896,256]{1,0:T(8,128)(2,1)S(1)} %copy-done.15), channel_id=1, source_target_pairs={{0,1},{1,0},{2,3},{3,2},{4,5},{5,4},{6,7},{7,6},{8,9},{9,8},{10,11... | collective-permute-start | bytes 1376264 | tf_op jit(solution)/shard_map/C2/ppermute | solution.py:20
  70.4 12.4 %collective-permute-start.22 = (bf16[128,1792]{1,0:T(8,128)(2,1)S(1)}, bf16[128,1792]{1,0:T(8,128)(2,1)S(1)}, u32[]{:S(2)}, u32[]{:S(2)}) collective-permute-start(bf16[128,1792]{1,0:T(8,128)(2,1)S(1)} %collective-permute-done.20.refs_22_), channel_id=1, source_target_pairs={{0,1},{1,0},{2,3},{3,2},{4,5},{5,4},{6,7},{7,6},{8,9},{9,8},{10,11... | collective-permute-start | bytes 1376264 | tf_op jit(solution)/shard_map/C4/ppermute | solution.py:20
  80.3 2.5 %collective-permute-start.18 = (bf16[896,256]{1,0:T(8,128)(2,1)S(1)}, bf16[896,256]{1,0:T(8,128)(2,1)S(1)}, u32[]{:S(2)}, u32[]{:S(2)}) collective-permute-start(bf16[896,256]{1,0:T(8,128)(2,1)S(1)} %collective-permute-done.16.refs_17_), channel_id=1, source_target_pairs={{0,1},{1,0},{2,3},{3,2},{4,5},{5,4},{6,7},{7,6},{8,9},{9,8},{10,11... | collective-permute-start | bytes 1376264 | tf_op jit(solution)/shard_map/C3/ppermute | solution.py:20
  81.9 1.9 %collective-permute-start.23 = (bf16[128,1792]{1,0:T(8,128)(2,1)S(1)}, bf16[128,1792]{1,0:T(8,128)(2,1)}, u32[]{:S(2)}, u32[]{:S(2)}) collective-permute-start(bf16[128,1792]{1,0:T(8,128)(2,1)S(1)} %collective-permute-done.21.refs_23_), channel_id=1, source_target_pairs={{0,1},{1,0},{2,3},{3,2},{4,5},{5,4},{6,7},{7,6},{8,9},{9,8},{10,11... | collective-permute-start | bytes 1376264 | tf_op jit(solution)/shard_map/C4/ppermute | solution.py:20
  81.9 15.0 %collective-permute-start.25 = (bf16[128,1792]{1,0:T(8,128)(2,1)S(1)}, bf16[128,1792]{1,0:T(8,128)(2,1)S(1)}, u32[]{:S(2)}, u32[]{:S(2)}) collective-permute-start(bf16[128,1792]{1,0:T(8,128)(2,1)S(1)} %collective-permute-done.24.refs_2_), channel_id=1, source_target_pairs={{0,16},{16,0},{1,17},{17,1},{2,18},{18,2},{3,19},{19,3},{4,20},{20... | collective-permute-start | bytes 1376264 | tf_op jit(solution)/shard_map/X5/ppermute | solution.py:26
  83.9 15.5 %copy-start.1 = (bf16[256,3584]{1,0:T(8,128)(2,1)S(1)}, bf16[256,3584]{1,0:T(8,128)(2,1)}, u32[]{:S(2)}) copy-start(bf16[256,3584]{1,0:T(8,128)(2,1)} %refs_0_.3) | copy-start | bytes 5505028
  96.9 1.9 %collective-permute-start.27 = (bf16[128,1792]{1,0:T(8,128)(2,1)S(1)}, bf16[128,1792]{1,0:T(8,128)(2,1)S(1)}, u32[]{:S(2)}, u32[]{:S(2)}) collective-permute-start(bf16[128,1792]{1,0:T(8,128)(2,1)S(1)} %collective-permute-done.25.refs_3_), channel_id=1, source_target_pairs={{0,1},{1,0},{2,3},{3,2},{4,5},{5,4},{6,7},{7,6},{8,9},{9,8},{10,11... | collective-permute-start | bytes 1376264 | tf_op jit(solution)/shard_map/C5/ppermute | solution.py:20
  97.1 2.3 %collective-permute-start.26 = (bf16[128,1792]{1,0:T(8,128)(2,1)S(1)}, bf16[128,1792]{1,0:T(8,128)(2,1)S(1)}, u32[]{:S(2)}, u32[]{:S(2)}) collective-permute-start(bf16[128,1792]{1,0:T(8,128)(2,1)S(1)} %collective-permute-done.24.refs_2_), channel_id=1, source_target_pairs={{0,1},{1,0},{2,3},{3,2},{4,5},{5,4},{6,7},{7,6},{8,9},{9,8},{10,11... | collective-permute-start | bytes 1376264 | tf_op jit(solution)/shard_map/C5/ppermute | solution.py:20
  97.4 10.3 %collective-permute-start.33 = (bf16[96,1792]{1,0:T(8,128)(2,1)}, bf16[96,1792]{1,0:T(8,128)(2,1)S(1)}, u32[]{:S(2)}, u32[]{:S(2)}) collective-permute-start(bf16[96,1792]{1,0:T(8,128)(2,1)} %get-tuple-element.53), channel_id=1, source_target_pairs={{8,0},{9,1},{10,2},{11,3},{0,4},{1,5},{2,6},{3,7},{12,8},{13,9},{1... | collective-permute-start | bytes 1032200 | tf_op jit(solution)/shard_map/mixed_back0/ppermute | solution.py:340
  104.9 29.4 %copy-start.2 = (bf16[128,3584]{1,0:T(8,128)(2,1)S(1)}, bf16[128,3584]{1,0:T(8,128)(2,1)}, u32[]{:S(2)}) copy-start(bf16[128,3584]{1,0:T(8,128)(2,1)} %refs_5_.3) | copy-start | bytes 2752516
  104.9 29.4 %copy-start.5 = (bf16[96,1792]{1,0:T(8,128)(2,1)S(1)}, bf16[96,1792]{1,0:T(8,128)(2,1)}, u32[]{:S(2)}) copy-start(bf16[96,1792]{1,0:T(8,128)(2,1)} %get-tuple-element.51.refs_0_) | copy-start | bytes 1032196
  104.9 29.4 %copy-start.6 = (f32[128,128]{1,0:T(8,128)S(1)}, f32[128,128]{1,0:T(8,128)}, u32[]{:S(2)}) copy-start(f32[128,128]{1,0:T(8,128)} %get-tuple-element.31.table) | copy-start | bytes 196612
  104.9 11.1 %collective-permute-start.29 = (bf16[96,1792]{1,0:T(8,128)(2,1)}, bf16[96,1792]{1,0:T(8,128)(2,1)S(1)}, u32[]{:S(2)}, u32[]{:S(2)}) collective-permute-start(bf16[96,1792]{1,0:T(8,128)(2,1)} %get-tuple-element.49), channel_id=1, source_target_pairs={{8,0},{9,1},{10,2},{11,3},{0,4},{1,5},{2,6},{3,7},{12,8},{13,9},{1... | collective-permute-start | bytes 1032200 | tf_op jit(solution)/shard_map/mixed_back1/ppermute | solution.py:340
  105.3 22.4 %collective-permute-start.32 = (bf16[96,1792]{1,0:T(8,128)(2,1)}, bf16[96,1792]{1,0:T(8,128)(2,1)S(1)}, u32[]{:S(2)}, u32[]{:S(2)}) collective-permute-start(bf16[96,1792]{1,0:T(8,128)(2,1)} %get-tuple-element.52), channel_id=1, source_target_pairs={{0,4},{1,5},{2,6},{3,7},{4,0},{5,1},{6,2},{7,3},{8,12},{9,13},{10,... | collective-permute-start | bytes 1032200 | tf_op jit(solution)/shard_map/near_back0/ppermute | solution.py:340
  108.3 26.0 %collective-permute-start.35 = (bf16[128,1792]{1,0:T(8,128)(2,1)S(1)}, bf16[128,1792]{1,0:T(8,128)(2,1)S(1)}, u32[]{:S(2)}, u32[]{:S(2)}) collective-permute-start(bf16[128,1792]{1,0:T(8,128)(2,1)S(1)} %shard_map.77), channel_id=1, source_target_pairs={{4,8},{5,9},{6,10},{7,11},{8,4},{9,5},{10,6},{11,7},{20,24},{21,25... | collective-permute-start | bytes 1376264 | tf_op jit(solution)/shard_map/sum_back0/ppermute | solution.py:340
  116.6 34.1 %collective-permute-start.31 = (bf16[128,1792]{1,0:T(8,128)(2,1)S(1)}, bf16[128,1792]{1,0:T(8,128)(2,1)S(1)}, u32[]{:S(2)}, u32[]{:S(2)}) collective-permute-start(bf16[128,1792]{1,0:T(8,128)(2,1)S(1)} %shard_map.76), channel_id=1, source_target_pairs={{4,8},{5,9},{6,10},{7,11},{8,4},{9,5},{10,6},{11,7},{20,24},{21,25... | collective-permute-start | bytes 1376264 | tf_op jit(solution)/shard_map/sum_back1/ppermute | solution.py:340
  119.7 8.7 %collective-permute-start.34 = (bf16[96,1792]{1,0:T(8,128)(2,1)S(1)}, bf16[96,1792]{1,0:T(8,128)(2,1)S(1)}, u32[]{:S(2)}, u32[]{:S(2)}) collective-permute-start(bf16[96,1792]{1,0:T(8,128)(2,1)S(1)} %copy-done.4), channel_id=1, source_target_pairs={{0,12},{1,13},{2,14},{3,15},{12,0},{13,1},{14,2},{15,3},{16,28},{1... | collective-permute-start | bytes 1032200 | tf_op jit(solution)/shard_map/far_back0/ppermute | solution.py:340
  120.4 19.8 %collective-permute-start.28 = (bf16[96,1792]{1,0:T(8,128)(2,1)S(1)}, bf16[96,1792]{1,0:T(8,128)(2,1)S(1)}, u32[]{:S(2)}, u32[]{:S(2)}) collective-permute-start(bf16[96,1792]{1,0:T(8,128)(2,1)S(1)} %copy-done.8), channel_id=1, source_target_pairs={{0,4},{1,5},{2,6},{3,7},{4,0},{5,1},{6,2},{7,3},{8,12},{9,13},{10,... | collective-permute-start | bytes 1032200 | tf_op jit(solution)/shard_map/near_back1/ppermute | solution.py:340
  127.7 12.4 %collective-permute-start.30 = (bf16[96,1792]{1,0:T(8,128)(2,1)S(1)}, bf16[96,1792]{1,0:T(8,128)(2,1)S(1)}, u32[]{:S(2)}, u32[]{:S(2)}) collective-permute-start(bf16[96,1792]{1,0:T(8,128)(2,1)S(1)} %get-tuple-element.50.refs_1_), channel_id=1, source_target_pairs={{0,12},{1,13},{2,14},{3,15},{12,0},{13,1},{14,2},{15,3},{16,28},{1... | collective-permute-start | bytes 1032200 | tf_op jit(solution)/shard_map/far_back1/ppermute | solution.py:340
  (14 other events, 74.1 us)

commit v4 on v3

--- a/solution.py
+++ b/solution.py
@@ -108,13 +108,14 @@
     return pieces
 
 
-def down_product(act, wd, outs):
+def down_product(act, wd, outs, first):
     block_rows = outs[0].shape[0]
+    held = pl.ds(first * block_rows, len(outs) * block_rows)
     width = wd.shape[1]
     step = 256 if width % 256 == 0 else 128
     for base in range(0, width, step):
         span = pl.ds(base, step)
-        value = jnp.dot(act[...], wd[:, span], preferred_element_type=jnp.float32)
+        value = jnp.dot(act[held, :], wd[:, span], preferred_element_type=jnp.float32)
         value = value.astype(jnp.bfloat16)
         for i, out in enumerate(outs):
             out[:, span] = value[i * block_rows : (i + 1) * block_rows, :]
@@ -165,10 +166,10 @@
         ).astype(jnp.bfloat16)
     for copy in stages[members]:
         copy.wait()
-    down_product(act, wd, outs)
-
-
-def expert_first(group, station, rows, weights, copies, downs, down_copies, sizes, members):
+    down_product(act, wd, outs, x.shape[0] // block_rows - len(outs))
+
+
+def expert_first(group, station, rows, weights, copies, downs, down_copies, sizes, members, done):
     block_rows, hidden, groups = sizes
     total_rows, width = rows.shape
     columns = down_copies[0][-1]
@@ -177,10 +178,10 @@
     out = pl.pallas_call(
         functools.partial(expert_kernel, plan),
         out_shape=[jax.ShapeDtypeStruct((total_rows, members * hidden), jnp.bfloat16)]
-        + [jax.ShapeDtypeStruct((block_rows, columns), jnp.bfloat16)] * blocks,
+        + [jax.ShapeDtypeStruct((block_rows, columns), jnp.bfloat16)] * done,
         in_specs=[pl.BlockSpec(memory_space=pltpu.SMEM)] * 2
         + [pl.BlockSpec(memory_space=pl.ANY)] * (1 + len(copies) + len(down_copies)),
-        out_specs=[pl.BlockSpec(memory_space=pltpu.VMEM)] * (1 + blocks),
+        out_specs=[pl.BlockSpec(memory_space=pltpu.VMEM)] * (1 + done),
         scratch_shapes=[
             pltpu.VMEM((total_rows, width), jnp.bfloat16),
             pltpu.VMEM((members, width, 2 * hidden), jnp.bfloat16),
@@ -202,12 +203,11 @@
         copy.start()
     for copy in waits:
         copy.wait()
-    down_product(act, wd, outs)
-
-
-def expert_later(group, act, downs, copies, sizes):
+    down_product(act, wd, outs, 0)
+
+
+def expert_later(group, act, downs, copies, sizes, blocks):
     block_rows, hidden, groups = sizes
-    blocks = act.shape[0] // block_rows
     columns = copies[0][-1]
     whole = pl.BlockSpec(memory_space=pltpu.VMEM)
     return pl.pallas_call(
@@ -386,7 +386,7 @@
     for n, (sent, distance, gate_up, chunk) in enumerate(jobs):
         if n == first_jobs:
             act, first_outs = expert_first(
-                group, station[None], rows, weights, copies, downs[0], down_copies[0], sizes, members
+                group, station[None], rows, weights, copies, downs[0], down_copies[0], sizes, members, half
             )
         for offset in range(2):
             for shift, part in enumerate([Y[n]] + X[n]):
@@ -406,7 +406,10 @@
     classes = [(r, r < half) for r in range(experts)]
     layer_out = None
     for c, (base, size) in enumerate(columns):
-        outs = first_outs if c == 0 else expert_later(group, act, downs[c], down_copies[c], sizes)
+        count = half if c == 0 else experts
+        outs = list(expert_later(group, act, downs[c], down_copies[c], sizes, count))
+        if c == 0:
+            outs += first_outs
         back = [outs[0]] + [None] * last
         for r in mixed:
             route = {b: a for a, b in mixed[r].items()}

time: 153 us -> 152 us (level)
  waiting for transfers between devices: 84.2 us -> 80.7 us
  Pallas kernels: 25.5 us -> 27.7 us
    pallas_call x1 -> x2, Pallas kernels: 3.66 us -> 6.87 us  [expert_later(): pl.pallas_call(functools.partial(down_kernel, (hidden, groups, copies)),...]
    ppermute x9, waiting for transfers between devices: 35.7 us -> 32.8 us  [along(): return lax.ppermute(value, 'expert', pairs)]
    unnamed x50 -> x66, local copies, waits for them, and re-layouts: 3.68 us -> 3.64 us
  transfers between devices with their start and end apart: 37 -> 37, of which waited for: 22 -> 19; matrix products, arithmetic and copies ran while one was open for 1% -> 1% of each run, Pallas kernels for 15% -> 17%
where the time goes in v4:
time: 152 us
  waiting for transfers between devices  80.7 us (53%)
  starting transfers between devices  36.7 us (24%)
  Pallas kernels  27.7 us (18%)
  local copies, waits for them, and re-layouts  6.14 us (4%)
    ppermute x21, waiting for transfers between devices, flipped(): return lax.ppermute(value, 'expert', pairs)  35 us
    ppermute x9, waiting for transfers between devices, along(): return lax.ppermute(value, 'expert', pairs)  32.8 us
    ppermute x9, starting transfers between devices, along(): return lax.ppermute(value, 'expert', pairs)  13.9 us
    ppermute x6, waiting for transfers between devices, turned(): return lax.ppermute(value, 'groups', pairs)  12.9 us
    pallas_call x1, Pallas kernels, expert_first(): pl.pallas_call(functools.partial(expert_kernel, plan), out_shape=[jax.Sha...  11.9 us
    ppermute x21, starting transfers between devices, flipped(): return lax.ppermute(value, 'expert', pairs)  8.85 us
    ppermute x6, starting transfers between devices, turned(): return lax.ppermute(value, 'groups', pairs)  8.82 us
    pallas_call x2, Pallas kernels, expert_later(): pl.pallas_call(functools.partial(down_kernel, (hidden, groups, copies)),...  6.87 us
  transfers between devices with their start and end apart: 37, of which 19 were waited for; matrix products, arithmetic and copies ran while one was open for 1% of the time, Pallas kernels for 17%

profile of v4, /device:TPU:16, one launch (start us, length us, event | category | flops | bytes accessed | tf_op | source)
XLA Modules:
  0.0 151.8 jit_solution(7409499851635155750)
XLA Ops:
  0.0 1.2 constant_dynamic-slice_fusion.3
  1.2 1.6 %collective-permute-start = (bf16[896,256]{1,0:T(8,128)(2,1)S(1)}, bf16[896,256]{1,0:T(8,128)(2,1)S(1)}, u32[]{:S(2)}, u32[]{:S(2)}) collective-permute-start(bf16[896,256]{1,0:T(8,128)(2,1)S(1)} %get-tuple-element.60), channel_id=1, source_target_pairs={{0,2},{1,3},{2,0},{3,1},{4,6},{5,7},{6,4},{7,5},{8,10},{9,11},{10,... | collective-permute-start | bytes 1376264 | tf_op jit(solution)/shard_map/Y0/ppermute | solution.py:20
  2.8 4.0 %shard_map.73 = (f32[128,128]{1,0:T(8,128)}, bf16[384,3584]{1,0:T(8,128)(2,1)}) custom-call(s32[1]{0:T(128)} %bitcast.1.station, bf16[128,3584]{1,0:T(8,128)(2,1)} %refs_5_.3, f32[3584]{0:T(1024)} %gain.1, bf16[4,3584]{1,0:T(4,128)(2,1)} %bitcast.8, s32[2,128]{1,0:T(2,128)} %bitcast.9), custom_call_target="tpu_custom_call" | custom-call | tf_op jit(solution)/shard_map/pallas_call | solution.py:84
  6.8 2.3 %collective-permute-start.1 = (f32[128,128]{1,0:T(8,128)}, f32[128,128]{1,0:T(8,128)S(1)}, u32[]{:S(2)}, u32[]{:S(2)}) collective-permute-start(f32[128,128]{1,0:T(8,128)} %get-tuple-element.31.table), channel_id=1, source_target_pairs={{4,8},{5,9},{6,10},{7,11},{8,4},{9,5},{10,6},{11,7},{20,24},{21,25... | collective-permute-start | bytes 196616 | tf_op jit(solution)/shard_map/table/ppermute | solution.py:340
  9.1 4.0 %collective-permute-done.1.table = f32[128,128]{1,0:T(8,128)S(1)} collective-permute-done((f32[128,128]{1,0:T(8,128)}, f32[128,128]{1,0:T(8,128)S(1)}, u32[]{:S(2)}, u32[]{:S(2)}) %collective-permute-start.1) | collective-permute-done | bytes 65568 | tf_op jit(solution)/shard_map/table/ppermute | solution.py:340
  13.5 5.2 %all-to-all-start = ((bf16[4,96,3584]{2,1,0:T(8,128)(2,1)}), bf16[4,96,3584]{2,1,0:T(8,128)(2,1)}, u32[]{:S(2)}, u32[]{:S(2)}) async-start(bf16[4,96,3584]{2,1,0:T(8,128)(2,1)} %bitcast.7), calls=%async_computation | async-start | bytes 5505024 | tf_op jit(solution)/shard_map/all_to_all | solution.py:380
  18.8 1.5 %collective-permute-start.7 = (bf16[896,256]{1,0:T(8,128)(2,1)S(1)}, bf16[896,256]{1,0:T(8,128)(2,1)S(1)}, u32[]{:S(2)}, u32[]{:S(2)}) collective-permute-start(bf16[896,256]{1,0:T(8,128)(2,1)S(1)} %get-tuple-element.34), channel_id=1, source_target_pairs={{0,2},{1,3},{2,0},{3,1},{4,6},{5,7},{6,4},{7,5},{8,10},{9,11},{10,... | collective-permute-start | bytes 1376264 | tf_op jit(solution)/shard_map/Y1/ppermute | solution.py:20
  20.3 1.5 collective-permute-start.4
  21.8 1.2 constant_dynamic-slice_fusion.1
  23.0 6.7 %collective-permute-done.7.refs_8_ = bf16[896,256]{1,0:T(8,128)(2,1)S(1)} collective-permute-done((bf16[896,256]{1,0:T(8,128)(2,1)S(1)}, bf16[896,256]{1,0:T(8,128)(2,1)S(1)}, u32[]{:S(2)}, u32[]{:S(2)}) %collective-permute-start.7) | collective-permute-done | bytes 458784 | tf_op jit(solution)/shard_map/Y1/ppermute | solution.py:20
  29.7 1.3 collective-permute-done.4.refs_5_
  31.5 1.4 collective-permute-start.8
  32.9 8.4 %collective-permute-done.11.refs_12_ = bf16[896,256]{1,0:T(8,128)(2,1)S(1)} collective-permute-done((bf16[896,256]{1,0:T(8,128)(2,1)S(1)}, bf16[896,256]{1,0:T(8,128)(2,1)S(1)}, u32[]{:S(2)}, u32[]{:S(2)}) %collective-permute-start.11) | collective-permute-done | bytes 458784 | tf_op jit(solution)/shard_map/Y2/ppermute | solution.py:20
  41.4 1.7 %collective-permute-start.15 = (bf16[896,256]{1,0:T(8,128)(2,1)S(1)}, bf16[896,256]{1,0:T(8,128)(2,1)S(1)}, u32[]{:S(2)}, u32[]{:S(2)}) collective-permute-start(bf16[896,256]{1,0:T(8,128)(2,1)S(1)} %get-tuple-element.38), channel_id=1, source_target_pairs={{0,2},{1,3},{2,0},{3,1},{4,6},{5,7},{6,4},{7,5},{8,10},{9,11},{10,... | collective-permute-start | bytes 1376264 | tf_op jit(solution)/shard_map/Y3/ppermute | solution.py:20
  43.1 1.6 %collective-permute-start.12 = (bf16[896,256]{1,0:T(8,128)(2,1)S(1)}, bf16[896,256]{1,0:T(8,128)(2,1)S(1)}, u32[]{:S(2)}, u32[]{:S(2)}) collective-permute-start(bf16[896,256]{1,0:T(8,128)(2,1)S(1)} %collective-permute-done.11.refs_12_), channel_id=1, source_target_pairs={{0,16},{16,0},{1,17},{17,1},{2,18},{18,2},{3,19},{19,3},{4,20},{20... | collective-permute-start | bytes 1376264 | tf_op jit(solution)/shard_map/X2/ppermute | solution.py:26
  45.3 5.1 %collective-permute-done.15.refs_16_ = bf16[896,256]{1,0:T(8,128)(2,1)S(1)} collective-permute-done((bf16[896,256]{1,0:T(8,128)(2,1)S(1)}, bf16[896,256]{1,0:T(8,128)(2,1)S(1)}, u32[]{:S(2)}, u32[]{:S(2)}) %collective-permute-start.15) | collective-permute-done | bytes 458784 | tf_op jit(solution)/shard_map/Y3/ppermute | solution.py:20
  50.4 1.2 collective-permute-done.12.refs_13_
  51.6 0.8 copy-done.25
  52.5 0.8 collective-permute-start.20
  53.4 1.6 %collective-permute-start.16 = (bf16[896,256]{1,0:T(8,128)(2,1)S(1)}, bf16[896,256]{1,0:T(8,128)(2,1)S(1)}, u32[]{:S(2)}, u32[]{:S(2)}) collective-permute-start(bf16[896,256]{1,0:T(8,128)(2,1)S(1)} %copy-done.24), channel_id=1, source_target_pairs={{0,16},{16,0},{1,17},{17,1},{2,18},{18,2},{3,19},{19,3},{4,20},{20... | collective-permute-start | bytes 1376264 | tf_op jit(solution)/shard_map/X3/ppermute | solution.py:26
  55.0 10.5 %collective-permute-done.20.refs_22_.refs_2_ = bf16[128,1792]{1,0:T(8,128)(2,1)S(1)} collective-permute-done((bf16[128,1792]{1,0:T(8,128)(2,1)S(1)}, bf16[128,1792]{1,0:T(8,128)(2,1)S(1)}, u32[]{:S(2)}, u32[]{:S(2)}) %collective-permute-start.20) | collective-permute-done | bytes 458784 | tf_op jit(solution)/shard_map/Y4/ppermute | solution.py:20
  65.4 0.9 collective-permute-done.16.refs_17_
  66.3 0.9 collective-permute-done.13.refs_14_
  67.3 1.6 %collective-permute-start.21 = (bf16[128,1792]{1,0:T(8,128)(2,1)S(1)}, bf16[128,1792]{1,0:T(8,128)(2,1)S(1)}, u32[]{:S(2)}, u32[]{:S(2)}) collective-permute-start(bf16[128,1792]{1,0:T(8,128)(2,1)S(1)} %collective-permute-done.20.refs_22_.refs_2_), channel_id=1, source_target_pairs={{0,16},{16,0},{1,17},{17,1},{2,18},{18,2},{3,19},{19,3},{4,20},{20... | collective-permute-start | bytes 1376264 | tf_op jit(solution)/shard_map/X4/ppermute | solution.py:26
  68.9 0.8 collective-permute-start.24
  70.3 9.5 %collective-permute-done.21.refs_23_.refs_3_ = bf16[128,1792]{1,0:T(8,128)(2,1)S(1)} collective-permute-done((bf16[128,1792]{1,0:T(8,128)(2,1)S(1)}, bf16[128,1792]{1,0:T(8,128)(2,1)S(1)}, u32[]{:S(2)}, u32[]{:S(2)}) %collective-permute-start.21) | collective-permute-done | bytes 458784 | tf_op jit(solution)/shard_map/X4/ppermute | solution.py:26
  79.8 1.4 collective-permute-done.24.refs_2_
  81.2 1.2 collective-permute-start.25
  82.4 0.8 copy-done.32
  84.0 11.9 %shard_map.74 = (bf16[384,1024]{1,0:T(8,128)(2,1)}, bf16[96,1792]{1,0:T(8,128)(2,1)}, bf16[96,1792]{1,0:T(8,128)(2,1)}) custom-call(s32[1]{0:T(128)} %bitcast.4.group, s32[1]{0:T(128)} %bitcast.1.station, bf16[384,3584]{1,0:T(8,128)(2,1)} %bitcast.6.rows, bf16[3584,256]{1,0:T(8,128)(2,1)} %refs_0_.3, bf16[3584,256]{1,0:T(8,128)(2,1)} %refs_1_.1, ...), custom_call_target="tpu_custom_call" | custom-call | tf_op jit(solution)/shard_map/pallas_call | solution.py:178
  96.9 1.1 collective-permute-done.27.refs_5_
  98.5 1.1 copy-done.3
  99.7 3.9 %shard_map.75 = (bf16[96,1792]{1,0:T(8,128)(2,1)S(1)}, bf16[96,1792]{1,0:T(8,128)(2,1)S(1)}, bf16[96,1792]{1,0:T(8,128)(2,1)}, bf16[96,1792]{1,0:T(8,128)(2,1)S(1)}) custom-call(s32[1]{0:T(128)} %bitcast.4.group, bf16[384,1024]{1,0:T(8,128)(2,1)S(1)} %copy-done.3, bf16[256,3584]{1,0:T(8,128)(2,1)S(1)} %copy-done.1, ...), custom_call_target="tpu_custom_call" | custom-call | tf_op jit(solution)/shard_map/pallas_call | solution.py:213
  103.6 0.6 collective-permute-start.29
  104.3 2.9 %shard_map.77 = (bf16[96,1792]{1,0:T(8,128)(2,1)S(1)}, bf16[96,1792]{1,0:T(8,128)(2,1)}) custom-call(s32[1]{0:T(128)} %bitcast.4.group, bf16[384,1024]{1,0:T(8,128)(2,1)S(1)} %copy-done.4, bf16[256,3584]{1,0:T(8,128)(2,1)S(1)} %copy-done.1, bf16[256,3584]{1,0:T(8,128)(2,1)} %collective-permute-done.19.refs_21_.refs_1_, bf16[128,1792]{1,0:T(8,128)(2,1)S(1)} %copy-done.6, ...), custom_call_target="tpu_custom_call" | custom-call | tf_op jit(solution)/shard_map/pallas_call | solution.py:213
  107.2 1.7 %collective-permute-start.32 = (bf16[96,1792]{1,0:T(8,128)(2,1)}, bf16[96,1792]{1,0:T(8,128)(2,1)S(1)}, u32[]{:S(2)}, u32[]{:S(2)}) collective-permute-start(bf16[96,1792]{1,0:T(8,128)(2,1)} %get-tuple-element.52), channel_id=1, source_target_pairs={{0,4},{1,5},{2,6},{3,7},{4,0},{5,1},{6,2},{7,3},{8,12},{9,13},{10,... | collective-permute-start | bytes 1032200 | tf_op jit(solution)/shard_map/near_back0/ppermute | solution.py:340
  109.5 3.0 %collective-permute-start.35 = (bf16[128,1792]{1,0:T(8,128)(2,1)S(1)}, bf16[128,1792]{1,0:T(8,128)(2,1)S(1)}, u32[]{:S(2)}, u32[]{:S(2)}) collective-permute-start(bf16[128,1792]{1,0:T(8,128)(2,1)S(1)} %shard_map.78), channel_id=1, source_target_pairs={{4,8},{5,9},{6,10},{7,11},{8,4},{9,5},{10,6},{11,7},{20,24},{21,25... | collective-permute-start | bytes 1376264 | tf_op jit(solution)/shard_map/sum_back0/ppermute | solution.py:340
  112.5 2.5 %collective-permute-done.29.refs_0_.refs_2_ = bf16[96,1792]{1,0:T(8,128)(2,1)S(1)} collective-permute-done((bf16[96,1792]{1,0:T(8,128)(2,1)}, bf16[96,1792]{1,0:T(8,128)(2,1)S(1)}, u32[]{:S(2)}, u32[]{:S(2)}) %collective-permute-start.29) | collective-permute-done | bytes 344096 | tf_op jit(solution)/shard_map/mixed_back1/ppermute | solution.py:340
  115.5 3.0 %collective-permute-start.31 = (bf16[128,1792]{1,0:T(8,128)(2,1)S(1)}, bf16[128,1792]{1,0:T(8,128)(2,1)S(1)}, u32[]{:S(2)}, u32[]{:S(2)}) collective-permute-start(bf16[128,1792]{1,0:T(8,128)(2,1)S(1)} %shard_map.76), channel_id=1, source_target_pairs={{4,8},{5,9},{6,10},{7,11},{8,4},{9,5},{10,6},{11,7},{20,24},{21,25... | collective-permute-start | bytes 1376264 | tf_op jit(solution)/shard_map/sum_back1/ppermute | solution.py:340
  118.6 0.7 collective-permute-start.34
  119.3 1.5 collective-permute-start.28
  120.7 6.2 %collective-permute-done.32.refs_1_ = bf16[96,1792]{1,0:T(8,128)(2,1)S(1)} collective-permute-done((bf16[96,1792]{1,0:T(8,128)(2,1)}, bf16[96,1792]{1,0:T(8,128)(2,1)S(1)}, u32[]{:S(2)}, u32[]{:S(2)}) %collective-permute-start.32) | collective-permute-done | bytes 344096 | tf_op jit(solution)/shard_map/near_back0/ppermute | solution.py:340
  127.0 0.7 collective-permute-start.30
  127.7 5.6 %collective-permute-done.35.refs_4_ = bf16[128,1792]{1,0:T(8,128)(2,1)S(1)} collective-permute-done((bf16[128,1792]{1,0:T(8,128)(2,1)S(1)}, bf16[128,1792]{1,0:T(8,128)(2,1)S(1)}, u32[]{:S(2)}, u32[]{:S(2)}) %collective-permute-start.35) | collective-permute-done | bytes 458784 | tf_op jit(solution)/shard_map/sum_back0/ppermute | solution.py:340
  133.2 1.9 %shard_map.79.refs_6_ = bf16[128,3584]{1,0:T(8,128)(2,1)} custom-call(s32[1]{0:T(128)} %bitcast.is_hub, f32[128,128]{1,0:T(8,128)S(1)} %copy-done.14, bf16[96,1792]{1,0:T(8,128)(2,1)S(1)} %get-tuple-element.51.refs_0_, bf16[96,1792]{1,0:T(8,128)(2,1)S(1)} %collective-permute-done.32.refs_1_, bf16[96,1792]{1,0:T(8,128)(2,1)S(1)} %collective-permute-done.33.refs_0_.refs_2_, ...), custom_call_target="tpu_custom_call" | custom-call | tf_op jit(solution)/shard_map/pallas_call | solution.py:295
  135.2 8.6 %collective-permute-done.28.refs_1_ = bf16[96,1792]{1,0:T(8,128)(2,1)S(1)} collective-permute-done((bf16[96,1792]{1,0:T(8,128)(2,1)S(1)}, bf16[96,1792]{1,0:T(8,128)(2,1)S(1)}, u32[]{:S(2)}, u32[]{:S(2)}) %collective-permute-start.28) | collective-permute-done | bytes 344096 | tf_op jit(solution)/shard_map/near_back1/ppermute | solution.py:340
  143.8 5.9 %collective-permute-done.31.refs_4_ = bf16[128,1792]{1,0:T(8,128)(2,1)S(1)} collective-permute-done((bf16[128,1792]{1,0:T(8,128)(2,1)S(1)}, bf16[128,1792]{1,0:T(8,128)(2,1)S(1)}, u32[]{:S(2)}, u32[]{:S(2)}) %collective-permute-start.31) | collective-permute-done | bytes 458784 | tf_op jit(solution)/shard_map/sum_back1/ppermute | solution.py:340
  149.7 1.9 %shard_map.80 = bf16[128,3584]{1,0:T(8,128)(2,1)} custom-call(s32[1]{0:T(128)} %bitcast.is_hub, f32[128,128]{1,0:T(8,128)S(1)} %copy-done.14, bf16[96,1792]{1,0:T(8,128)(2,1)S(1)} %get-tuple-element.47.refs_0_, bf16[96,1792]{1,0:T(8,128)(2,1)S(1)} %collective-permute-done.28.refs_1_, ...), custom_call_target="tpu_custom_call", output_to_operand_aliasing={{}: (8, {})} | custom-call | tf_op jit(solution)/shard_map/pallas_call | solution.py:295
  (103 shorter events, 5.7 us)
Async XLA Ops:
  1.2 12.3 %collective-permute-start = (bf16[896,256]{1,0:T(8,128)(2,1)S(1)}, bf16[896,256]{1,0:T(8,128)(2,1)S(1)}, u32[]{:S(2)}, u32[]{:S(2)}) collective-permute-start(bf16[896,256]{1,0:T(8,128)(2,1)S(1)} %get-tuple-element.60), channel_id=1, source_target_pairs={{0,2},{1,3},{2,0},{3,1},{4,6},{5,7},{6,4},{7,5},{8,10},{9,11},{10,... | collective-permute-start | bytes 1376264 | tf_op jit(solution)/shard_map/Y0/ppermute | solution.py:20
  6.8 6.4 %collective-permute-start.1 = (f32[128,128]{1,0:T(8,128)}, f32[128,128]{1,0:T(8,128)S(1)}, u32[]{:S(2)}, u32[]{:S(2)}) collective-permute-start(f32[128,128]{1,0:T(8,128)} %get-tuple-element.31.table), channel_id=1, source_target_pairs={{4,8},{5,9},{6,10},{7,11},{8,4},{9,5},{10,6},{11,7},{20,24},{21,25... | collective-permute-start | bytes 196616 | tf_op jit(solution)/shard_map/table/ppermute | solution.py:340
  13.5 19.4 %copy-start.17 = (bf16[896,256]{1,0:T(8,128)(2,1)}, bf16[896,256]{1,0:T(8,128)(2,1)S(1)}, u32[]{:S(2)}) copy-start(bf16[896,256]{1,0:T(8,128)(2,1)S(1)} %collective-permute-done.refs_4_) | copy-start | bytes 1376260
  13.5 69.7 %all-to-all-start = ((bf16[4,96,3584]{2,1,0:T(8,128)(2,1)}), bf16[4,96,3584]{2,1,0:T(8,128)(2,1)}, u32[]{:S(2)}, u32[]{:S(2)}) async-start(bf16[4,96,3584]{2,1,0:T(8,128)(2,1)} %bitcast.7), calls=%async_computation | async-start | bytes 5505024 | tf_op jit(solution)/shard_map/all_to_all | solution.py:380
  18.8 25.9 %copy-start = (bf16[256,3584]{1,0:T(8,128)(2,1)S(1)}, bf16[256,3584]{1,0:T(8,128)(2,1)}, u32[]{:S(2)}) copy-start(bf16[256,3584]{1,0:T(8,128)(2,1)} %refs_0_.5) | copy-start | bytes 5505028
  18.8 10.9 %collective-permute-start.7 = (bf16[896,256]{1,0:T(8,128)(2,1)S(1)}, bf16[896,256]{1,0:T(8,128)(2,1)S(1)}, u32[]{:S(2)}, u32[]{:S(2)}) collective-permute-start(bf16[896,256]{1,0:T(8,128)(2,1)S(1)} %get-tuple-element.34), channel_id=1, source_target_pairs={{0,2},{1,3},{2,0},{3,1},{4,6},{5,7},{6,4},{7,5},{8,10},{9,11},{10,... | collective-permute-start | bytes 1376264 | tf_op jit(solution)/shard_map/Y1/ppermute | solution.py:20
  20.3 10.7 %collective-permute-start.4 = (bf16[896,256]{1,0:T(8,128)(2,1)S(1)}, bf16[896,256]{1,0:T(8,128)(2,1)}, u32[]{:S(2)}, u32[]{:S(2)}) collective-permute-start(bf16[896,256]{1,0:T(8,128)(2,1)S(1)} %collective-permute-done.refs_4_), channel_id=1, source_target_pairs={{0,16},{16,0},{1,17},{17,1},{2,18},{18,2},{3,19},{19,3},{4,20},{20... | collective-permute-start | bytes 1376264 | tf_op jit(solution)/shard_map/X0/ppermute | solution.py:26
  29.7 36.7 %copy-start.18 = (bf16[896,256]{1,0:T(8,128)(2,1)}, bf16[896,256]{1,0:T(8,128)(2,1)S(1)}, u32[]{:S(2)}) copy-start(bf16[896,256]{1,0:T(8,128)(2,1)S(1)} %collective-permute-done.7.refs_8_) | copy-start | bytes 1376260
  30.9 10.4 %collective-permute-start.11 = (bf16[896,256]{1,0:T(8,128)(2,1)S(1)}, bf16[896,256]{1,0:T(8,128)(2,1)S(1)}, u32[]{:S(2)}, u32[]{:S(2)}) collective-permute-start(bf16[896,256]{1,0:T(8,128)(2,1)S(1)} %get-tuple-element.36), channel_id=1, source_target_pairs={{0,2},{1,3},{2,0},{3,1},{4,6},{5,7},{6,4},{7,5},{8,10},{9,11},{10,... | collective-permute-start | bytes 1376264 | tf_op jit(solution)/shard_map/Y2/ppermute | solution.py:20
  31.5 9.8 %collective-permute-start.8 = (bf16[896,256]{1,0:T(8,128)(2,1)S(1)}, bf16[896,256]{1,0:T(8,128)(2,1)S(1)}, u32[]{:S(2)}, u32[]{:S(2)}) collective-permute-start(bf16[896,256]{1,0:T(8,128)(2,1)S(1)} %collective-permute-done.7.refs_8_), channel_id=1, source_target_pairs={{0,16},{16,0},{1,17},{17,1},{2,18},{18,2},{3,19},{19,3},{4,20},{20... | collective-permute-start | bytes 1376264 | tf_op jit(solution)/shard_map/X1/ppermute | solution.py:26
  32.9 12.3 %collective-permute-start.5 = (bf16[896,256]{1,0:T(8,128)(2,1)S(1)}, bf16[896,256]{1,0:T(8,128)(2,1)S(1)}, u32[]{:S(2)}, u32[]{:S(2)}) collective-permute-start(bf16[896,256]{1,0:T(8,128)(2,1)S(1)} %collective-permute-done.refs_4_), channel_id=1, source_target_pairs={{0,1},{1,0},{2,3},{3,2},{4,5},{5,4},{6,7},{7,6},{8,9},{9,8},{10,11... | collective-permute-start | bytes 1376264 | tf_op jit(solution)/shard_map/C0/ppermute | solution.py:20
  41.3 27.5 %copy-start.19 = (bf16[896,256]{1,0:T(8,128)(2,1)}, bf16[896,256]{1,0:T(8,128)(2,1)S(1)}, u32[]{:S(2)}) copy-start(bf16[896,256]{1,0:T(8,128)(2,1)S(1)} %collective-permute-done.11.refs_12_) | copy-start | bytes 1376260
  41.4 9.0 %collective-permute-start.15 = (bf16[896,256]{1,0:T(8,128)(2,1)S(1)}, bf16[896,256]{1,0:T(8,128)(2,1)S(1)}, u32[]{:S(2)}, u32[]{:S(2)}) collective-permute-start(bf16[896,256]{1,0:T(8,128)(2,1)S(1)} %get-tuple-element.38), channel_id=1, source_target_pairs={{0,2},{1,3},{2,0},{3,1},{4,6},{5,7},{6,4},{7,5},{8,10},{9,11},{10,... | collective-permute-start | bytes 1376264 | tf_op jit(solution)/shard_map/Y3/ppermute | solution.py:20
  43.1 8.5 %collective-permute-start.12 = (bf16[896,256]{1,0:T(8,128)(2,1)S(1)}, bf16[896,256]{1,0:T(8,128)(2,1)S(1)}, u32[]{:S(2)}, u32[]{:S(2)}) collective-permute-start(bf16[896,256]{1,0:T(8,128)(2,1)S(1)} %collective-permute-done.11.refs_12_), channel_id=1, source_target_pairs={{0,16},{16,0},{1,17},{17,1},{2,18},{18,2},{3,19},{19,3},{4,20},{20... | collective-permute-start | bytes 1376264 | tf_op jit(solution)/shard_map/X2/ppermute | solution.py:26
  44.7 25.0 %collective-permute-start.19 = (bf16[256,3584]{1,0:T(8,128)(2,1)S(1)}, bf16[256,3584]{1,0:T(8,128)(2,1)}, u32[]{:S(2)}, u32[]{:S(2)}) collective-permute-start(bf16[256,3584]{1,0:T(8,128)(2,1)S(1)} %copy-done), channel_id=1, source_target_pairs={{0,1},{1,0},{2,3},{3,2},{4,5},{5,4},{6,7},{7,6},{8,9},{9,8},{10,11... | collective-permute-start | bytes 5505032 | tf_op jit(solution)/shard_map/own/ppermute | solution.py:20
  44.7 25.0 %collective-permute-start.2 = (bf16[3584,256]{1,0:T(8,128)(2,1)}, bf16[3584,256]{1,0:T(8,128)(2,1)}, u32[]{:S(2)}, u32[]{:S(2)}) collective-permute-start(bf16[3584,256]{1,0:T(8,128)(2,1)} %refs_0_.3), channel_id=1, source_target_pairs={{0,1},{1,0},{2,3},{3,2},{4,5},{5,4},{6,7},{7,6},{8,9},{9,8},{10,11... | collective-permute-start | bytes 5505032 | tf_op jit(solution)/shard_map/own/ppermute | solution.py:20
  45.2 7.3 %collective-permute-start.9 = (bf16[896,256]{1,0:T(8,128)(2,1)S(1)}, bf16[896,256]{1,0:T(8,128)(2,1)}, u32[]{:S(2)}, u32[]{:S(2)}) collective-permute-start(bf16[896,256]{1,0:T(8,128)(2,1)S(1)} %collective-permute-done.7.refs_8_), channel_id=1, source_target_pairs={{0,1},{1,0},{2,3},{3,2},{4,5},{5,4},{6,7},{7,6},{8,9},{9,8},{10,11... | collective-permute-start | bytes 1376264 | tf_op jit(solution)/shard_map/C1/ppermute | solution.py:20
  50.4 2.9 %collective-permute-start.6 = (bf16[896,256]{1,0:T(8,128)(2,1)}, bf16[896,256]{1,0:T(8,128)(2,1)}, u32[]{:S(2)}, u32[]{:S(2)}) collective-permute-start(bf16[896,256]{1,0:T(8,128)(2,1)} %collective-permute-done.4.refs_5_), channel_id=1, source_target_pairs={{0,1},{1,0},{2,3},{3,2},{4,5},{5,4},{6,7},{7,6},{8,9},{9,8},{10,11... | collective-permute-start | bytes 1376264 | tf_op jit(solution)/shard_map/C0/ppermute | solution.py:20
  52.4 17.9 %collective-permute-start.3 = (bf16[3584,256]{1,0:T(8,128)(2,1)}, bf16[3584,256]{1,0:T(8,128)(2,1)}, u32[]{:S(2)}, u32[]{:S(2)}) collective-permute-start(bf16[3584,256]{1,0:T(8,128)(2,1)} %refs_1_.1), channel_id=1, source_target_pairs={{0,1},{1,0},{2,3},{3,2},{4,5},{5,4},{6,7},{7,6},{8,9},{9,8},{10,11... | collective-permute-start | bytes 5505032 | tf_op jit(solution)/shard_map/own/ppermute | solution.py:20
  52.4 17.3 %copy-start.26 = (bf16[896,256]{1,0:T(8,128)(2,1)S(1)}, bf16[896,256]{1,0:T(8,128)(2,1)}, u32[]{:S(2)}) copy-start(bf16[896,256]{1,0:T(8,128)(2,1)} %copy-done.25) | copy-start | bytes 1376260
  52.5 13.0 %collective-permute-start.20 = (bf16[128,1792]{1,0:T(8,128)(2,1)S(1)}, bf16[128,1792]{1,0:T(8,128)(2,1)S(1)}, u32[]{:S(2)}, u32[]{:S(2)}) collective-permute-start(bf16[128,1792]{1,0:T(8,128)(2,1)S(1)} %get-tuple-element.40), channel_id=1, source_target_pairs={{0,2},{1,3},{2,0},{3,1},{4,6},{5,7},{6,4},{7,5},{8,10},{9,11},{10,... | collective-permute-start | bytes 1376264 | tf_op jit(solution)/shard_map/Y4/ppermute | solution.py:20
  53.4 12.9 %collective-permute-start.16 = (bf16[896,256]{1,0:T(8,128)(2,1)S(1)}, bf16[896,256]{1,0:T(8,128)(2,1)S(1)}, u32[]{:S(2)}, u32[]{:S(2)}) collective-permute-start(bf16[896,256]{1,0:T(8,128)(2,1)S(1)} %copy-done.24), channel_id=1, source_target_pairs={{0,16},{16,0},{1,17},{17,1},{2,18},{18,2},{3,19},{19,3},{4,20},{20... | collective-permute-start | bytes 1376264 | tf_op jit(solution)/shard_map/X3/ppermute | solution.py:26
  65.4 17.8 %copy-start.5 = (bf16[128,1792]{1,0:T(8,128)(2,1)}, bf16[128,1792]{1,0:T(8,128)(2,1)S(1)}, u32[]{:S(2)}) copy-start(bf16[128,1792]{1,0:T(8,128)(2,1)S(1)} %collective-permute-done.20.refs_22_.refs_2_) | copy-start | bytes 1376260
  65.4 1.8 %collective-permute-start.13 = (bf16[896,256]{1,0:T(8,128)(2,1)S(1)}, bf16[896,256]{1,0:T(8,128)(2,1)S(1)}, u32[]{:S(2)}, u32[]{:S(2)}) collective-permute-start(bf16[896,256]{1,0:T(8,128)(2,1)S(1)} %collective-permute-done.11.refs_12_), channel_id=1, source_target_pairs={{0,1},{1,0},{2,3},{3,2},{4,5},{5,4},{6,7},{7,6},{8,9},{9,8},{10,11... | collective-permute-start | bytes 1376264 | tf_op jit(solution)/shard_map/C2/ppermute | solution.py:20
  66.3 16.1 %copy-start.27 = (bf16[896,256]{1,0:T(8,128)(2,1)}, bf16[896,256]{1,0:T(8,128)(2,1)S(1)}, u32[]{:S(2)}) copy-start(bf16[896,256]{1,0:T(8,128)(2,1)S(1)} %collective-permute-done.16.refs_17_) | copy-start | bytes 1376260
  66.3 2.5 %collective-permute-start.10 = (bf16[896,256]{1,0:T(8,128)(2,1)S(1)}, bf16[896,256]{1,0:T(8,128)(2,1)S(1)}, u32[]{:S(2)}, u32[]{:S(2)}) collective-permute-start(bf16[896,256]{1,0:T(8,128)(2,1)S(1)} %copy-done.21), channel_id=1, source_target_pairs={{0,1},{1,0},{2,3},{3,2},{4,5},{5,4},{6,7},{7,6},{8,9},{9,8},{10,11... | collective-permute-start | bytes 1376264 | tf_op jit(solution)/shard_map/C1/ppermute | solution.py:20
  67.3 15.1 %copy-start.28 = (bf16[896,256]{1,0:T(8,128)(2,1)}, bf16[896,256]{1,0:T(8,128)(2,1)S(1)}, u32[]{:S(2)}) copy-start(bf16[896,256]{1,0:T(8,128)(2,1)S(1)} %collective-permute-done.13.refs_14_) | copy-start | bytes 1376260
  67.3 12.6 %collective-permute-start.21 = (bf16[128,1792]{1,0:T(8,128)(2,1)S(1)}, bf16[128,1792]{1,0:T(8,128)(2,1)S(1)}, u32[]{:S(2)}, u32[]{:S(2)}) collective-permute-start(bf16[128,1792]{1,0:T(8,128)(2,1)S(1)} %collective-permute-done.20.refs_22_.refs_2_), channel_id=1, source_target_pairs={{0,16},{16,0},{1,17},{17,1},{2,18},{18,2},{3,19},{19,3},{4,20},{20... | collective-permute-start | bytes 1376264 | tf_op jit(solution)/shard_map/X4/ppermute | solution.py:26
  68.9 12.3 %collective-permute-start.24 = (bf16[128,1792]{1,0:T(8,128)(2,1)S(1)}, bf16[128,1792]{1,0:T(8,128)(2,1)S(1)}, u32[]{:S(2)}, u32[]{:S(2)}) collective-permute-start(bf16[128,1792]{1,0:T(8,128)(2,1)S(1)} %get-tuple-element.43), channel_id=1, source_target_pairs={{0,2},{1,3},{2,0},{3,1},{4,6},{5,7},{6,4},{7,5},{8,10},{9,11},{10,... | collective-permute-start | bytes 1376264 | tf_op jit(solution)/shard_map/Y5/ppermute | solution.py:20
  69.7 11.5 %collective-permute-start.17 = (bf16[896,256]{1,0:T(8,128)(2,1)S(1)}, bf16[896,256]{1,0:T(8,128)(2,1)S(1)}, u32[]{:S(2)}, u32[]{:S(2)}) collective-permute-start(bf16[896,256]{1,0:T(8,128)(2,1)S(1)} %copy-done.24), channel_id=1, source_target_pairs={{0,1},{1,0},{2,3},{3,2},{4,5},{5,4},{6,7},{7,6},{8,9},{9,8},{10,11... | collective-permute-start | bytes 1376264 | tf_op jit(solution)/shard_map/C3/ppermute | solution.py:20
  69.7 12.7 %collective-permute-start.14 = (bf16[896,256]{1,0:T(8,128)(2,1)S(1)}, bf16[896,256]{1,0:T(8,128)(2,1)S(1)}, u32[]{:S(2)}, u32[]{:S(2)}) collective-permute-start(bf16[896,256]{1,0:T(8,128)(2,1)S(1)} %copy-done.26), channel_id=1, source_target_pairs={{0,1},{1,0},{2,3},{3,2},{4,5},{5,4},{6,7},{7,6},{8,9},{9,8},{10,11... | collective-permute-start | bytes 1376264 | tf_op jit(solution)/shard_map/C2/ppermute | solution.py:20
  70.2 12.2 %collective-permute-start.22 = (bf16[128,1792]{1,0:T(8,128)(2,1)S(1)}, bf16[128,1792]{1,0:T(8,128)(2,1)S(1)}, u32[]{:S(2)}, u32[]{:S(2)}) collective-permute-start(bf16[128,1792]{1,0:T(8,128)(2,1)S(1)} %collective-permute-done.20.refs_22_.refs_2_), channel_id=1, source_target_pairs={{0,1},{1,0},{2,3},{3,2},{4,5},{5,4},{6,7},{7,6},{8,9},{9,8},{10,11... | collective-permute-start | bytes 1376264 | tf_op jit(solution)/shard_map/C4/ppermute | solution.py:20
  79.8 2.6 %collective-permute-start.18 = (bf16[896,256]{1,0:T(8,128)(2,1)S(1)}, bf16[896,256]{1,0:T(8,128)(2,1)S(1)}, u32[]{:S(2)}, u32[]{:S(2)}) collective-permute-start(bf16[896,256]{1,0:T(8,128)(2,1)S(1)} %collective-permute-done.16.refs_17_), channel_id=1, source_target_pairs={{0,1},{1,0},{2,3},{3,2},{4,5},{5,4},{6,7},{7,6},{8,9},{9,8},{10,11... | collective-permute-start | bytes 1376264 | tf_op jit(solution)/shard_map/C3/ppermute | solution.py:20
  81.2 2.1 %collective-permute-start.23 = (bf16[128,1792]{1,0:T(8,128)(2,1)S(1)}, bf16[128,1792]{1,0:T(8,128)(2,1)S(1)}, u32[]{:S(2)}, u32[]{:S(2)}) collective-permute-start(bf16[128,1792]{1,0:T(8,128)(2,1)S(1)} %collective-permute-done.21.refs_23_.refs_3_), channel_id=1, source_target_pairs={{0,1},{1,0},{2,3},{3,2},{4,5},{5,4},{6,7},{7,6},{8,9},{9,8},{10,11... | collective-permute-start | bytes 1376264 | tf_op jit(solution)/shard_map/C4/ppermute | solution.py:20
  81.2 14.8 %collective-permute-start.25 = (bf16[128,1792]{1,0:T(8,128)(2,1)S(1)}, bf16[128,1792]{1,0:T(8,128)(2,1)}, u32[]{:S(2)}, u32[]{:S(2)}) collective-permute-start(bf16[128,1792]{1,0:T(8,128)(2,1)S(1)} %collective-permute-done.24.refs_2_), channel_id=1, source_target_pairs={{0,16},{16,0},{1,17},{17,1},{2,18},{18,2},{3,19},{19,3},{4,20},{20... | collective-permute-start | bytes 1376264 | tf_op jit(solution)/shard_map/X5/ppermute | solution.py:26
  84.0 14.5 %copy-start.1 = (bf16[256,3584]{1,0:T(8,128)(2,1)S(1)}, bf16[256,3584]{1,0:T(8,128)(2,1)}, u32[]{:S(2)}) copy-start(bf16[256,3584]{1,0:T(8,128)(2,1)} %refs_0_.5) | copy-start | bytes 5505028
  96.0 2.1 %collective-permute-start.27 = (bf16[128,1792]{1,0:T(8,128)(2,1)}, bf16[128,1792]{1,0:T(8,128)(2,1)S(1)}, u32[]{:S(2)}, u32[]{:S(2)}) collective-permute-start(bf16[128,1792]{1,0:T(8,128)(2,1)} %collective-permute-done.25.refs_3_), channel_id=1, source_target_pairs={{0,1},{1,0},{2,3},{3,2},{4,5},{5,4},{6,7},{7,6},{8,9},{9,8},{10,11... | collective-permute-start | bytes 1376264 | tf_op jit(solution)/shard_map/C5/ppermute | solution.py:20
  96.2 2.3 %collective-permute-start.26 = (bf16[128,1792]{1,0:T(8,128)(2,1)S(1)}, bf16[128,1792]{1,0:T(8,128)(2,1)S(1)}, u32[]{:S(2)}, u32[]{:S(2)}) collective-permute-start(bf16[128,1792]{1,0:T(8,128)(2,1)S(1)} %collective-permute-done.24.refs_2_), channel_id=1, source_target_pairs={{0,1},{1,0},{2,3},{3,2},{4,5},{5,4},{6,7},{7,6},{8,9},{9,8},{10,11... | collective-permute-start | bytes 1376264 | tf_op jit(solution)/shard_map/C5/ppermute | solution.py:20
  96.6 12.4 %collective-permute-start.33 = (bf16[96,1792]{1,0:T(8,128)(2,1)}, bf16[96,1792]{1,0:T(8,128)(2,1)S(1)}, u32[]{:S(2)}, u32[]{:S(2)}) collective-permute-start(bf16[96,1792]{1,0:T(8,128)(2,1)} %get-tuple-element.53), channel_id=1, source_target_pairs={{8,0},{9,1},{10,2},{11,3},{0,4},{1,5},{2,6},{3,7},{12,8},{13,9},{1... | collective-permute-start | bytes 1032200 | tf_op jit(solution)/shard_map/mixed_back0/ppermute | solution.py:340
  103.6 11.3 %collective-permute-start.29 = (bf16[96,1792]{1,0:T(8,128)(2,1)}, bf16[96,1792]{1,0:T(8,128)(2,1)S(1)}, u32[]{:S(2)}, u32[]{:S(2)}) collective-permute-start(bf16[96,1792]{1,0:T(8,128)(2,1)} %get-tuple-element.49), channel_id=1, source_target_pairs={{8,0},{9,1},{10,2},{11,3},{0,4},{1,5},{2,6},{3,7},{12,8},{13,9},{1... | collective-permute-start | bytes 1032200 | tf_op jit(solution)/shard_map/mixed_back1/ppermute | solution.py:340
  107.2 26.0 %copy-start.2 = (bf16[128,3584]{1,0:T(8,128)(2,1)S(1)}, bf16[128,3584]{1,0:T(8,128)(2,1)}, u32[]{:S(2)}) copy-start(bf16[128,3584]{1,0:T(8,128)(2,1)} %refs_5_.3) | copy-start | bytes 2752516
  107.2 26.0 %copy-start.14 = (f32[128,128]{1,0:T(8,128)S(1)}, f32[128,128]{1,0:T(8,128)}, u32[]{:S(2)}) copy-start(f32[128,128]{1,0:T(8,128)} %get-tuple-element.31.table) | copy-start | bytes 196612
  107.2 19.7 %collective-permute-start.32 = (bf16[96,1792]{1,0:T(8,128)(2,1)}, bf16[96,1792]{1,0:T(8,128)(2,1)S(1)}, u32[]{:S(2)}, u32[]{:S(2)}) collective-permute-start(bf16[96,1792]{1,0:T(8,128)(2,1)} %get-tuple-element.52), channel_id=1, source_target_pairs={{0,4},{1,5},{2,6},{3,7},{4,0},{5,1},{6,2},{7,3},{8,12},{9,13},{10,... | collective-permute-start | bytes 1032200 | tf_op jit(solution)/shard_map/near_back0/ppermute | solution.py:340
  109.5 23.7 %collective-permute-start.35 = (bf16[128,1792]{1,0:T(8,128)(2,1)S(1)}, bf16[128,1792]{1,0:T(8,128)(2,1)S(1)}, u32[]{:S(2)}, u32[]{:S(2)}) collective-permute-start(bf16[128,1792]{1,0:T(8,128)(2,1)S(1)} %shard_map.78), channel_id=1, source_target_pairs={{4,8},{5,9},{6,10},{7,11},{8,4},{9,5},{10,6},{11,7},{20,24},{21,25... | collective-permute-start | bytes 1376264 | tf_op jit(solution)/shard_map/sum_back0/ppermute | solution.py:340
  115.5 34.2 %collective-permute-start.31 = (bf16[128,1792]{1,0:T(8,128)(2,1)S(1)}, bf16[128,1792]{1,0:T(8,128)(2,1)S(1)}, u32[]{:S(2)}, u32[]{:S(2)}) collective-permute-start(bf16[128,1792]{1,0:T(8,128)(2,1)S(1)} %shard_map.76), channel_id=1, source_target_pairs={{4,8},{5,9},{6,10},{7,11},{8,4},{9,5},{10,6},{11,7},{20,24},{21,25... | collective-permute-start | bytes 1376264 | tf_op jit(solution)/shard_map/sum_back1/ppermute | solution.py:340
  118.6 9.1 %collective-permute-start.34 = (bf16[96,1792]{1,0:T(8,128)(2,1)S(1)}, bf16[96,1792]{1,0:T(8,128)(2,1)S(1)}, u32[]{:S(2)}, u32[]{:S(2)}) collective-permute-start(bf16[96,1792]{1,0:T(8,128)(2,1)S(1)} %copy-done.13), channel_id=1, source_target_pairs={{0,12},{1,13},{2,14},{3,15},{12,0},{13,1},{14,2},{15,3},{16,28},{1... | collective-permute-start | bytes 1032200 | tf_op jit(solution)/shard_map/far_back0/ppermute | solution.py:340
  119.3 24.5 %collective-permute-start.28 = (bf16[96,1792]{1,0:T(8,128)(2,1)S(1)}, bf16[96,1792]{1,0:T(8,128)(2,1)S(1)}, u32[]{:S(2)}, u32[]{:S(2)}) collective-permute-start(bf16[96,1792]{1,0:T(8,128)(2,1)S(1)} %copy-done.16), channel_id=1, source_target_pairs={{0,4},{1,5},{2,6},{3,7},{4,0},{5,1},{6,2},{7,3},{8,12},{9,13},{10,... | collective-permute-start | bytes 1032200 | tf_op jit(solution)/shard_map/near_back1/ppermute | solution.py:340
  127.0 16.8 %collective-permute-start.30 = (bf16[96,1792]{1,0:T(8,128)(2,1)S(1)}, bf16[96,1792]{1,0:T(8,128)(2,1)S(1)}, u32[]{:S(2)}, u32[]{:S(2)}) collective-permute-start(bf16[96,1792]{1,0:T(8,128)(2,1)S(1)} %get-tuple-element.50.refs_1_), channel_id=1, source_target_pairs={{0,12},{1,13},{2,14},{3,15},{12,0},{13,1},{14,2},{15,3},{16,28},{1... | collective-permute-start | bytes 1032200 | tf_op jit(solution)/shard_map/far_back1/ppermute | solution.py:340
  (22 other events, 99.7 us)

commit v5 on v4

--- a/solution.py
+++ b/solution.py
@@ -374,7 +374,7 @@
     Y, X = [], []
     rows = None
     for n, (sent, distance, gate_up, chunk) in enumerate(jobs):
-        Y.append(named(f"Y{n}", flipped, after(sent, *Y[-1:], *(X[-2] if n > 1 else [])), distance))
+        Y.append(named(f"Y{n}", flipped, after(sent, *Y[-1:], *(X[-3] if n > 2 else [])), distance))
         if n == 0:
             packed = after(packed, Y[0], hub_table)
             rows = lax.all_to_all(packed, "expert", 0, 0, axis_index_groups=lines, tiled=True)

time: 152 us -> 152 us (level)
  waiting for transfers between devices: 80.7 us -> 83.7 us
  starting transfers between devices: 36.7 us -> 34 us
    ppermute x6, waiting for transfers between devices: 12.9 us -> 37 us  [turned(): return lax.ppermute(value, 'groups', pairs)]
    ppermute x21, waiting for transfers between devices: 35 us -> 14 us  [flipped(): return lax.ppermute(value, 'expert', pairs)]
    ppermute x21, starting transfers between devices: 8.85 us -> 7.13 us  [flipped(): return lax.ppermute(value, 'expert', pairs)]
    ppermute x6, starting transfers between devices: 8.82 us -> 7.29 us  [turned(): return lax.ppermute(value, 'groups', pairs)]
    unnamed x66 -> x64, local copies, waits for them, and re-layouts: 3.64 us -> 2.94 us
  transfers between devices with their start and end apart: 37 -> 37, of which waited for: 19 -> 20; matrix products, arithmetic and copies ran while one was open for 1% -> 1% of each run, Pallas kernels for 17% -> 17%
where the time goes in v5:
time: 152 us; the launch traced here: 151 us
  waiting for transfers between devices  83.7 us (55%)
  starting transfers between devices  34 us (22%)
  Pallas kernels  27.6 us (18%)
  local copies, waits for them, and re-layouts  5.44 us (4%)
    ppermute x6, waiting for transfers between devices, turned(): return lax.ppermute(value, 'groups', pairs)  37 us
    ppermute x9, waiting for transfers between devices, along(): return lax.ppermute(value, 'expert', pairs)  32.7 us
    ppermute x9, starting transfers between devices, along(): return lax.ppermute(value, 'expert', pairs)  14.3 us
    ppermute x21, waiting for transfers between devices, flipped(): return lax.ppermute(value, 'expert', pairs)  14 us
    pallas_call x1, Pallas kernels, expert_first(): pl.pallas_call(functools.partial(expert_kernel, plan), out_shape=[jax.Sha...  11.9 us
    ppermute x6, starting transfers between devices, turned(): return lax.ppermute(value, 'groups', pairs)  7.29 us
    ppermute x21, starting transfers between devices, flipped(): return lax.ppermute(value, 'expert', pairs)  7.13 us
    pallas_call x2, Pallas kernels, expert_later(): pl.pallas_call(functools.partial(down_kernel, (hidden, groups, copies)),...  6.85 us
  transfers between devices with their start and end apart: 37, of which 20 were waited for; matrix products, arithmetic and copies ran while one was open for 1% of the time, Pallas kernels for 17%

profile of v5, /device:TPU:16, one launch (start us, length us, event | category | flops | bytes accessed | tf_op | source)
XLA Modules:
  0.0 151.3 jit_solution(6656558015616289491)
XLA Ops:
  0.0 1.2 constant_dynamic-slice_fusion.3
  1.2 1.6 %collective-permute-start = (bf16[896,256]{1,0:T(8,128)(2,1)S(1)}, bf16[896,256]{1,0:T(8,128)(2,1)S(1)}, u32[]{:S(2)}, u32[]{:S(2)}) collective-permute-start(bf16[896,256]{1,0:T(8,128)(2,1)S(1)} %get-tuple-element.60), channel_id=1, source_target_pairs={{0,2},{1,3},{2,0},{3,1},{4,6},{5,7},{6,4},{7,5},{8,10},{9,11},{10,... | collective-permute-start | bytes 1376264 | tf_op jit(solution)/shard_map/Y0/ppermute | solution.py:20
  2.8 3.9 %shard_map.73 = (f32[128,128]{1,0:T(8,128)}, bf16[384,3584]{1,0:T(8,128)(2,1)}) custom-call(s32[1]{0:T(128)} %bitcast.1.station, bf16[128,3584]{1,0:T(8,128)(2,1)} %refs_5_.3, f32[3584]{0:T(1024)} %gain.1, bf16[4,3584]{1,0:T(4,128)(2,1)} %bitcast.8, s32[2,128]{1,0:T(2,128)} %bitcast.9), custom_call_target="tpu_custom_call" | custom-call | tf_op jit(solution)/shard_map/pallas_call | solution.py:84
  6.8 2.3 %collective-permute-start.1 = (f32[128,128]{1,0:T(8,128)}, f32[128,128]{1,0:T(8,128)S(1)}, u32[]{:S(2)}, u32[]{:S(2)}) collective-permute-start(f32[128,128]{1,0:T(8,128)} %get-tuple-element.31.table), channel_id=1, source_target_pairs={{4,8},{5,9},{6,10},{7,11},{8,4},{9,5},{10,6},{11,7},{20,24},{21,25... | collective-permute-start | bytes 196616 | tf_op jit(solution)/shard_map/table/ppermute | solution.py:340
  9.1 4.0 %collective-permute-done.1.table = f32[128,128]{1,0:T(8,128)S(1)} collective-permute-done((f32[128,128]{1,0:T(8,128)}, f32[128,128]{1,0:T(8,128)S(1)}, u32[]{:S(2)}, u32[]{:S(2)}) %collective-permute-start.1) | collective-permute-done | bytes 65568 | tf_op jit(solution)/shard_map/table/ppermute | solution.py:340
  13.5 5.2 %all-to-all-start = ((bf16[4,96,3584]{2,1,0:T(8,128)(2,1)}), bf16[4,96,3584]{2,1,0:T(8,128)(2,1)}, u32[]{:S(2)}, u32[]{:S(2)}) async-start(bf16[4,96,3584]{2,1,0:T(8,128)(2,1)} %bitcast.7), calls=%async_computation | async-start | bytes 5505024 | tf_op jit(solution)/shard_map/all_to_all | solution.py:380
  18.8 1.5 %collective-permute-start.7 = (bf16[896,256]{1,0:T(8,128)(2,1)S(1)}, bf16[896,256]{1,0:T(8,128)(2,1)S(1)}, u32[]{:S(2)}, u32[]{:S(2)}) collective-permute-start(bf16[896,256]{1,0:T(8,128)(2,1)S(1)} %get-tuple-element.34), channel_id=1, source_target_pairs={{0,2},{1,3},{2,0},{3,1},{4,6},{5,7},{6,4},{7,5},{8,10},{9,11},{10,... | collective-permute-start | bytes 1376264 | tf_op jit(solution)/shard_map/Y1/ppermute | solution.py:20
  20.3 1.5 collective-permute-start.4
  21.8 1.2 constant_dynamic-slice_fusion.1
  23.0 6.7 %collective-permute-done.7.refs_8_ = bf16[896,256]{1,0:T(8,128)(2,1)S(1)} collective-permute-done((bf16[896,256]{1,0:T(8,128)(2,1)S(1)}, bf16[896,256]{1,0:T(8,128)(2,1)S(1)}, u32[]{:S(2)}, u32[]{:S(2)}) %collective-permute-start.7) | collective-permute-done | bytes 458784 | tf_op jit(solution)/shard_map/Y1/ppermute | solution.py:20
  29.6 1.3 collective-permute-done.4.refs_5_
  31.0 1.5 collective-permute-start.8
  32.9 7.8 %collective-permute-done.8.refs_9_ = bf16[896,256]{1,0:T(8,128)(2,1)S(1)} collective-permute-done((bf16[896,256]{1,0:T(8,128)(2,1)S(1)}, bf16[896,256]{1,0:T(8,128)(2,1)S(1)}, u32[]{:S(2)}, u32[]{:S(2)}) %collective-permute-start.8) | collective-permute-done | bytes 458784 | tf_op jit(solution)/shard_map/X1/ppermute | solution.py:26
  40.8 1.7 %collective-permute-done.11.refs_12_ = bf16[896,256]{1,0:T(8,128)(2,1)S(1)} collective-permute-done((bf16[896,256]{1,0:T(8,128)(2,1)S(1)}, bf16[896,256]{1,0:T(8,128)(2,1)S(1)}, u32[]{:S(2)}, u32[]{:S(2)}) %collective-permute-start.11) | collective-permute-done | bytes 458784 | tf_op jit(solution)/shard_map/Y2/ppermute | solution.py:20
  44.1 6.9 %collective-permute-done.12.refs_13_ = bf16[896,256]{1,0:T(8,128)(2,1)S(1)} collective-permute-done((bf16[896,256]{1,0:T(8,128)(2,1)S(1)}, bf16[896,256]{1,0:T(8,128)(2,1)S(1)}, u32[]{:S(2)}, u32[]{:S(2)}) %collective-permute-start.12) | collective-permute-done | bytes 458784 | tf_op jit(solution)/shard_map/X2/ppermute | solution.py:26
  51.0 0.7 collective-permute-done.15.refs_16_
  51.9 1.5 collective-permute-start.16
  53.4 0.6 collective-permute-start.20
  54.0 11.1 %collective-permute-done.16.refs_17_ = bf16[896,256]{1,0:T(8,128)(2,1)S(1)} collective-permute-done((bf16[896,256]{1,0:T(8,128)(2,1)}, bf16[896,256]{1,0:T(8,128)(2,1)S(1)}, u32[]{:S(2)}, u32[]{:S(2)}) %collective-permute-start.16) | collective-permute-done | bytes 458784 | tf_op jit(solution)/shard_map/X3/ppermute | solution.py:26
  65.1 0.9 collective-permute-done.20.refs_22_.refs_2_
  66.0 0.9 collective-permute-done.10.refs_11_
  66.9 1.4 collective-permute-start.21
  68.3 0.7 collective-permute-start.24
  69.6 9.9 %collective-permute-done.21.refs_23_.refs_3_ = bf16[128,1792]{1,0:T(8,128)(2,1)S(1)} collective-permute-done((bf16[128,1792]{1,0:T(8,128)(2,1)S(1)}, bf16[128,1792]{1,0:T(8,128)(2,1)S(1)}, u32[]{:S(2)}, u32[]{:S(2)}) %collective-permute-start.21) | collective-permute-done | bytes 458784 | tf_op jit(solution)/shard_map/X4/ppermute | solution.py:26
  79.5 1.2 collective-permute-done.24.refs_2_
  80.7 0.9 collective-permute-start.25
  81.7 0.8 copy-done.31
  82.5 0.7 copy-done.9
  83.4 11.9 %shard_map.74 = (bf16[384,1024]{1,0:T(8,128)(2,1)}, bf16[96,1792]{1,0:T(8,128)(2,1)}, bf16[96,1792]{1,0:T(8,128)(2,1)}) custom-call(s32[1]{0:T(128)} %bitcast.4.group, s32[1]{0:T(128)} %bitcast.1.station, bf16[384,3584]{1,0:T(8,128)(2,1)} %bitcast.6.rows, bf16[3584,256]{1,0:T(8,128)(2,1)} %refs_0_.3, bf16[3584,256]{1,0:T(8,128)(2,1)} %refs_1_.1, ...), custom_call_target="tpu_custom_call" | custom-call | tf_op jit(solution)/shard_map/pallas_call | solution.py:178
  96.4 1.0 collective-permute-done.27.refs_5_
  97.9 1.1 copy-done.3
  99.0 3.9 %shard_map.75 = (bf16[96,1792]{1,0:T(8,128)(2,1)S(1)}, bf16[96,1792]{1,0:T(8,128)(2,1)S(1)}, bf16[96,1792]{1,0:T(8,128)(2,1)}, bf16[96,1792]{1,0:T(8,128)(2,1)S(1)}) custom-call(s32[1]{0:T(128)} %bitcast.4.group, bf16[384,1024]{1,0:T(8,128)(2,1)S(1)} %copy-done.3, bf16[256,3584]{1,0:T(8,128)(2,1)S(1)} %copy-done.1, ...), custom_call_target="tpu_custom_call" | custom-call | tf_op jit(solution)/shard_map/pallas_call | solution.py:213
  103.0 0.7 collective-permute-start.29
  103.8 2.9 %shard_map.77 = (bf16[96,1792]{1,0:T(8,128)(2,1)S(1)}, bf16[96,1792]{1,0:T(8,128)(2,1)}) custom-call(s32[1]{0:T(128)} %bitcast.4.group, bf16[384,1024]{1,0:T(8,128)(2,1)S(1)} %copy-done.4, bf16[256,3584]{1,0:T(8,128)(2,1)S(1)} %copy-done.1, bf16[256,3584]{1,0:T(8,128)(2,1)} %collective-permute-done.19.refs_21_.refs_1_, bf16[128,1792]{1,0:T(8,128)(2,1)S(1)} %copy-done.6, ...), custom_call_target="tpu_custom_call" | custom-call | tf_op jit(solution)/shard_map/pallas_call | solution.py:213
  106.7 1.6 %collective-permute-start.32 = (bf16[96,1792]{1,0:T(8,128)(2,1)}, bf16[96,1792]{1,0:T(8,128)(2,1)S(1)}, u32[]{:S(2)}, u32[]{:S(2)}) collective-permute-start(bf16[96,1792]{1,0:T(8,128)(2,1)} %get-tuple-element.52), channel_id=1, source_target_pairs={{0,4},{1,5},{2,6},{3,7},{4,0},{5,1},{6,2},{7,3},{8,12},{9,13},{10,... | collective-permute-start | bytes 1032200 | tf_op jit(solution)/shard_map/near_back0/ppermute | solution.py:340
  108.3 0.5 shard_map.78
  108.9 3.1 %collective-permute-start.35 = (bf16[128,1792]{1,0:T(8,128)(2,1)S(1)}, bf16[128,1792]{1,0:T(8,128)(2,1)S(1)}, u32[]{:S(2)}, u32[]{:S(2)}) collective-permute-start(bf16[128,1792]{1,0:T(8,128)(2,1)S(1)} %shard_map.78), channel_id=1, source_target_pairs={{4,8},{5,9},{6,10},{7,11},{8,4},{9,5},{10,6},{11,7},{20,24},{21,25... | collective-permute-start | bytes 1376264 | tf_op jit(solution)/shard_map/sum_back0/ppermute | solution.py:340
  112.0 2.3 %collective-permute-done.29.refs_0_.refs_2_ = bf16[96,1792]{1,0:T(8,128)(2,1)S(1)} collective-permute-done((bf16[96,1792]{1,0:T(8,128)(2,1)}, bf16[96,1792]{1,0:T(8,128)(2,1)S(1)}, u32[]{:S(2)}, u32[]{:S(2)}) %collective-permute-start.29) | collective-permute-done | bytes 344096 | tf_op jit(solution)/shard_map/mixed_back1/ppermute | solution.py:340
  114.9 3.2 %collective-permute-start.31 = (bf16[128,1792]{1,0:T(8,128)(2,1)S(1)}, bf16[128,1792]{1,0:T(8,128)(2,1)S(1)}, u32[]{:S(2)}, u32[]{:S(2)}) collective-permute-start(bf16[128,1792]{1,0:T(8,128)(2,1)S(1)} %shard_map.76), channel_id=1, source_target_pairs={{4,8},{5,9},{6,10},{7,11},{8,4},{9,5},{10,6},{11,7},{20,24},{21,25... | collective-permute-start | bytes 1376264 | tf_op jit(solution)/shard_map/sum_back1/ppermute | solution.py:340
  118.1 0.7 collective-permute-start.34
  118.8 1.5 collective-permute-start.28
  120.2 6.3 %collective-permute-done.32.refs_1_ = bf16[96,1792]{1,0:T(8,128)(2,1)S(1)} collective-permute-done((bf16[96,1792]{1,0:T(8,128)(2,1)}, bf16[96,1792]{1,0:T(8,128)(2,1)S(1)}, u32[]{:S(2)}, u32[]{:S(2)}) %collective-permute-start.32) | collective-permute-done | bytes 344096 | tf_op jit(solution)/shard_map/near_back0/ppermute | solution.py:340
  126.5 0.7 collective-permute-start.30
  127.2 5.5 %collective-permute-done.35.refs_4_ = bf16[128,1792]{1,0:T(8,128)(2,1)S(1)} collective-permute-done((bf16[128,1792]{1,0:T(8,128)(2,1)S(1)}, bf16[128,1792]{1,0:T(8,128)(2,1)S(1)}, u32[]{:S(2)}, u32[]{:S(2)}) %collective-permute-start.35) | collective-permute-done | bytes 458784 | tf_op jit(solution)/shard_map/sum_back0/ppermute | solution.py:340
  132.7 1.9 %shard_map.79.refs_6_ = bf16[128,3584]{1,0:T(8,128)(2,1)} custom-call(s32[1]{0:T(128)} %bitcast.is_hub, f32[128,128]{1,0:T(8,128)S(1)} %copy-done.14, bf16[96,1792]{1,0:T(8,128)(2,1)S(1)} %get-tuple-element.51.refs_0_, bf16[96,1792]{1,0:T(8,128)(2,1)S(1)} %collective-permute-done.32.refs_1_, bf16[96,1792]{1,0:T(8,128)(2,1)S(1)} %collective-permute-done.33.refs_0_.refs_2_, ...), custom_call_target="tpu_custom_call" | custom-call | tf_op jit(solution)/shard_map/pallas_call | solution.py:295
  134.7 8.6 %collective-permute-done.28.refs_1_ = bf16[96,1792]{1,0:T(8,128)(2,1)S(1)} collective-permute-done((bf16[96,1792]{1,0:T(8,128)(2,1)S(1)}, bf16[96,1792]{1,0:T(8,128)(2,1)S(1)}, u32[]{:S(2)}, u32[]{:S(2)}) %collective-permute-start.28) | collective-permute-done | bytes 344096 | tf_op jit(solution)/shard_map/near_back1/ppermute | solution.py:340
  143.3 5.9 %collective-permute-done.31.refs_4_ = bf16[128,1792]{1,0:T(8,128)(2,1)S(1)} collective-permute-done((bf16[128,1792]{1,0:T(8,128)(2,1)S(1)}, bf16[128,1792]{1,0:T(8,128)(2,1)S(1)}, u32[]{:S(2)}, u32[]{:S(2)}) %collective-permute-start.31) | collective-permute-done | bytes 458784 | tf_op jit(solution)/shard_map/sum_back1/ppermute | solution.py:340
  149.2 1.9 %shard_map.80 = bf16[128,3584]{1,0:T(8,128)(2,1)} custom-call(s32[1]{0:T(128)} %bitcast.is_hub, f32[128,128]{1,0:T(8,128)S(1)} %copy-done.14, bf16[96,1792]{1,0:T(8,128)(2,1)S(1)} %get-tuple-element.47.refs_0_, bf16[96,1792]{1,0:T(8,128)(2,1)S(1)} %collective-permute-done.28.refs_1_, ...), custom_call_target="tpu_custom_call", output_to_operand_aliasing={{}: (8, {})} | custom-call | tf_op jit(solution)/shard_map/pallas_call | solution.py:295
  (101 shorter events, 5.7 us)
Async XLA Ops:
  1.2 12.3 %collective-permute-start = (bf16[896,256]{1,0:T(8,128)(2,1)S(1)}, bf16[896,256]{1,0:T(8,128)(2,1)S(1)}, u32[]{:S(2)}, u32[]{:S(2)}) collective-permute-start(bf16[896,256]{1,0:T(8,128)(2,1)S(1)} %get-tuple-element.60), channel_id=1, source_target_pairs={{0,2},{1,3},{2,0},{3,1},{4,6},{5,7},{6,4},{7,5},{8,10},{9,11},{10,... | collective-permute-start | bytes 1376264 | tf_op jit(solution)/shard_map/Y0/ppermute | solution.py:20
  6.8 6.4 %collective-permute-start.1 = (f32[128,128]{1,0:T(8,128)}, f32[128,128]{1,0:T(8,128)S(1)}, u32[]{:S(2)}, u32[]{:S(2)}) collective-permute-start(f32[128,128]{1,0:T(8,128)} %get-tuple-element.31.table), channel_id=1, source_target_pairs={{4,8},{5,9},{6,10},{7,11},{8,4},{9,5},{10,6},{11,7},{20,24},{21,25... | collective-permute-start | bytes 196616 | tf_op jit(solution)/shard_map/table/ppermute | solution.py:340
  13.5 19.4 %copy-start.17 = (bf16[896,256]{1,0:T(8,128)(2,1)}, bf16[896,256]{1,0:T(8,128)(2,1)S(1)}, u32[]{:S(2)}) copy-start(bf16[896,256]{1,0:T(8,128)(2,1)S(1)} %collective-permute-done.refs_4_) | copy-start | bytes 1376260
  13.5 68.9 %all-to-all-start = ((bf16[4,96,3584]{2,1,0:T(8,128)(2,1)}), bf16[4,96,3584]{2,1,0:T(8,128)(2,1)}, u32[]{:S(2)}, u32[]{:S(2)}) async-start(bf16[4,96,3584]{2,1,0:T(8,128)(2,1)} %bitcast.7), calls=%async_computation | async-start | bytes 5505024 | tf_op jit(solution)/shard_map/all_to_all | solution.py:380
  18.8 24.8 %copy-start = (bf16[256,3584]{1,0:T(8,128)(2,1)S(1)}, bf16[256,3584]{1,0:T(8,128)(2,1)}, u32[]{:S(2)}) copy-start(bf16[256,3584]{1,0:T(8,128)(2,1)} %refs_0_.5) | copy-start | bytes 5505028
  18.8 10.9 %collective-permute-start.7 = (bf16[896,256]{1,0:T(8,128)(2,1)S(1)}, bf16[896,256]{1,0:T(8,128)(2,1)S(1)}, u32[]{:S(2)}, u32[]{:S(2)}) collective-permute-start(bf16[896,256]{1,0:T(8,128)(2,1)S(1)} %get-tuple-element.34), channel_id=1, source_target_pairs={{0,2},{1,3},{2,0},{3,1},{4,6},{5,7},{6,4},{7,5},{8,10},{9,11},{10,... | collective-permute-start | bytes 1376264 | tf_op jit(solution)/shard_map/Y1/ppermute | solution.py:20
  20.3 10.7 %collective-permute-start.4 = (bf16[896,256]{1,0:T(8,128)(2,1)S(1)}, bf16[896,256]{1,0:T(8,128)(2,1)}, u32[]{:S(2)}, u32[]{:S(2)}) collective-permute-start(bf16[896,256]{1,0:T(8,128)(2,1)S(1)} %collective-permute-done.refs_4_), channel_id=1, source_target_pairs={{0,16},{16,0},{1,17},{17,1},{2,18},{18,2},{3,19},{19,3},{4,20},{20... | collective-permute-start | bytes 1376264 | tf_op jit(solution)/shard_map/X0/ppermute | solution.py:26
  29.6 36.4 %copy-start.18 = (bf16[896,256]{1,0:T(8,128)(2,1)}, bf16[896,256]{1,0:T(8,128)(2,1)S(1)}, u32[]{:S(2)}) copy-start(bf16[896,256]{1,0:T(8,128)(2,1)S(1)} %collective-permute-done.7.refs_8_) | copy-start | bytes 1376260
  31.0 9.8 %collective-permute-start.8 = (bf16[896,256]{1,0:T(8,128)(2,1)S(1)}, bf16[896,256]{1,0:T(8,128)(2,1)S(1)}, u32[]{:S(2)}, u32[]{:S(2)}) collective-permute-start(bf16[896,256]{1,0:T(8,128)(2,1)S(1)} %collective-permute-done.7.refs_8_), channel_id=1, source_target_pairs={{0,16},{16,0},{1,17},{17,1},{2,18},{18,2},{3,19},{19,3},{4,20},{20... | collective-permute-start | bytes 1376264 | tf_op jit(solution)/shard_map/X1/ppermute | solution.py:26
  32.4 10.0 %collective-permute-start.11 = (bf16[896,256]{1,0:T(8,128)(2,1)S(1)}, bf16[896,256]{1,0:T(8,128)(2,1)S(1)}, u32[]{:S(2)}, u32[]{:S(2)}) collective-permute-start(bf16[896,256]{1,0:T(8,128)(2,1)S(1)} %get-tuple-element.36), channel_id=1, source_target_pairs={{0,2},{1,3},{2,0},{3,1},{4,6},{5,7},{6,4},{7,5},{8,10},{9,11},{10,... | collective-permute-start | bytes 1376264 | tf_op jit(solution)/shard_map/Y2/ppermute | solution.py:20
  32.9 11.1 %collective-permute-start.5 = (bf16[896,256]{1,0:T(8,128)(2,1)S(1)}, bf16[896,256]{1,0:T(8,128)(2,1)S(1)}, u32[]{:S(2)}, u32[]{:S(2)}) collective-permute-start(bf16[896,256]{1,0:T(8,128)(2,1)S(1)} %collective-permute-done.refs_4_), channel_id=1, source_target_pairs={{0,1},{1,0},{2,3},{3,2},{4,5},{5,4},{6,7},{7,6},{8,9},{9,8},{10,11... | collective-permute-start | bytes 1376264 | tf_op jit(solution)/shard_map/C0/ppermute | solution.py:20
  40.8 27.5 %copy-start.19 = (bf16[896,256]{1,0:T(8,128)(2,1)}, bf16[896,256]{1,0:T(8,128)(2,1)S(1)}, u32[]{:S(2)}) copy-start(bf16[896,256]{1,0:T(8,128)(2,1)S(1)} %collective-permute-done.8.refs_9_) | copy-start | bytes 1376260
  42.5 8.5 %collective-permute-start.12 = (bf16[896,256]{1,0:T(8,128)(2,1)S(1)}, bf16[896,256]{1,0:T(8,128)(2,1)S(1)}, u32[]{:S(2)}, u32[]{:S(2)}) collective-permute-start(bf16[896,256]{1,0:T(8,128)(2,1)S(1)} %collective-permute-done.11.refs_12_), channel_id=1, source_target_pairs={{0,16},{16,0},{1,17},{17,1},{2,18},{18,2},{3,19},{19,3},{4,20},{20... | collective-permute-start | bytes 1376264 | tf_op jit(solution)/shard_map/X2/ppermute | solution.py:26
  43.0 8.7 %collective-permute-start.15 = (bf16[896,256]{1,0:T(8,128)(2,1)S(1)}, bf16[896,256]{1,0:T(8,128)(2,1)}, u32[]{:S(2)}, u32[]{:S(2)}) collective-permute-start(bf16[896,256]{1,0:T(8,128)(2,1)S(1)} %get-tuple-element.38), channel_id=1, source_target_pairs={{0,2},{1,3},{2,0},{3,1},{4,6},{5,7},{6,4},{7,5},{8,10},{9,11},{10,... | collective-permute-start | bytes 1376264 | tf_op jit(solution)/shard_map/Y3/ppermute | solution.py:20
  43.5 25.5 %collective-permute-start.19 = (bf16[256,3584]{1,0:T(8,128)(2,1)S(1)}, bf16[256,3584]{1,0:T(8,128)(2,1)}, u32[]{:S(2)}, u32[]{:S(2)}) collective-permute-start(bf16[256,3584]{1,0:T(8,128)(2,1)S(1)} %copy-done), channel_id=1, source_target_pairs={{0,1},{1,0},{2,3},{3,2},{4,5},{5,4},{6,7},{7,6},{8,9},{9,8},{10,11... | collective-permute-start | bytes 5505032 | tf_op jit(solution)/shard_map/own/ppermute | solution.py:20
  43.5 25.5 %collective-permute-start.2 = (bf16[3584,256]{1,0:T(8,128)(2,1)}, bf16[3584,256]{1,0:T(8,128)(2,1)}, u32[]{:S(2)}, u32[]{:S(2)}) collective-permute-start(bf16[3584,256]{1,0:T(8,128)(2,1)} %refs_0_.3), channel_id=1, source_target_pairs={{0,1},{1,0},{2,3},{3,2},{4,5},{5,4},{6,7},{7,6},{8,9},{9,8},{10,11... | collective-permute-start | bytes 5505032 | tf_op jit(solution)/shard_map/own/ppermute | solution.py:20
  44.0 7.9 %collective-permute-start.9 = (bf16[896,256]{1,0:T(8,128)(2,1)S(1)}, bf16[896,256]{1,0:T(8,128)(2,1)S(1)}, u32[]{:S(2)}, u32[]{:S(2)}) collective-permute-start(bf16[896,256]{1,0:T(8,128)(2,1)S(1)} %collective-permute-done.7.refs_8_), channel_id=1, source_target_pairs={{0,1},{1,0},{2,3},{3,2},{4,5},{5,4},{6,7},{7,6},{8,9},{9,8},{10,11... | collective-permute-start | bytes 1376264 | tf_op jit(solution)/shard_map/C1/ppermute | solution.py:20
  51.0 2.4 %collective-permute-start.6 = (bf16[896,256]{1,0:T(8,128)(2,1)}, bf16[896,256]{1,0:T(8,128)(2,1)}, u32[]{:S(2)}, u32[]{:S(2)}) collective-permute-start(bf16[896,256]{1,0:T(8,128)(2,1)} %collective-permute-done.4.refs_5_), channel_id=1, source_target_pairs={{0,1},{1,0},{2,3},{3,2},{4,5},{5,4},{6,7},{7,6},{8,9},{9,8},{10,11... | collective-permute-start | bytes 1376264 | tf_op jit(solution)/shard_map/C0/ppermute | solution.py:20
  51.8 17.7 %collective-permute-start.3 = (bf16[3584,256]{1,0:T(8,128)(2,1)}, bf16[3584,256]{1,0:T(8,128)(2,1)}, u32[]{:S(2)}, u32[]{:S(2)}) collective-permute-start(bf16[3584,256]{1,0:T(8,128)(2,1)} %refs_1_.1), channel_id=1, source_target_pairs={{0,1},{1,0},{2,3},{3,2},{4,5},{5,4},{6,7},{7,6},{8,9},{9,8},{10,11... | collective-permute-start | bytes 5505032 | tf_op jit(solution)/shard_map/own/ppermute | solution.py:20
  51.8 17.2 %copy-start.24 = (bf16[896,256]{1,0:T(8,128)(2,1)S(1)}, bf16[896,256]{1,0:T(8,128)(2,1)}, u32[]{:S(2)}) copy-start(bf16[896,256]{1,0:T(8,128)(2,1)} %copy-done.23) | copy-start | bytes 1376260
  51.9 13.2 %collective-permute-start.16 = (bf16[896,256]{1,0:T(8,128)(2,1)}, bf16[896,256]{1,0:T(8,128)(2,1)S(1)}, u32[]{:S(2)}, u32[]{:S(2)}) collective-permute-start(bf16[896,256]{1,0:T(8,128)(2,1)} %collective-permute-done.15.refs_16_), channel_id=1, source_target_pairs={{0,16},{16,0},{1,17},{17,1},{2,18},{18,2},{3,19},{19,3},{4,20},{20... | collective-permute-start | bytes 1376264 | tf_op jit(solution)/shard_map/X3/ppermute | solution.py:26
  53.4 12.6 %collective-permute-start.20 = (bf16[128,1792]{1,0:T(8,128)(2,1)S(1)}, bf16[128,1792]{1,0:T(8,128)(2,1)S(1)}, u32[]{:S(2)}, u32[]{:S(2)}) collective-permute-start(bf16[128,1792]{1,0:T(8,128)(2,1)S(1)} %get-tuple-element.40), channel_id=1, source_target_pairs={{0,2},{1,3},{2,0},{3,1},{4,6},{5,7},{6,4},{7,5},{8,10},{9,11},{10,... | collective-permute-start | bytes 1376264 | tf_op jit(solution)/shard_map/Y4/ppermute | solution.py:20
  65.1 16.5 %copy-start.26 = (bf16[896,256]{1,0:T(8,128)(2,1)}, bf16[896,256]{1,0:T(8,128)(2,1)S(1)}, u32[]{:S(2)}) copy-start(bf16[896,256]{1,0:T(8,128)(2,1)S(1)} %collective-permute-done.16.refs_17_) | copy-start | bytes 1376260
  65.1 1.8 %collective-permute-start.10 = (bf16[896,256]{1,0:T(8,128)(2,1)S(1)}, bf16[896,256]{1,0:T(8,128)(2,1)S(1)}, u32[]{:S(2)}, u32[]{:S(2)}) collective-permute-start(bf16[896,256]{1,0:T(8,128)(2,1)S(1)} %collective-permute-done.8.refs_9_), channel_id=1, source_target_pairs={{0,1},{1,0},{2,3},{3,2},{4,5},{5,4},{6,7},{7,6},{8,9},{9,8},{10,11... | collective-permute-start | bytes 1376264 | tf_op jit(solution)/shard_map/C1/ppermute | solution.py:20
  66.0 16.5 %copy-start.5 = (bf16[128,1792]{1,0:T(8,128)(2,1)}, bf16[128,1792]{1,0:T(8,128)(2,1)S(1)}, u32[]{:S(2)}) copy-start(bf16[128,1792]{1,0:T(8,128)(2,1)S(1)} %collective-permute-done.20.refs_22_.refs_2_) | copy-start | bytes 1376260
  66.0 2.3 %collective-permute-start.13 = (bf16[896,256]{1,0:T(8,128)(2,1)S(1)}, bf16[896,256]{1,0:T(8,128)(2,1)S(1)}, u32[]{:S(2)}, u32[]{:S(2)}) collective-permute-start(bf16[896,256]{1,0:T(8,128)(2,1)S(1)} %copy-done.21), channel_id=1, source_target_pairs={{0,1},{1,0},{2,3},{3,2},{4,5},{5,4},{6,7},{7,6},{8,9},{9,8},{10,11... | collective-permute-start | bytes 1376264 | tf_op jit(solution)/shard_map/C2/ppermute | solution.py:20
  66.9 14.7 %copy-start.27 = (bf16[896,256]{1,0:T(8,128)(2,1)}, bf16[896,256]{1,0:T(8,128)(2,1)S(1)}, u32[]{:S(2)}) copy-start(bf16[896,256]{1,0:T(8,128)(2,1)S(1)} %collective-permute-done.10.refs_11_) | copy-start | bytes 1376260
  66.9 12.6 %collective-permute-start.21 = (bf16[128,1792]{1,0:T(8,128)(2,1)S(1)}, bf16[128,1792]{1,0:T(8,128)(2,1)S(1)}, u32[]{:S(2)}, u32[]{:S(2)}) collective-permute-start(bf16[128,1792]{1,0:T(8,128)(2,1)S(1)} %collective-permute-done.20.refs_22_.refs_2_), channel_id=1, source_target_pairs={{0,16},{16,0},{1,17},{17,1},{2,18},{18,2},{3,19},{19,3},{4,20},{20... | collective-permute-start | bytes 1376264 | tf_op jit(solution)/shard_map/X4/ppermute | solution.py:26
  68.3 12.3 %collective-permute-start.24 = (bf16[128,1792]{1,0:T(8,128)(2,1)S(1)}, bf16[128,1792]{1,0:T(8,128)(2,1)S(1)}, u32[]{:S(2)}, u32[]{:S(2)}) collective-permute-start(bf16[128,1792]{1,0:T(8,128)(2,1)S(1)} %get-tuple-element.43), channel_id=1, source_target_pairs={{0,2},{1,3},{2,0},{3,1},{4,6},{5,7},{6,4},{7,5},{8,10},{9,11},{10,... | collective-permute-start | bytes 1376264 | tf_op jit(solution)/shard_map/Y5/ppermute | solution.py:20
  69.0 11.7 %collective-permute-start.14 = (bf16[896,256]{1,0:T(8,128)(2,1)S(1)}, bf16[896,256]{1,0:T(8,128)(2,1)S(1)}, u32[]{:S(2)}, u32[]{:S(2)}) collective-permute-start(bf16[896,256]{1,0:T(8,128)(2,1)S(1)} %copy-done.24), channel_id=1, source_target_pairs={{0,1},{1,0},{2,3},{3,2},{4,5},{5,4},{6,7},{7,6},{8,9},{9,8},{10,11... | collective-permute-start | bytes 1376264 | tf_op jit(solution)/shard_map/C2/ppermute | solution.py:20
  69.0 12.6 %collective-permute-start.17 = (bf16[896,256]{1,0:T(8,128)(2,1)}, bf16[896,256]{1,0:T(8,128)(2,1)S(1)}, u32[]{:S(2)}, u32[]{:S(2)}) collective-permute-start(bf16[896,256]{1,0:T(8,128)(2,1)} %collective-permute-done.15.refs_16_), channel_id=1, source_target_pairs={{0,1},{1,0},{2,3},{3,2},{4,5},{5,4},{6,7},{7,6},{8,9},{9,8},{10,11... | collective-permute-start | bytes 1376264 | tf_op jit(solution)/shard_map/C3/ppermute | solution.py:20
  69.5 12.1 %collective-permute-start.18 = (bf16[896,256]{1,0:T(8,128)(2,1)S(1)}, bf16[896,256]{1,0:T(8,128)(2,1)S(1)}, u32[]{:S(2)}, u32[]{:S(2)}) collective-permute-start(bf16[896,256]{1,0:T(8,128)(2,1)S(1)} %collective-permute-done.16.refs_17_), channel_id=1, source_target_pairs={{0,1},{1,0},{2,3},{3,2},{4,5},{5,4},{6,7},{7,6},{8,9},{9,8},{10,11... | collective-permute-start | bytes 1376264 | tf_op jit(solution)/shard_map/C3/ppermute | solution.py:20
  79.5 2.1 %collective-permute-start.22 = (bf16[128,1792]{1,0:T(8,128)(2,1)S(1)}, bf16[128,1792]{1,0:T(8,128)(2,1)S(1)}, u32[]{:S(2)}, u32[]{:S(2)}) collective-permute-start(bf16[128,1792]{1,0:T(8,128)(2,1)S(1)} %collective-permute-done.20.refs_22_.refs_2_), channel_id=1, source_target_pairs={{0,1},{1,0},{2,3},{3,2},{4,5},{5,4},{6,7},{7,6},{8,9},{9,8},{10,11... | collective-permute-start | bytes 1376264 | tf_op jit(solution)/shard_map/C4/ppermute | solution.py:20
  80.7 1.8 %collective-permute-start.23 = (bf16[128,1792]{1,0:T(8,128)(2,1)S(1)}, bf16[128,1792]{1,0:T(8,128)(2,1)S(1)}, u32[]{:S(2)}, u32[]{:S(2)}) collective-permute-start(bf16[128,1792]{1,0:T(8,128)(2,1)S(1)} %collective-permute-done.21.refs_23_.refs_3_), channel_id=1, source_target_pairs={{0,1},{1,0},{2,3},{3,2},{4,5},{5,4},{6,7},{7,6},{8,9},{9,8},{10,11... | collective-permute-start | bytes 1376264 | tf_op jit(solution)/shard_map/C4/ppermute | solution.py:20
  80.7 14.7 %collective-permute-start.25 = (bf16[128,1792]{1,0:T(8,128)(2,1)S(1)}, bf16[128,1792]{1,0:T(8,128)(2,1)}, u32[]{:S(2)}, u32[]{:S(2)}) collective-permute-start(bf16[128,1792]{1,0:T(8,128)(2,1)S(1)} %collective-permute-done.24.refs_2_), channel_id=1, source_target_pairs={{0,16},{16,0},{1,17},{17,1},{2,18},{18,2},{3,19},{19,3},{4,20},{20... | collective-permute-start | bytes 1376264 | tf_op jit(solution)/shard_map/X5/ppermute | solution.py:26
  83.4 14.5 %copy-start.1 = (bf16[256,3584]{1,0:T(8,128)(2,1)S(1)}, bf16[256,3584]{1,0:T(8,128)(2,1)}, u32[]{:S(2)}) copy-start(bf16[256,3584]{1,0:T(8,128)(2,1)} %refs_0_.5) | copy-start | bytes 5505028
  95.3 2.1 %collective-permute-start.27 = (bf16[128,1792]{1,0:T(8,128)(2,1)}, bf16[128,1792]{1,0:T(8,128)(2,1)S(1)}, u32[]{:S(2)}, u32[]{:S(2)}) collective-permute-start(bf16[128,1792]{1,0:T(8,128)(2,1)} %collective-permute-done.25.refs_3_), channel_id=1, source_target_pairs={{0,1},{1,0},{2,3},{3,2},{4,5},{5,4},{6,7},{7,6},{8,9},{9,8},{10,11... | collective-permute-start | bytes 1376264 | tf_op jit(solution)/shard_map/C5/ppermute | solution.py:20
  95.6 2.3 %collective-permute-start.26 = (bf16[128,1792]{1,0:T(8,128)(2,1)S(1)}, bf16[128,1792]{1,0:T(8,128)(2,1)S(1)}, u32[]{:S(2)}, u32[]{:S(2)}) collective-permute-start(bf16[128,1792]{1,0:T(8,128)(2,1)S(1)} %collective-permute-done.24.refs_2_), channel_id=1, source_target_pairs={{0,1},{1,0},{2,3},{3,2},{4,5},{5,4},{6,7},{7,6},{8,9},{9,8},{10,11... | collective-permute-start | bytes 1376264 | tf_op jit(solution)/shard_map/C5/ppermute | solution.py:20
  95.9 12.4 %collective-permute-start.33 = (bf16[96,1792]{1,0:T(8,128)(2,1)}, bf16[96,1792]{1,0:T(8,128)(2,1)S(1)}, u32[]{:S(2)}, u32[]{:S(2)}) collective-permute-start(bf16[96,1792]{1,0:T(8,128)(2,1)} %get-tuple-element.53), channel_id=1, source_target_pairs={{8,0},{9,1},{10,2},{11,3},{0,4},{1,5},{2,6},{3,7},{12,8},{13,9},{1... | collective-permute-start | bytes 1032200 | tf_op jit(solution)/shard_map/mixed_back0/ppermute | solution.py:340
  103.0 11.3 %collective-permute-start.29 = (bf16[96,1792]{1,0:T(8,128)(2,1)}, bf16[96,1792]{1,0:T(8,128)(2,1)S(1)}, u32[]{:S(2)}, u32[]{:S(2)}) collective-permute-start(bf16[96,1792]{1,0:T(8,128)(2,1)} %get-tuple-element.49), channel_id=1, source_target_pairs={{8,0},{9,1},{10,2},{11,3},{0,4},{1,5},{2,6},{3,7},{12,8},{13,9},{1... | collective-permute-start | bytes 1032200 | tf_op jit(solution)/shard_map/mixed_back1/ppermute | solution.py:340
  106.7 26.0 %copy-start.2 = (bf16[128,3584]{1,0:T(8,128)(2,1)S(1)}, bf16[128,3584]{1,0:T(8,128)(2,1)}, u32[]{:S(2)}) copy-start(bf16[128,3584]{1,0:T(8,128)(2,1)} %refs_5_.3) | copy-start | bytes 2752516
  106.7 26.0 %copy-start.14 = (f32[128,128]{1,0:T(8,128)S(1)}, f32[128,128]{1,0:T(8,128)}, u32[]{:S(2)}) copy-start(f32[128,128]{1,0:T(8,128)} %get-tuple-element.31.table) | copy-start | bytes 196612
  106.7 19.8 %collective-permute-start.32 = (bf16[96,1792]{1,0:T(8,128)(2,1)}, bf16[96,1792]{1,0:T(8,128)(2,1)S(1)}, u32[]{:S(2)}, u32[]{:S(2)}) collective-permute-start(bf16[96,1792]{1,0:T(8,128)(2,1)} %get-tuple-element.52), channel_id=1, source_target_pairs={{0,4},{1,5},{2,6},{3,7},{4,0},{5,1},{6,2},{7,3},{8,12},{9,13},{10,... | collective-permute-start | bytes 1032200 | tf_op jit(solution)/shard_map/near_back0/ppermute | solution.py:340
  108.9 23.9 %collective-permute-start.35 = (bf16[128,1792]{1,0:T(8,128)(2,1)S(1)}, bf16[128,1792]{1,0:T(8,128)(2,1)S(1)}, u32[]{:S(2)}, u32[]{:S(2)}) collective-permute-start(bf16[128,1792]{1,0:T(8,128)(2,1)S(1)} %shard_map.78), channel_id=1, source_target_pairs={{4,8},{5,9},{6,10},{7,11},{8,4},{9,5},{10,6},{11,7},{20,24},{21,25... | collective-permute-start | bytes 1376264 | tf_op jit(solution)/shard_map/sum_back0/ppermute | solution.py:340
  114.9 34.3 %collective-permute-start.31 = (bf16[128,1792]{1,0:T(8,128)(2,1)S(1)}, bf16[128,1792]{1,0:T(8,128)(2,1)S(1)}, u32[]{:S(2)}, u32[]{:S(2)}) collective-permute-start(bf16[128,1792]{1,0:T(8,128)(2,1)S(1)} %shard_map.76), channel_id=1, source_target_pairs={{4,8},{5,9},{6,10},{7,11},{8,4},{9,5},{10,6},{11,7},{20,24},{21,25... | collective-permute-start | bytes 1376264 | tf_op jit(solution)/shard_map/sum_back1/ppermute | solution.py:340
  118.1 9.1 %collective-permute-start.34 = (bf16[96,1792]{1,0:T(8,128)(2,1)S(1)}, bf16[96,1792]{1,0:T(8,128)(2,1)S(1)}, u32[]{:S(2)}, u32[]{:S(2)}) collective-permute-start(bf16[96,1792]{1,0:T(8,128)(2,1)S(1)} %copy-done.13), channel_id=1, source_target_pairs={{0,12},{1,13},{2,14},{3,15},{12,0},{13,1},{14,2},{15,3},{16,28},{1... | collective-permute-start | bytes 1032200 | tf_op jit(solution)/shard_map/far_back0/ppermute | solution.py:340
  118.8 24.5 %collective-permute-start.28 = (bf16[96,1792]{1,0:T(8,128)(2,1)S(1)}, bf16[96,1792]{1,0:T(8,128)(2,1)S(1)}, u32[]{:S(2)}, u32[]{:S(2)}) collective-permute-start(bf16[96,1792]{1,0:T(8,128)(2,1)S(1)} %copy-done.16), channel_id=1, source_target_pairs={{0,4},{1,5},{2,6},{3,7},{4,0},{5,1},{6,2},{7,3},{8,12},{9,13},{10,... | collective-permute-start | bytes 1032200 | tf_op jit(solution)/shard_map/near_back1/ppermute | solution.py:340
  126.5 16.8 %collective-permute-start.30 = (bf16[96,1792]{1,0:T(8,128)(2,1)S(1)}, bf16[96,1792]{1,0:T(8,128)(2,1)S(1)}, u32[]{:S(2)}, u32[]{:S(2)}) collective-permute-start(bf16[96,1792]{1,0:T(8,128)(2,1)S(1)} %get-tuple-element.50.refs_1_), channel_id=1, source_target_pairs={{0,12},{1,13},{2,14},{3,15},{12,0},{13,1},{14,2},{15,3},{16,28},{1... | collective-permute-start | bytes 1032200 | tf_op jit(solution)/shard_map/far_back1/ppermute | solution.py:340
  (21 other events, 99.3 us)
